TPU v7x, 32 devices: a whole 2x2x4 slice. The times are simulated.
32 devices in a mesh: rows: 8 (over z, y), tm: 4 (over x, core).
Axes of the slice: x: 2, y: 2, z: 4, core: 2. Of those that a mesh axis runs over, the one named last changes fastest.
Arguments:
- frames: bfloat16 [8, 1024, 1024], P('rows', 'tm'), may hold values from -6 to 6
- segments: int32 [8, 1024], P('rows'), may hold values from 0 to 2, never falling along the last dimension, each value on 1 to 682 neighbouring positions
- ffn1_in: bfloat16 [1024, 4096], P('rows', 'tm'), may hold values from -0.1875 to 0.1875
- ffn1_out: bfloat16 [4096, 1024], P('rows', 'tm'), may hold values from -0.09375 to 0.09375
- query_w: bfloat16 [1024, 1024], P('rows', 'tm'), may hold values from -0.1875 to 0.1875
- key_w: bfloat16 [1024, 1024], P('rows', 'tm'), may hold values from -0.1875 to 0.1875
- value_w: bfloat16 [1024, 1024], P('rows', 'tm'), may hold values from -0.1875 to 0.1875
- attn_out: bfloat16 [1024, 1024], P('rows', 'tm'), may hold values from -2 to 2
- conv_in: bfloat16 [1024, 2048], P('rows', 'tm'), may hold values from -0.1875 to 0.1875
- conv_out: bfloat16 [1024, 1024], P('rows', 'tm'), may hold values from -0.1875 to 0.1875
- ffn2_in: bfloat16 [1024, 4096], P('rows', 'tm'), may hold values from -0.1875 to 0.1875
- ffn2_out: bfloat16 [4096, 1024], P('rows', 'tm'), may hold values from -0.09375 to 0.09375
- norm_gains: float32 [5, 1024], replicated, may hold values from 0.5 to 1.5
- conv_kernel: float32 [5, 1024], replicated, may hold values from -3 to 3
- bn_gain: float32 [1024], replicated, may hold values from 0.5 to 1.5
- bn_bias: float32 [1024], replicated, may hold values from -3 to 3
- rel_table: float32 [8, 17], replicated, may hold values from -4 to 4
- cotangent: bfloat16 [8, 1024, 1024], P('rows', 'tm'), may hold values from -6 to 6
Outputs:
- output: bfloat16 [8, 1024, 1024], P('rows', 'tm')
- grad_frames: bfloat16 [8, 1024, 1024], P('rows', 'tm')
- grad_ffn1_in: float32 [1024, 4096], P('rows', 'tm')
- grad_ffn1_out: float32 [4096, 1024], P('rows', 'tm')
- grad_query: float32 [1024, 1024], P('rows', 'tm')
- grad_key: float32 [1024, 1024], P('rows', 'tm')
- grad_value: float32 [1024, 1024], P('rows', 'tm')
- grad_attn_out: float32 [1024, 1024], P('rows', 'tm')
- grad_conv_in: float32 [1024, 2048], P('rows', 'tm')
- grad_conv_out: float32 [1024, 1024], P('rows', 'tm')
- grad_ffn2_in: float32 [1024, 4096], P('rows', 'tm')
- grad_ffn2_out: float32 [4096, 1024], P('rows', 'tm')
- grad_norm_gains: float32 [5, 1024], replicated
- grad_conv_kernel: float32 [5, 1024], replicated
- grad_bn_gain: float32 [1024], replicated
- grad_bn_bias: float32 [1024], replicated
- grad_rel_table: float32 [8, 17], replicated
Inputs may be any that keep to these rules, and one draw needn't show every extreme that they name: `segments`: in each row the ids never fall, each of the 3 utterances has 1 to 682 frames, and one has exactly 682.
All inputs are finite; a program needn't handle non-finite values.
Results may differ from a plain program's by a relative error of at most 0.025.
Values may be sent and summed in bfloat16 or wider, within the bound.
No kernel may reach another device: no remote copies, remote signals or barrier semaphores. Data moves between devices by JAX's collectives and lax.ppermute only.
A program may use at most 640 MiB of HBM per device.

v0:
```python
import jax
import jax.numpy as jnp
from jax import lax
from jax.sharding import PartitionSpec as P

HEAD_DIM = 128
RELMAX = 8


epsilon = 1e-05


def with_halo(array, sides, width):
    for axis, dim in sides:
        peers, length = (lax.axis_size(axis), array.shape[dim])
        up = [(i, (i + 1) % peers) for i in range(peers - 1)]
        down = [(j, i) for i, j in up]
        last = lax.slice_in_dim(array, length - width, length, axis=dim)
        initial = lax.slice_in_dim(array, 0, width, axis=dim)
        before = lax.ppermute(last, axis, up)
        after = lax.ppermute(initial, axis, down)
        array = jnp.concatenate([before, array, after], axis=dim)
    return array


def matmul(first_op, second_op):
    return jnp.dot(first_op, second_op, preferred_element_type=jnp.float32)


def matmul_tn(first_op, second_op):
    return lax.dot_general(
        first_op, second_op, (((0,), (0,)), ((), ())), preferred_element_type=jnp.float32
    )


def matmul_nt(first_op, second_op):
    return lax.dot_general(
        first_op, second_op, (((1,), (1,)), ((), ())), preferred_element_type=jnp.float32
    )


def silu_slope(preact):
    sigmoid = jax.nn.sigmoid(preact)
    return sigmoid * (1.0 + preact * (1.0 - sigmoid))


def norm_rows(inputs, gain_row):
    center = inputs - jnp.mean(inputs, axis=-1, keepdims=True)
    spread = jnp.mean(center * center, axis=-1, keepdims=True)
    inverse = lax.rsqrt(spread + epsilon)
    normed = center * inverse
    return (normed * gain_row, normed, inverse)


def norm_back(gradient, normed, inverse, gain_row):
    scaled = gradient * gain_row
    back_rows = inverse * (
        scaled
        - jnp.mean(scaled, axis=-1, keepdims=True)
        - normed * jnp.mean(scaled * normed, axis=-1, keepdims=True)
    )
    return (back_rows, jnp.sum(gradient * normed, axis=0))


def fetch(matrix_one, matrix_two, matrix_three, matrix_four, matrix_five):
    by_column = (
        lax.all_gather(matrix_one, "tm", axis=1, tiled=True),
        lax.all_gather(matrix_two, "tm", axis=1, tiled=True),
        lax.all_gather(matrix_three, "tm", axis=1, tiled=True),
        lax.all_gather(matrix_four, "tm", axis=1, tiled=True),
        lax.all_gather(matrix_five, "tm", axis=1, tiled=True),
    )
    return (
        lax.all_gather(by_column[0], "rows", axis=0, tiled=True),
        lax.all_gather(by_column[1], "rows", axis=0, tiled=True),
        lax.all_gather(by_column[2], "rows", axis=0, tiled=True),
        lax.all_gather(by_column[3], "rows", axis=0, tiled=True),
        lax.all_gather(by_column[4], "rows", axis=0, tiled=True),
    )


def reduce_grads(matrix_one, matrix_two, matrix_three, matrix_four, matrix_five):
    by_row = (
        lax.psum_scatter(
            matrix_one.astype(jnp.bfloat16), "rows", scatter_dimension=0, tiled=True
        ).astype(jnp.float32),
        lax.psum_scatter(
            matrix_two.astype(jnp.bfloat16), "rows", scatter_dimension=0, tiled=True
        ).astype(jnp.float32),
        lax.psum_scatter(
            matrix_three.astype(jnp.bfloat16), "rows", scatter_dimension=0, tiled=True
        ).astype(jnp.float32),
        lax.psum_scatter(
            matrix_four.astype(jnp.bfloat16), "rows", scatter_dimension=0, tiled=True
        ).astype(jnp.float32),
        lax.psum_scatter(
            matrix_five.astype(jnp.bfloat16), "rows", scatter_dimension=0, tiled=True
        ).astype(jnp.float32),
    )
    return (
        lax.psum_scatter(
            by_row[0].astype(jnp.bfloat16), "tm", scatter_dimension=1, tiled=True
        ).astype(jnp.float32),
        lax.psum_scatter(
            by_row[1].astype(jnp.bfloat16), "tm", scatter_dimension=1, tiled=True
        ).astype(jnp.float32),
        lax.psum_scatter(
            by_row[2].astype(jnp.bfloat16), "tm", scatter_dimension=1, tiled=True
        ).astype(jnp.float32),
        lax.psum_scatter(
            by_row[3].astype(jnp.bfloat16), "tm", scatter_dimension=1, tiled=True
        ).astype(jnp.float32),
        lax.psum_scatter(
            by_row[4].astype(jnp.bfloat16), "tm", scatter_dimension=1, tiled=True
        ).astype(jnp.float32),
    )


def feed_forward(inputs, gain_row, weight_in, weight_out):
    normed_out, normed, inverse = norm_rows(inputs, gain_row)
    hidden = normed_out.astype(jnp.bfloat16)
    preact = matmul(hidden, weight_in)
    active = (preact * jax.nn.sigmoid(preact)).astype(jnp.bfloat16)
    return (matmul(active, weight_out), (normed, inverse, hidden, preact, active))


def feed_back(gradient, stored, gain_row, weight_in, weight_out):
    normed, inverse, hidden, preact, active = stored
    grad_low = (0.5 * gradient).astype(jnp.bfloat16)
    grad_weight_out = matmul_tn(active, grad_low)
    grad_active = matmul_nt(grad_low, weight_out)
    grad_preact = (grad_active * silu_slope(preact)).astype(jnp.bfloat16)
    grad_weight_in = matmul_tn(hidden, grad_preact)
    back_rows, grad_gain = norm_back(matmul_nt(grad_preact, weight_in), normed, inverse, gain_row)
    return (gradient + back_rows, grad_gain, grad_weight_in, grad_weight_out)


def block_buckets(length, first_row, block_rows):
    positions = jnp.arange(length, dtype=jnp.int32)
    rows_at = first_row + jnp.arange(block_rows, dtype=jnp.int32)
    return jnp.clip(positions[None, :] - rows_at[:, None], -RELMAX, RELMAX) + RELMAX


def scores_block(q_block, key_rows, bias_here, seg_row, first_row, block_rows):
    raw_scores = jnp.einsum(
        "qhd,khd->hqk", q_block, key_rows, preferred_element_type=jnp.float32
    ) * key_rows.shape[2] ** (-0.5)
    same_seg = seg_row[first_row : first_row + block_rows][:, None] == seg_row[None, :]
    return jnp.where(same_seg[None], raw_scores + bias_here, -jnp.inf)


def table_terms(grad_scores, bucket, first_row):
    wide_grad = grad_scores.astype(jnp.float32)
    total = jnp.sum(wide_grad, axis=(1, 2))
    lower = jnp.sum(jnp.where(bucket[None] == 0, wide_grad, 0.0), axis=(1, 2))
    inner = [
        jnp.sum(jnp.diagonal(wide_grad, offset=first_row + offset, axis1=1, axis2=2), axis=1)
        for offset in range(1 - RELMAX, RELMAX)
    ]
    band = inner[0]
    for term in inner[1:]:
        band = band + term
    upper = total - lower - band
    return jnp.stack([lower] + inner + [upper], axis=1)


def attend_row(queries, key_rows, values, seg_row, biases):
    length = key_rows.shape[0]
    block_rows = min(512, length)
    outputs = []
    logsums = []
    for block_id, first_row in enumerate(range(0, length, block_rows)):
        scores = scores_block(
            queries[first_row : first_row + block_rows],
            key_rows,
            biases[block_id],
            seg_row,
            first_row,
            block_rows,
        )
        row_peak = jnp.max(scores, axis=-1, keepdims=True)
        logsum = row_peak + jnp.log(jnp.sum(jnp.exp(scores - row_peak), axis=-1, keepdims=True))
        soft_probs = jnp.exp(scores - logsum).astype(jnp.bfloat16)
        outputs.append(
            jnp.einsum("hqk,khd->qhd", soft_probs, values, preferred_element_type=jnp.float32)
        )
        logsums.append(logsum)
    return (jnp.concatenate(outputs, axis=0), jnp.concatenate(logsums, axis=1))


def attend_back(
    queries, key_rows, values, seg_row, biases, buckets, table_shape, logsums, grad_out
):
    length = key_rows.shape[0]
    block_rows = min(512, length)
    score_scale = key_rows.shape[2] ** (-0.5)
    grad_keys = jnp.zeros(key_rows.shape, jnp.float32)
    grad_values = jnp.zeros(values.shape, jnp.float32)
    grad_table = jnp.zeros(table_shape, jnp.float32)
    grad_query = []
    for block_id, first_row in enumerate(range(0, length, block_rows)):
        q_block = queries[first_row : first_row + block_rows]
        out_block = grad_out[first_row : first_row + block_rows]
        scores = scores_block(q_block, key_rows, biases[block_id], seg_row, first_row, block_rows)
        soft_probs = jnp.exp(scores - logsums[:, first_row : first_row + block_rows])
        grad_probs = jnp.einsum(
            "qhd,khd->hqk", out_block, values, preferred_element_type=jnp.float32
        )
        inner_sum = jnp.sum(soft_probs * grad_probs, axis=-1, keepdims=True)
        grad_scores = (soft_probs * (grad_probs - inner_sum)).astype(jnp.bfloat16)
        grad_values = grad_values + jnp.einsum(
            "hqk,qhd->khd",
            soft_probs.astype(jnp.bfloat16),
            out_block,
            preferred_element_type=jnp.float32,
        )
        grad_query.append(
            jnp.einsum("hqk,khd->qhd", grad_scores, key_rows, preferred_element_type=jnp.float32)
            * score_scale
        )
        grad_keys = (
            grad_keys
            + jnp.einsum("hqk,qhd->khd", grad_scores, q_block, preferred_element_type=jnp.float32)
            * score_scale
        )
        grad_table = grad_table + table_terms(grad_scores, buckets[block_id], first_row)
    return (jnp.concatenate(grad_query, axis=0), grad_keys, grad_values, grad_table)


def shards(
    frames,
    segments,
    ffn1_in,
    ffn1_out,
    query_w,
    key_w,
    value_w,
    attn_out,
    conv_in,
    conv_out,
    ffn2_in,
    ffn2_out,
    norm_gains,
    conv_kernel,
    bn_gain,
    bn_bias,
    rel_table,
    cotangent,
):
    row_count, frame_count, model_width = frames.shape
    flat_rows = row_count * frame_count
    position = lax.axis_index("tm")
    heads_local = rel_table.shape[0] // lax.axis_size("tm")
    local_width = heads_local * HEAD_DIM
    table_local = lax.dynamic_slice_in_dim(rel_table, position * heads_local, heads_local, 0)
    tap_count = conv_kernel.shape[0]
    halo_reach = tap_count // 2
    frame_total = float(flat_rows * lax.axis_size("rows") * lax.axis_size("tm"))
    padded_seg = jnp.pad(segments, ((0, 0), (halo_reach, halo_reach)), constant_values=-1)
    seg_near = lax.dynamic_slice_in_dim(
        padded_seg, position * frame_count, frame_count + 2 * halo_reach, 1
    )
    seg_own = seg_near[:, halo_reach : halo_reach + frame_count]
    same_tap = [
        (seg_near[:, tap_id : tap_id + frame_count] == seg_own)[:, :, None]
        for tap_id in range(tap_count)
    ]
    full_ffn1_in, full_ffn1_out, full_query, full_key, full_value = fetch(
        ffn1_in, ffn1_out, query_w, key_w, value_w
    )
    inputs = frames.astype(jnp.float32).reshape(flat_rows, model_width)
    branch_one, stored_one = feed_forward(inputs, norm_gains[0], full_ffn1_in, full_ffn1_out)
    resid_one = inputs + 0.5 * branch_one
    attn_norm, normed_two, inverse_two = norm_rows(resid_one, norm_gains[1])
    hidden_two = attn_norm.astype(jnp.bfloat16)
    stacked = (
        jnp.stack(
            [
                matmul(hidden_two, full_query),
                matmul(hidden_two, full_key),
                matmul(hidden_two, full_value),
            ]
        )
        .astype(jnp.bfloat16)
        .reshape(3, row_count, frame_count, model_width)
    )
    full_attn_out, full_conv_in, full_conv_out, full_ffn2_in, full_ffn2_out = fetch(
        attn_out, conv_in, conv_out, ffn2_in, ffn2_out
    )
    head_major = lax.all_to_all(stacked, "tm", split_axis=3, concat_axis=2, tiled=True)
    length = head_major.shape[2]
    block_rows = min(512, length)
    buckets = [
        block_buckets(length, first_row, block_rows) for first_row in range(0, length, block_rows)
    ]
    biases = [jnp.take(table_local, bucket, axis=1) for bucket in buckets]
    split_heads = head_major.reshape(3, row_count, length, heads_local, HEAD_DIM)
    row_id = 0
    attended, logsums = attend_row(
        split_heads[0, row_id],
        split_heads[1, row_id],
        split_heads[2, row_id],
        segments[row_id],
        biases,
    )
    attended_rows = [attended.astype(jnp.bfloat16).reshape(length, local_width)]
    logsum_rows = [logsums]
    mixed_heads = jnp.stack(attended_rows)
    time_major = lax.all_to_all(mixed_heads, "tm", split_axis=1, concat_axis=2, tiled=True)
    attn_flat = time_major.reshape(flat_rows, model_width)
    resid_two = resid_one + matmul(attn_flat, full_attn_out)
    conv_norm, normed_three, inverse_three = norm_rows(resid_two, norm_gains[2])
    hidden_three = conv_norm.astype(jnp.bfloat16)
    upper_proj = matmul(hidden_three, full_conv_in)
    upper_lin = upper_proj[:, :model_width]
    upper_sig = jax.nn.sigmoid(upper_proj[:, model_width:])
    gated_glu = (
        (upper_lin * upper_sig).astype(jnp.bfloat16).reshape(row_count, frame_count, model_width)
    )
    gated_near = with_halo(gated_glu, (("tm", 1),), halo_reach)
    conv_sum = jnp.zeros((row_count, frame_count, model_width), jnp.float32)
    for tap_id in range(tap_count):
        conv_sum = conv_sum + jnp.where(
            same_tap[tap_id],
            gated_near[:, tap_id : tap_id + frame_count].astype(jnp.float32) * conv_kernel[tap_id],
            0.0,
        )
    conv_flat = conv_sum.reshape(flat_rows, model_width)
    moments = lax.psum(
        (jnp.sum(conv_flat, axis=0), jnp.sum(conv_flat * conv_flat, axis=0)), ("rows", "tm")
    )
    centre = moments[0] / frame_total
    inverse_bn = lax.rsqrt(moments[1] / frame_total - centre * centre + epsilon)
    normed_bn = (conv_flat - centre) * inverse_bn
    shifted = normed_bn * bn_gain + bn_bias
    active_bn = (shifted * jax.nn.sigmoid(shifted)).astype(jnp.bfloat16)
    resid_three = resid_two + matmul(active_bn, full_conv_out)
    branch_four, stored_four = feed_forward(resid_three, norm_gains[3], full_ffn2_in, full_ffn2_out)
    resid_four = resid_three + 0.5 * branch_four
    final_norm, normed_five, inverse_five = norm_rows(resid_four, norm_gains[4])
    output = final_norm.astype(jnp.bfloat16).reshape(row_count, frame_count, model_width)
    gradient = cotangent.astype(jnp.float32).reshape(flat_rows, model_width)
    grad_four, gain_five = norm_back(gradient, normed_five, inverse_five, norm_gains[4])
    back_attn_out, back_conv_in, back_conv_out, back_ffn2_in, back_ffn2_out = (
        full_attn_out,
        full_conv_in,
        full_conv_out,
        full_ffn2_in,
        full_ffn2_out,
    )
    grad_three, gain_four, grad_ffn2_in, grad_ffn2_out = feed_back(
        grad_four, stored_four, norm_gains[3], back_ffn2_in, back_ffn2_out
    )
    grad_low = grad_three.astype(jnp.bfloat16)
    grad_conv_out = matmul_tn(active_bn, grad_low)
    grad_shift = matmul_nt(grad_low, back_conv_out) * silu_slope(shifted)
    bn_sums = lax.psum(
        (jnp.sum(grad_shift, axis=0), jnp.sum(grad_shift * normed_bn, axis=0)), ("rows", "tm")
    )
    grad_conv = (
        (
            bn_gain
            * inverse_bn
            * (grad_shift - bn_sums[0] / frame_total - normed_bn * (bn_sums[1] / frame_total))
        )
        .astype(jnp.bfloat16)
        .reshape(row_count, frame_count, model_width)
    )
    grad_near = with_halo(grad_conv, (("tm", 1),), halo_reach)
    grad_conv_wide = grad_conv.astype(jnp.float32)
    grad_gated = jnp.zeros((row_count, frame_count, model_width), jnp.float32)
    kernel_grads = []
    for tap_id in range(tap_count):
        mirror = tap_count - 1 - tap_id
        grad_gated = grad_gated + jnp.where(
            same_tap[mirror],
            grad_near[:, mirror : mirror + frame_count].astype(jnp.float32) * conv_kernel[tap_id],
            0.0,
        )
        kernel_grads.append(
            jnp.sum(
                jnp.where(
                    same_tap[tap_id],
                    gated_near[:, tap_id : tap_id + frame_count].astype(jnp.float32)
                    * grad_conv_wide,
                    0.0,
                ),
                axis=(0, 1),
            )
        )
    grad_gated = grad_gated.reshape(flat_rows, model_width)
    grad_upper = jnp.concatenate(
        [grad_gated * upper_sig, grad_gated * upper_lin * upper_sig * (1.0 - upper_sig)], axis=1
    ).astype(jnp.bfloat16)
    grad_conv_in = matmul_tn(hidden_three, grad_upper)
    back_three, gain_three = norm_back(
        matmul_nt(grad_upper, back_conv_in), normed_three, inverse_three, norm_gains[2]
    )
    grad_two = grad_three + back_three
    grad_low_two = grad_two.astype(jnp.bfloat16)
    grad_attn_out = matmul_tn(attn_flat, grad_low_two)
    grad_time = (
        matmul_nt(grad_low_two, back_attn_out)
        .astype(jnp.bfloat16)
        .reshape(row_count, frame_count, model_width)
    )
    early_sums = reduce_grads(
        grad_ffn2_in, grad_ffn2_out, grad_conv_in, grad_conv_out, grad_attn_out
    )
    grad_heads = lax.all_to_all(grad_time, "tm", split_axis=2, concat_axis=1, tiled=True)
    back_ffn1_in, back_ffn1_out, back_query, back_key, back_value = (
        full_ffn1_in,
        full_ffn1_out,
        full_query,
        full_key,
        full_value,
    )
    grad_heads_split = grad_heads.reshape(row_count, length, heads_local, HEAD_DIM)
    table_grad = jnp.zeros(table_local.shape, jnp.float32)
    row_id = 0
    grad_q, grad_k, grad_v, grad_tab = attend_back(
        split_heads[0, row_id],
        split_heads[1, row_id],
        split_heads[2, row_id],
        segments[row_id],
        biases,
        buckets,
        table_local.shape,
        logsum_rows[row_id],
        grad_heads_split[row_id],
    )
    table_grad = table_grad + grad_tab
    grad_qkv_rows = [jnp.stack([grad_q, grad_k, grad_v]).reshape(3, length, local_width)]
    grad_qkv = jnp.stack(grad_qkv_rows, axis=1).astype(jnp.bfloat16)
    grad_proj = lax.all_to_all(grad_qkv, "tm", split_axis=2, concat_axis=3, tiled=True).reshape(
        3, flat_rows, model_width
    )
    grad_query = matmul_tn(hidden_two, grad_proj[0])
    grad_key = matmul_tn(hidden_two, grad_proj[1])
    grad_value = matmul_tn(hidden_two, grad_proj[2])
    grad_hidden_two = (
        matmul_nt(grad_proj[0], back_query)
        + matmul_nt(grad_proj[1], back_key)
        + matmul_nt(grad_proj[2], back_value)
    )
    back_two, gain_two = norm_back(grad_hidden_two, normed_two, inverse_two, norm_gains[1])
    grad_one = grad_two + back_two
    grad_inputs, gain_one, grad_ffn1_in, grad_ffn1_out = feed_back(
        grad_one, stored_one, norm_gains[0], back_ffn1_in, back_ffn1_out
    )
    late_sums = reduce_grads(grad_query, grad_key, grad_value, grad_ffn1_in, grad_ffn1_out)
    full_table = lax.dynamic_update_slice_in_dim(
        jnp.zeros(rel_table.shape, jnp.float32), table_grad, position * heads_local, 0
    )
    gathered_small = lax.psum(
        (
            jnp.stack([gain_one, gain_two, gain_three, gain_four, gain_five]),
            jnp.stack(kernel_grads),
            full_table,
        ),
        ("rows", "tm"),
    )
    return (
        output,
        grad_inputs.astype(jnp.bfloat16).reshape(row_count, frame_count, model_width),
        late_sums[3],
        late_sums[4],
        late_sums[0],
        late_sums[1],
        late_sums[2],
        early_sums[4],
        early_sums[2],
        early_sums[3],
        early_sums[0],
        early_sums[1],
        gathered_small[0],
        gathered_small[1],
        bn_sums[1],
        bn_sums[0],
        gathered_small[2],
    )


def solution(mesh):
    placed = (
        P("rows", "tm", None),
        P("rows", None),
        P("rows", "tm"),
        P("rows", "tm"),
        P("rows", "tm"),
        P("rows", "tm"),
        P("rows", "tm"),
        P("rows", "tm"),
        P("rows", "tm"),
        P("rows", "tm"),
        P("rows", "tm"),
        P("rows", "tm"),
        P(),
        P(),
        P(),
        P(),
        P(),
        P("rows", "tm", None),
    )
    return jax.shard_map(
        shards,
        mesh=mesh,
        in_specs=placed,
        out_specs=(
            P("rows", "tm", None),
            P("rows", "tm", None),
            P("rows", "tm"),
            P("rows", "tm"),
            P("rows", "tm"),
            P("rows", "tm"),
            P("rows", "tm"),
            P("rows", "tm"),
            P("rows", "tm"),
            P("rows", "tm"),
            P("rows", "tm"),
            P("rows", "tm"),
            P(),
            P(),
            P(),
            P(),
            P(),
        ),
        check_vma=False,
    )
```

profile of v0, /device:TPU:0, one launch (start us, length us, event | category | flops | bytes accessed | tf_op | source)
XLA Modules:
  0.0 5691.8 jit_solution(7039866144237022406)
XLA Ops:
  10.1 19.0 all-gather.15.cloned.1.call-done
  29.2 18.4 all-gather.19.cloned.1.call-done
  103.7 111.6 %all-gather.17.cloned.1.call-done = bf16[1024,4096]{1,0:T(8,128)(2,1)} async-done(((bf16[128,4096]{1,0:T(8,128)(2,1)}), bf16[1024,4096]{1,0:T(8,128)(2,1)}) %all-gather.17.cloned.1.call-update) | async-done | bytes 8388624 | tf_op jit(solution)/shard_map/all_gather | solution.py:74
  223.2 117.3 %all-gather.21.cloned.1.call-done = bf16[4096,1024]{1,0:T(8,128)(2,1)} async-done(((bf16[512,1024]{1,0:T(8,128)(2,1)}), bf16[4096,1024]{1,0:T(8,128)(2,1)}) %all-gather.21.cloned.1.call-update) | async-done | bytes 8388624 | tf_op jit(solution)/shard_map/all_gather | solution.py:75
  348.8 41.3 all-gather.23.cloned.1.call-done
  392.4 47.6 all-gather.25.cloned.1.call-done
  443.1 46.8 all-gather.27.cloned.1.call-done
  503.6 1719.3 %gather_fusion.30 = f32[524288,2]{1,0:T(8,128)} fusion(f32[2,17]{0,1:T(8,128)S(1)} %copy.491, s32[524288]{0:T(1024)S(1)} %broadcast_clamp_fusion.1), kind=kCustom, calls=%fused_computation.clone | custom fusion | bytes 10485760 | tf_op jit(solution)/shard_map/jit(_take)/gather | solution.py:296
  2222.8 139.6 %copy.487 = f32[512,1024,2]{1,0,2:T(8,128)} copy(f32[512,1024,2]{2,1,0:T(8,128)} %bitcast.11) | data formatting | bytes 8388608 | tf_op jit(solution)/shard_map/jit(_take)/gather | solution.py:296
  2362.5 1719.3 %gather_fusion.31 = f32[524288,2]{1,0:T(8,128)} fusion(f32[2,17]{0,1:T(8,128)S(1)} %copy.491, s32[524288]{0:T(1024)S(1)} %copy-done.30), kind=kCustom, calls=%fused_computation.1.clone | custom fusion | bytes 10485760 | tf_op jit(solution)/shard_map/jit(_take)/gather | solution.py:296
  4081.7 139.5 %copy.488 = f32[512,1024,2]{1,0,2:T(8,128)} copy(f32[512,1024,2]{2,1,0:T(8,128)} %bitcast.16) | data formatting | bytes 8388608 | tf_op jit(solution)/shard_map/jit(_take)/gather | solution.py:296
  4286.9 40.3 all-reduce.3
  4372.9 40.5 all-reduce.2
  4495.9 28.3 all_to_all.61
  4597.0 70.0 %reduce-scatter.33.cloned.1.call-done = bf16[128,1024]{1,0:T(8,128)(2,1)} async-done(((bf16[1024,1024]{1,0:T(8,128)(2,1)}), bf16[128,1024]{1,0:T(8,128)(2,1)}) %reduce-scatter.33.cloned.1.call-update) | async-done | bytes 262160 | tf_op jit(solution)/shard_map/reduce_scatter | solution.py:87
  4667.1 70.3 %reduce-scatter.37.cloned.1.call-done = bf16[128,1024]{1,0:T(8,128)(2,1)} async-done(((bf16[1024,1024]{1,0:T(8,128)(2,1)}), bf16[128,1024]{1,0:T(8,128)(2,1)}) %reduce-scatter.37.cloned.1.call-update) | async-done | bytes 262160 | tf_op jit(solution)/shard_map/reduce_scatter | solution.py:90
  4737.4 90.5 %reduce-scatter.45.cloned.1.call-done = bf16[128,2048]{1,0:T(8,128)(2,1)} async-done(((bf16[1024,2048]{1,0:T(8,128)(2,1)}), bf16[128,2048]{1,0:T(8,128)(2,1)}) %reduce-scatter.45.cloned.1.call-update) | async-done | bytes 524304 | tf_op jit(solution)/shard_map/reduce_scatter | solution.py:90
  4828.0 152.8 %reduce-scatter.57.cloned.1.call-done = bf16[512,1024]{1,0:T(8,128)(2,1)} async-done(((bf16[4096,1024]{1,0:T(8,128)(2,1)}), bf16[512,1024]{1,0:T(8,128)(2,1)}) %reduce-scatter.57.cloned.1.call-update) | async-done | bytes 1048592 | tf_op jit(solution)/shard_map/reduce_scatter | solution.py:87
  4980.8 151.7 %reduce-scatter.53.cloned.1.call-done = bf16[128,4096]{1,0:T(8,128)(2,1)} async-done(((bf16[1024,4096]{1,0:T(8,128)(2,1)}), bf16[128,4096]{1,0:T(8,128)(2,1)}) %reduce-scatter.53.cloned.1.call-update) | async-done | bytes 1048592 | tf_op jit(solution)/shard_map/reduce_scatter | solution.py:84
  5132.6 152.0 %reduce-scatter.25.cloned.1.call-done = bf16[512,1024]{1,0:T(8,128)(2,1)} async-done(((bf16[4096,1024]{1,0:T(8,128)(2,1)}), bf16[512,1024]{1,0:T(8,128)(2,1)}) %reduce-scatter.25.cloned.1.call-update) | async-done | bytes 1048592 | tf_op jit(solution)/shard_map/reduce_scatter | solution.py:96
  5405.1 31.1 reduce-scatter.21.cloned.1.call-done
  5561.8 40.5 all-reduce.1
  5629.7 25.7 reduce-scatter.27.cloned.1.call-done
  5657.2 25.7 reduce-scatter.23.cloned.1.call-done
  (621 shorter events, 636.1 us)
Async XLA Ops:
  47.6 342.5 %all-gather.23.cloned.1.call-start = ((), (), s32[]{:S(2)}) async-start(), calls=%async_computation.28 | async-start | bytes 2359296 | tf_op jit(solution)/shard_map/all_gather | solution.py:76
  54.1 385.9 %all-gather.25.cloned.1.call-start = ((), (), s32[]{:S(2)}) async-start(), calls=%async_computation.29 | async-start | bytes 2359296 | tf_op jit(solution)/shard_map/all_gather | solution.py:77
  63.3 426.6 %all-gather.27.cloned.1.call-start = ((), (), s32[]{:S(2)}) async-start(), calls=%async_computation.30 | async-start | bytes 2359296 | tf_op jit(solution)/shard_map/all_gather | solution.py:78
  69.8 4198.4 %all-gather.29.cloned.1.call-start = ((), (), s32[]{:S(2)}) async-start(), calls=%async_computation.31 | async-start | bytes 2359296 | tf_op jit(solution)/shard_map/all_gather | solution.py:74
  76.2 4195.9 %all-gather.31.cloned.1.call-start = ((), (), s32[]{:S(2)}) async-start(), calls=%async_computation.32 | async-start | bytes 4718592 | tf_op jit(solution)/shard_map/all_gather | solution.py:75
  87.2 4240.1 %all-gather.33.cloned.1.call-start = ((), (), s32[]{:S(2)}) async-start(), calls=%async_computation.33 | async-start | bytes 2359296 | tf_op jit(solution)/shard_map/all_gather | solution.py:76
  93.6 4238.1 %all-gather.37.cloned.1.call-start = ((), (), s32[]{:S(2)}) async-start(), calls=%async_computation.35 | async-start | bytes 9437184 | tf_op jit(solution)/shard_map/all_gather | solution.py:77
  95.8 4244.0 %all-gather.41.cloned.1.call-start = ((), (), s32[]{:S(2)}) async-start(), calls=%async_computation.37 | async-start | bytes 9437184 | tf_op jit(solution)/shard_map/all_gather | solution.py:78
  498.8 3727.4 %all-to-all-start = ((bf16[3,1,256,1024]{2,0,1,3:T(4,128)(2,1)}), bf16[3,1,256,1024]{2,0,1,3:T(4,128)(2,1)}, u32[]{:S(2)}, u32[]{:S(2)}) async-start(bf16[3,1,256,1024]{2,0,1,3:T(4,128)(2,1)} %copy.385), calls=%async_computation | async-start | bytes 4194304 | tf_op jit(solution)/shard_map/all_to_all | solution.py:290
  503.2 4090.4 %reduce-scatter.49.cloned.1.call-start = ((), (), s32[]{:S(2)}) async-start(), calls=%async_computation.52 | async-start | bytes 2359296 | tf_op jit(solution)/shard_map/reduce_scatter | solution.py:93
  4546.7 434.1 %reduce-scatter.57.cloned.1.call-start = ((), (), s32[]{:S(2)}) async-start(), calls=%async_computation.56 | async-start | bytes 9437184 | tf_op jit(solution)/shard_map/reduce_scatter | solution.py:87
  4556.2 576.3 %reduce-scatter.53.cloned.1.call-start = ((), (), s32[]{:S(2)}) async-start(), calls=%async_computation.54 | async-start | bytes 9437184 | tf_op jit(solution)/shard_map/reduce_scatter | solution.py:84
  4564.6 720.0 %reduce-scatter.25.cloned.1.call-start = ((), (), s32[]{:S(2)}) async-start(), calls=%async_computation.40 | async-start | bytes 9437184 | tf_op jit(solution)/shard_map/reduce_scatter | solution.py:96
  4578.5 857.7 %reduce-scatter.21.cloned.1.call-start = ((), (), s32[]{:S(2)}) async-start(), calls=%async_computation.38 | async-start | bytes 9437184 | tf_op jit(solution)/shard_map/reduce_scatter | solution.py:93
  4593.6 1010.0 %reduce-scatter.51.cloned.1.call-start = ((), (), s32[]{:S(2)}) async-start(), calls=%async_computation.53 | async-start | bytes 327680 | tf_op jit(solution)/shard_map/reduce_scatter | solution.py:110
  4594.3 1010.7 %reduce-scatter.43.cloned.1.call-start = ((), (), s32[]{:S(2)}) async-start(), calls=%async_computation.49 | async-start | bytes 327680 | tf_op jit(solution)/shard_map/reduce_scatter | solution.py:113
  4594.9 1011.7 %reduce-scatter.31.cloned.1.call-start = ((), (), s32[]{:S(2)}) async-start(), calls=%async_computation.43 | async-start | bytes 327680 | tf_op jit(solution)/shard_map/reduce_scatter | solution.py:101
  4596.9 1011.1 %reduce-scatter.35.cloned.1.call-start = ((), (), s32[]{:S(2)}) async-start(), calls=%async_computation.45 | async-start | bytes 327680 | tf_op jit(solution)/shard_map/reduce_scatter | solution.py:104
  4667.0 942.5 %reduce-scatter.39.cloned.1.call-start = ((), (), s32[]{:S(2)}) async-start(), calls=%async_computation.47 | async-start | bytes 327680 | tf_op jit(solution)/shard_map/reduce_scatter | solution.py:107
  4737.4 873.7 %reduce-scatter.47.cloned.1.call-start = ((), (), s32[]{:S(2)}) async-start(), calls=%async_computation.51 | async-start | bytes 655360 | tf_op jit(solution)/shard_map/reduce_scatter | solution.py:107
  4827.9 784.8 %reduce-scatter.59.cloned.1.call-start = ((), (), s32[]{:S(2)}) async-start(), calls=%async_computation.57 | async-start | bytes 1310720 | tf_op jit(solution)/shard_map/reduce_scatter | solution.py:104
  4980.8 647.1 %reduce-scatter.55.cloned.1.call-start = ((), (), s32[]{:S(2)}) async-start(), calls=%async_computation.55 | async-start | bytes 1310720 | tf_op jit(solution)/shard_map/reduce_scatter | solution.py:101
  5132.5 522.9 %reduce-scatter.27.cloned.1.call-start = ((), (), s32[]{:S(2)}) async-start(), calls=%async_computation.41 | async-start | bytes 1310720 | tf_op jit(solution)/shard_map/reduce_scatter | solution.py:113
  5284.6 398.3 %reduce-scatter.23.cloned.1.call-start = ((), (), s32[]{:S(2)}) async-start(), calls=%async_computation.39 | async-start | bytes 1310720 | tf_op jit(solution)/shard_map/reduce_scatter | solution.py:110
  (134 other events, 11114.3 us)
Sparse Core Ops, SparseCore 0:
  90.3 124.9 all-gather.16
  217.3 123.1 all-gather.20
  342.6 47.4 all-gather.22
  392.2 47.7 all-gather.24
  442.1 47.7 all-gather.26
  491.9 47.9 all-gather.28
  542.0 71.8 all-gather.30
  615.9 47.5 all-gather.32
  665.6 123.4 all-gather.36
  791.0 123.1 all-gather.40
  4368.8 68.1 reduce-scatter.48
  4446.2 67.6 reduce-scatter.40
  4531.0 65.8 reduce-scatter.28
  4600.3 66.6 reduce-scatter.32
  4670.5 66.7 reduce-scatter.36
  4740.8 87.0 reduce-scatter.44
  4832.0 148.7 reduce-scatter.56
  4984.4 148.0 reduce-scatter.52
  5136.6 147.9 reduce-scatter.24
  5288.1 148.0 reduce-scatter.20
  5575.1 24.9 reduce-scatter.58
  5602.6 25.2 reduce-scatter.54
  5630.5 24.8 reduce-scatter.26
  5657.9 24.9 reduce-scatter.22
  (10 shorter events, 194.7 us)
where the time goes:
time: 5700 us; the launch traced here: 5690 us
  local copies, waits for them, and re-layouts  4010 us (70%)
  waiting for transfers between devices  1200 us (21%)
  blocking collectives  207 us (4%)
  matrix products  165 us (3%)
  other arithmetic  75.5 us (1%)
    gather x4, local copies, waits for them, and re-layouts, shards(): biases = [jnp.take(table_local, bucket, axis=1) for bucket in buckets]  3720 us
    reduce_scatter x2, waiting for transfers between devices, reduce_grads(): lax.psum_scatter(matrix_two.astype(jnp.bfloat16), 'rows', scatter_dimensi...  223 us
    gather x30, local copies, waits for them, and re-layouts, table_terms(): jnp.diagonal(wide_grad, offset=first_row + offset, axis1=1, axis2=2)  218 us
    reduce_scatter x2, waiting for transfers between devices, reduce_grads(): lax.psum_scatter(matrix_three.astype(jnp.bfloat16), 'rows', scatter_dimen...  161 us
    reduce_scatter x2, waiting for transfers between devices, reduce_grads(): lax.psum_scatter(matrix_one.astype(jnp.bfloat16), 'rows', scatter_dimensi...  154 us
    reduce_scatter x2, waiting for transfers between devices, reduce_grads(): lax.psum_scatter(matrix_five.astype(jnp.bfloat16), 'rows', scatter_dimens...  152 us
    all_gather x2, waiting for transfers between devices, fetch(): lax.all_gather(by_column[1], 'rows', axis=0, tiled=True)  117 us
  transfers between devices with their start and end apart: 40, of which 21 were waited for; matrix products, arithmetic and copies ran while one was open for 74% of the time, Pallas kernels for 0%

commit v1 on v0

v1 whole, which is shorter than its diff:
```python
import functools

import jax
import jax.numpy as jnp
from jax import lax
from jax.experimental import pallas as pl
from jax.experimental.pallas import tpu as pltpu
from jax.sharding import PartitionSpec as P

HEAD_DIM = 128
RELMAX = 8
LANES = 128
EPS = 1e-05
BF = jnp.bfloat16
F32 = jnp.float32


def mm(a, b):
    return jnp.dot(a, b, preferred_element_type=F32)


def mm_tn(a, b):
    return lax.dot_general(a, b, (((0,), (0,)), ((), ())), preferred_element_type=F32)


def mm_nt(a, b):
    return lax.dot_general(a, b, (((1,), (1,)), ((), ())), preferred_element_type=F32)


def silu_slope(a):
    s = jax.nn.sigmoid(a)
    return s * (1.0 + a * (1.0 - s))


def norm_rows(v, g):
    center = v - jnp.mean(v, axis=-1, keepdims=True)
    spread = jnp.mean(center * center, axis=-1, keepdims=True)
    inverse = lax.rsqrt(spread + EPS)
    normed = center * inverse
    return normed * g, normed, inverse


def norm_back(grad, normed, inverse, g):
    scaled = grad * g
    back = inverse * (
        scaled
        - jnp.mean(scaled, axis=-1, keepdims=True)
        - normed * jnp.mean(scaled * normed, axis=-1, keepdims=True)
    )
    return back, jnp.sum(grad * normed, axis=0)


def tm_peer(dx, dc):
    size = lax.axis_size("tm")
    chips = size // 2
    return [
        (((t // 2 + dx) % chips) * 2 + ((t % 2) ^ dc), t) for t in range(size)
    ]


def from_peer(a, dx, dc):
    return lax.ppermute(a, "tm", tm_peer(dx, dc))


def peer_index(dx, dc):
    chips = lax.axis_size("tm") // 2
    t = lax.axis_index("tm")
    return lax.rem(t // 2 + dx, chips) * 2 + jnp.bitwise_xor(t % 2, dc)


def gather_tm(a):
    size = lax.axis_size("tm")
    n, w = a.shape
    far = [from_peer(a, dx, 0) for dx in range(1, size // 2)]
    held = {(0, 0): a, (0, 1): from_peer(a, 0, 1)}
    for dx, b in enumerate(far, 1):
        held[dx, 0] = b
        held[dx, 1] = from_peer(b, 0, 1)
    out = jnp.zeros((size, n, w), a.dtype)
    for (dx, dc), b in held.items():
        out = lax.dynamic_update_index_in_dim(out, b, peer_index(dx, dc), 0)
    return out.reshape(size * n, w)


def scatter_tm(p):
    size = lax.axis_size("tm")
    chips = size // 2
    t = lax.axis_index("tm")
    x, c = t // 2, t % 2
    w = p.shape[1]
    p = p.reshape(chips, 2, p.shape[0] // size, w)
    mine = lax.dynamic_index_in_dim(p, c, 1, keepdims=False)
    theirs = lax.dynamic_index_in_dim(p, 1 - c, 1, keepdims=False).astype(BF)
    q = mine.astype(F32) + from_peer(theirs, 0, 1).astype(F32)
    total = lax.dynamic_index_in_dim(q, x, 0, keepdims=False)
    for dx in range(1, chips):
        piece = lax.dynamic_index_in_dim(q, lax.rem(x + chips - dx, chips), 0, keepdims=False)
        total = total + from_peer(piece.astype(BF), dx, 0).astype(F32)
    return total


def exchange_tm(pieces):
    size = lax.axis_size("tm")
    chips = size // 2
    t = lax.axis_index("tm")
    out = jnp.zeros(pieces.shape, pieces.dtype)
    out = lax.dynamic_update_index_in_dim(
        out, lax.dynamic_index_in_dim(pieces, t, 0, keepdims=False), t, 0
    )
    for dx in range(chips):
        for dc in range(2):
            if dx or dc:
                piece = lax.dynamic_index_in_dim(
                    pieces, peer_index(chips - dx, dc), 0, keepdims=False
                )
                out = lax.dynamic_update_index_in_dim(
                    out, from_peer(piece, dx, dc), peer_index(dx, dc), 0
                )
    return out


def sum_axis(v, axis):
    size, bit = lax.axis_size(axis), 1
    while bit < size:
        v = v + lax.ppermute(v, axis, [(i, i ^ bit) for i in range(size)])
        bit *= 2
    return v


def ffn_pieces(w_in, w_out):
    rows, size = lax.axis_size("rows"), lax.axis_size("tm")
    unit = w_out.shape[0] // size
    m, w = w_in.shape
    a = w_in.reshape(m, w // (size * unit), size, unit).transpose(2, 0, 1, 3)
    return a.reshape(size, m, w // size), w_out.reshape(size, unit, w_out.shape[1])


def ffn_ready(w_in, w_out):
    size = lax.axis_size("tm")
    a, b = ffn_pieces(w_in, w_out)
    if a.shape == b.shape:
        both = exchange_tm(jnp.concatenate([a, b], axis=1))
        a, b = both[:, : a.shape[1]], both[:, a.shape[1] :]
    else:
        a, b = exchange_tm(a), exchange_tm(b)
    a = a.transpose(1, 0, 2).reshape(a.shape[1], -1)
    b = b.transpose(1, 0, 2).reshape(b.shape[1], -1)
    if a.shape == b.shape:
        full = lax.all_gather(jnp.concatenate([a, b], axis=1), "rows", axis=0, tiled=True)
        return full[:, : a.shape[1]], full[:, a.shape[1] :]
    return tuple(lax.all_gather(v, "rows", axis=0, tiled=True) for v in (a, b))


def ffn_return(g_in, g_out, like_in, like_out):
    rows, size = lax.axis_size("rows"), lax.axis_size("tm")
    if g_in.shape == g_out.shape:
        both = lax.psum_scatter(
            jnp.concatenate([g_in, g_out], axis=1), "rows", scatter_dimension=0, tiled=True
        )
        a, b = both[:, : g_in.shape[1]], both[:, g_in.shape[1] :]
    else:
        a, b = (lax.psum_scatter(v, "rows", scatter_dimension=0, tiled=True) for v in (g_in, g_out))
    a = a.reshape(a.shape[0], size, -1).transpose(1, 0, 2)
    b = b.reshape(b.shape[0], size, -1).transpose(1, 0, 2)
    if a.shape == b.shape:
        both = exchange_tm(jnp.concatenate([a, b], axis=1))
        a, b = both[:, : a.shape[1]], both[:, a.shape[1] :]
    else:
        a, b = exchange_tm(a), exchange_tm(b)
    unit = like_out[0] // size
    m, w = like_in
    a = a.reshape(size, m, w // (size * unit), unit).transpose(1, 2, 0, 3).reshape(m, w)
    return a.astype(F32), b.reshape(like_out).astype(F32)


def head_rows_perm():
    rows, size = lax.axis_size("rows"), lax.axis_size("tm")
    perm = []
    for r in range(rows):
        for t in range(size):
            k, u = divmod(r, size)
            perm.append(((t * (rows // size) + k) * size + u, r * size + t))
    return perm


def fill_bias(tab_ref, head, strip, length):
    lo, hi = length - LANES, length + 2 * LANES
    first, last = tab_ref[head, 0], tab_ref[head, 2 * RELMAX]
    offset = (
        lax.broadcasted_iota(jnp.int32, (LANES, hi - lo), 1)
        - LANES
        - lax.broadcasted_iota(jnp.int32, (LANES, hi - lo), 0)
    )
    tile = jnp.where(offset <= -RELMAX, first, last)
    for b in range(1, 2 * RELMAX):
        tile = jnp.where(offset == b - RELMAX, tab_ref[head, b], tile)
    strip[:, :lo] = jnp.full((LANES, lo), first, F32)
    strip[:, lo:hi] = tile
    strip[:, hi:] = jnp.full((LANES, 2 * length - hi), last, F32)


def biased(q, k, seg_col, seg_row, strip, first, length):
    raw = mm_nt(q, k) * HEAD_DIM ** (-0.5)
    parts = [
        strip[:, length - (first + a) : 2 * length - (first + a)]
        for a in range(0, q.shape[0], LANES)
    ]
    bias = parts[0] if len(parts) == 1 else jnp.concatenate(parts, axis=0)
    return jnp.where(seg_col == seg_row, raw + bias, -jnp.inf)


def attend_kernel(tab_ref, seg_row_ref, seg_col_ref, q_ref, k_ref, v_ref, o_ref, lse_ref, strip):
    length = q_ref.shape[0]
    block = min(256, length)
    fill_bias(tab_ref, pl.program_id(0), strip, length)
    k, v = k_ref[...], v_ref[...]
    for first in range(0, length, block):
        own = slice(first, first + block)
        sc = biased(q_ref[own, :], k, seg_col_ref[own, :], seg_row_ref[...], strip, first, length)
        peak = jnp.max(sc, axis=1, keepdims=True)
        e = jnp.exp(sc - peak)
        total = jnp.sum(e, axis=1, keepdims=True)
        p = (e * (1.0 / total)).astype(BF)
        o_ref[own, :] = mm(p, v).astype(BF)
        lse_ref[0, own, :] = peak + jnp.log(total)


def attend(qkv, seg_row, table):
    length = qkv.shape[0]
    heads = table.shape[0]
    column = lambda first: pl.BlockSpec((length, HEAD_DIM), lambda h: (0, first + h))
    return pl.pallas_call(
        attend_kernel,
        grid=(heads,),
        in_specs=[
            pl.BlockSpec(memory_space=pltpu.SMEM),
            pl.BlockSpec((1, length), lambda h: (0, 0)),
            pl.BlockSpec((length, 1), lambda h: (0, 0)),
            column(0),
            column(heads),
            column(2 * heads),
        ],
        out_specs=[column(0), pl.BlockSpec((1, length, 1), lambda h: (h, 0, 0))],
        out_shape=[
            jax.ShapeDtypeStruct((length, heads * HEAD_DIM), BF),
            jax.ShapeDtypeStruct((heads, length, 1), F32),
        ],
        scratch_shapes=[pltpu.VMEM((LANES, 2 * length), F32)],
        compiler_params=pltpu.CompilerParams(vmem_limit_bytes=40 * 1024 * 1024),
        cost_estimate=pl.CostEstimate(
            flops=4 * heads * length * length * HEAD_DIM,
            bytes_accessed=8 * length * heads * HEAD_DIM,
            transcendentals=heads * length * length,
        ),
    )(table, seg_row.reshape(1, length), seg_row.reshape(length, 1), qkv, qkv, qkv)


def attend_back_kernel(
    tab_ref, seg_row_ref, seg_col_ref, q_ref, k_ref, v_ref, do_ref, lse_ref, dqkv_ref, band_ref,
    strip, dk_sum, dv_sum,
):
    length = q_ref.shape[0]
    block = min(256, length)
    head, heads = pl.program_id(0), pl.num_programs(0)
    fill_bias(tab_ref, head, strip, length)
    k, v = k_ref[...], v_ref[...]
    scale = HEAD_DIM ** (-0.5)
    at = lambda n: pl.ds(pl.multiple_of((n * heads + head) * HEAD_DIM, HEAD_DIM), HEAD_DIM)
    low = jnp.zeros((LANES, LANES), F32)
    high = jnp.zeros((LANES, LANES), F32)
    band = [jnp.zeros((LANES, LANES), F32) for _ in range(3)]
    for first in range(0, length, block):
        own = slice(first, first + block)
        q, do = q_ref[own, :], do_ref[own, :]
        sc = biased(q, k, seg_col_ref[own, :], seg_row_ref[...], strip, first, length)
        p = jnp.exp(sc - lse_ref[0, own, :])
        dp = mm_nt(do, v)
        inner = jnp.sum(p * dp, axis=1, keepdims=True)
        ds = (p * (dp - inner)).astype(BF)
        dv = mm_tn(p.astype(BF), do)
        dk = mm_tn(ds, q)
        if first == 0:
            dv_sum[...] = dv
            dk_sum[...] = dk
        else:
            dv_sum[...] += dv
            dk_sum[...] += dk
        dqkv_ref[own, at(0)] = (mm(ds, k) * scale).astype(BF)
        wide = ds.astype(F32)
        for a in range(0, block, LANES):
            for b in range(0, length, LANES):
                part = wide[a : a + LANES, b : b + LANES]
                apart = (b - first - a) // LANES
                if apart < -1:
                    low = low + part
                elif apart > 1:
                    high = high + part
                else:
                    band[apart + 1] = band[apart + 1] + part
    dqkv_ref[:, at(1)] = (dk_sum[...] * scale).astype(BF)
    dqkv_ref[:, at(2)] = dv_sum[...].astype(BF)
    for i, part in enumerate([low] + band + [high]):
        band_ref[0, :, i * LANES : (i + 1) * LANES] = part


def attend_back(qkv, seg_row, table, lse, grad):
    length = qkv.shape[0]
    heads = table.shape[0]
    column = lambda first: pl.BlockSpec((length, HEAD_DIM), lambda h: (0, first + h))
    dqkv, band = pl.pallas_call(
        attend_back_kernel,
        grid=(heads,),
        in_specs=[
            pl.BlockSpec(memory_space=pltpu.SMEM),
            pl.BlockSpec((1, length), lambda h: (0, 0)),
            pl.BlockSpec((length, 1), lambda h: (0, 0)),
            column(0),
            column(heads),
            column(2 * heads),
            column(0),
            pl.BlockSpec((1, length, 1), lambda h: (h, 0, 0)),
        ],
        out_specs=[
            pl.BlockSpec((length, 3 * heads * HEAD_DIM), lambda h: (0, 0)),
            pl.BlockSpec((1, LANES, 5 * LANES), lambda h: (h, 0, 0)),
        ],
        out_shape=[
            jax.ShapeDtypeStruct((length, 3 * heads * HEAD_DIM), BF),
            jax.ShapeDtypeStruct((heads, LANES, 5 * LANES), F32),
        ],
        scratch_shapes=[
            pltpu.VMEM((LANES, 2 * length), F32),
            pltpu.VMEM((length, HEAD_DIM), F32),
            pltpu.VMEM((length, HEAD_DIM), F32),
        ],
        compiler_params=pltpu.CompilerParams(vmem_limit_bytes=48 * 1024 * 1024),
        cost_estimate=pl.CostEstimate(
            flops=10 * heads * length * length * HEAD_DIM,
            bytes_accessed=16 * length * heads * HEAD_DIM,
            transcendentals=heads * length * length,
        ),
    )(table, seg_row.reshape(1, length), seg_row.reshape(length, 1), qkv, qkv, qkv, grad, lse)
    offset = (
        lax.broadcasted_iota(jnp.int32, (LANES, 3 * LANES), 1)
        - LANES
        - lax.broadcasted_iota(jnp.int32, (LANES, 3 * LANES), 0)
    )
    middle = band[:, :, LANES : 4 * LANES]
    inner = [
        jnp.sum(jnp.where(offset == b, middle, 0.0), axis=(1, 2)) for b in range(1 - RELMAX, RELMAX)
    ]
    lower = jnp.sum(jnp.where(offset <= -RELMAX, middle, 0.0), axis=(1, 2))
    upper = jnp.sum(jnp.where(offset >= RELMAX, middle, 0.0), axis=(1, 2))
    lower = lower + jnp.sum(band[:, :, :LANES], axis=(1, 2))
    upper = upper + jnp.sum(band[:, :, 4 * LANES :], axis=(1, 2))
    return dqkv, jnp.stack([lower] + inner + [upper], axis=1)


def shards(
    frames,
    segments,
    ffn1_in,
    ffn1_out,
    query_w,
    key_w,
    value_w,
    attn_out,
    conv_in,
    conv_out,
    ffn2_in,
    ffn2_out,
    norm_gains,
    conv_kernel,
    bn_gain,
    bn_bias,
    rel_table,
    cotangent,
):
    rows, size = lax.axis_size("rows"), lax.axis_size("tm")
    t = lax.axis_index("tm")
    own, width = frames.shape[1], frames.shape[2]
    length = own * size
    share = width // size
    heads = rel_table.shape[0] // size
    taps = conv_kernel.shape[0]
    reach = taps // 2
    frame_total = float(length * rows)
    seg = segments[0]
    table = lax.dynamic_slice_in_dim(rel_table, t * heads, heads, 0)
    depth = width // rows
    unit = depth // size

    def mine(v):
        v = v.reshape(-1, rows, size, unit)
        return lax.dynamic_index_in_dim(v, t, 2, keepdims=False).reshape(-1, share)

    def placed(v):
        n = v.shape[0]
        out = jnp.zeros((n, rows, size, unit), F32)
        return lax.dynamic_update_index_in_dim(
            out, v.reshape(n, rows, unit), t, 2
        ).reshape(n, width)

    kernel_own = mine(conv_kernel)
    bn_gain_own, bn_bias_own = mine(bn_gain[None]), mine(bn_bias[None])

    f1_in, f1_out = ffn_ready(ffn1_in, ffn1_out)
    perm = head_rows_perm()
    out_block = lax.ppermute(attn_out, ("rows", "tm"), perm)
    attn_w = lax.all_gather(
        jnp.concatenate([query_w, key_w, value_w, out_block], axis=1), "rows", axis=0, tiled=True
    )
    qkv_w = attn_w[:, : 3 * share]
    groups = rows // size
    attn_out_w = (
        attn_w[:, 3 * share :]
        .reshape(groups, size, depth, share)
        .transpose(0, 2, 1, 3)
        .reshape(share, width)
    )
    wide = conv_in.shape[1]
    conv_in_x = exchange_tm(
        conv_in.reshape(depth, wide // depth, size, unit)
        .transpose(2, 0, 1, 3)
        .reshape(size, depth, wide // size)
    )
    conv_in_x = conv_in_x.transpose(1, 0, 2).reshape(depth, wide)
    conv_out_x = exchange_tm(conv_out.reshape(size, unit, share)).reshape(depth, share)
    conv_w = lax.all_gather(
        jnp.concatenate([conv_in_x, conv_out_x], axis=1), "rows", axis=0, tiled=True
    )
    conv_in_w = conv_w[:, :wide]
    conv_out_w = (
        conv_w[:, wide:]
        .reshape(rows, size, unit, share)
        .transpose(0, 2, 1, 3)
        .reshape(share, width)
    )
    f2_in, f2_out = ffn_ready(ffn2_in, ffn2_out)

    inputs = frames[0].astype(F32)
    n1, normed_one, inverse_one = norm_rows(inputs, norm_gains[0])
    h1 = gather_tm(n1.astype(BF))
    a1 = mm(h1, f1_in)
    s1 = (a1 * jax.nn.sigmoid(a1)).astype(BF)
    x1 = inputs + 0.5 * scatter_tm(mm(s1, f1_out).astype(BF))

    n2, normed_two, inverse_two = norm_rows(x1, norm_gains[1])
    h2 = gather_tm(n2.astype(BF))
    qkv = mm(h2, qkv_w).astype(BF)
    att, lse = attend(qkv, seg, table)
    x2 = x1 + scatter_tm(mm(att, attn_out_w).astype(BF))

    n3, normed_three, inverse_three = norm_rows(x2, norm_gains[2])
    h3 = gather_tm(n3.astype(BF))
    u = mm(h3, conv_in_w)
    u_lin, u_sig = u[:, :share], jax.nn.sigmoid(u[:, share:])
    z = (u_lin * u_sig).astype(BF)
    seg_pad = jnp.pad(seg, (reach, reach), constant_values=-1)
    same = [(seg_pad[k : k + length] == seg)[:, None] for k in range(taps)]

    def shifted_rows(v):
        v = jnp.pad(v, ((reach, reach), (0, 0)))
        return [v[k : k + length] for k in range(taps)]

    z_near = shifted_rows(z)
    conv = jnp.zeros((length, share), F32)
    for k in range(taps):
        conv = conv + jnp.where(same[k], z_near[k].astype(F32) * kernel_own[k], 0.0)
    moments = sum_axis(
        jnp.stack([jnp.sum(conv, axis=0), jnp.sum(conv * conv, axis=0)]), "rows"
    )
    centre = moments[0] / frame_total
    inverse_bn = lax.rsqrt(moments[1] / frame_total - centre * centre + EPS)
    normed_bn = (conv - centre) * inverse_bn
    shifted = normed_bn * bn_gain_own + bn_bias_own
    e = (shifted * jax.nn.sigmoid(shifted)).astype(BF)
    x3 = x2 + scatter_tm(mm(e, conv_out_w).astype(BF))

    n4, normed_four, inverse_four = norm_rows(x3, norm_gains[3])
    h4 = gather_tm(n4.astype(BF))
    a4 = mm(h4, f2_in)
    s4 = (a4 * jax.nn.sigmoid(a4)).astype(BF)
    x4 = x3 + 0.5 * scatter_tm(mm(s4, f2_out).astype(BF))
    n5, normed_five, inverse_five = norm_rows(x4, norm_gains[4])
    output = n5.astype(BF)[None]

    d4, gain_five = norm_back(cotangent[0].astype(F32), normed_five, inverse_five, norm_gains[4])
    g4 = gather_tm((0.5 * d4).astype(BF))
    d_f2_out = mm_tn(s4, g4).astype(BF)
    da4 = (mm_nt(g4, f2_out) * silu_slope(a4)).astype(BF)
    d_f2_in = mm_tn(h4, da4).astype(BF)
    back, gain_four = norm_back(
        scatter_tm(mm_nt(da4, f2_in).astype(BF)), normed_four, inverse_four, norm_gains[3]
    )
    d3 = d4 + back
    grad_ffn2_in, grad_ffn2_out = ffn_return(d_f2_in, d_f2_out, ffn2_in.shape, ffn2_out.shape)

    g3 = gather_tm(d3.astype(BF))
    d_conv_out = mm_tn(e, g3).astype(BF)
    dn = mm_nt(g3, conv_out_w) * silu_slope(shifted)
    bn_part = jnp.stack([jnp.sum(dn, axis=0), jnp.sum(dn * normed_bn, axis=0)])
    bn_sums = sum_axis(bn_part, "rows")
    dc = (
        bn_gain_own
        * inverse_bn
        * (dn - bn_sums[0] / frame_total - normed_bn * (bn_sums[1] / frame_total))
    ).astype(BF)
    dc_near = shifted_rows(dc)
    dc_wide = dc.astype(F32)
    dz = jnp.zeros((length, share), F32)
    d_kernel = []
    for k in range(taps):
        mirror = taps - 1 - k
        dz = dz + jnp.where(same[mirror], dc_near[mirror].astype(F32) * kernel_own[k], 0.0)
        d_kernel.append(
            jnp.sum(jnp.where(same[k], z_near[k].astype(F32) * dc_wide, 0.0), axis=0)
        )
    du = jnp.concatenate([dz * u_sig, dz * u_lin * u_sig * (1.0 - u_sig)], axis=1).astype(BF)
    d_conv_in = mm_tn(h3, du).astype(BF)
    back, gain_three = norm_back(
        scatter_tm(mm_nt(du, conv_in_w).astype(BF)), normed_three, inverse_three, norm_gains[2]
    )
    d2 = d3 + back

    g2 = gather_tm(d2.astype(BF))
    d_attn_out = mm_tn(att, g2).astype(BF)
    d_att = mm_nt(g2, attn_out_w).astype(BF)
    dqkv, d_table = attend_back(qkv, seg, table, lse, d_att)
    d_qkv = mm_tn(h2, dqkv).astype(BF)
    back, gain_two = norm_back(
        scatter_tm(mm_nt(dqkv, qkv_w).astype(BF)), normed_two, inverse_two, norm_gains[1]
    )
    d1 = d2 + back

    d_attn_blocks = (
        d_attn_out.reshape(groups, depth, size, share).transpose(0, 2, 1, 3).reshape(width, share)
    )
    d_conv_blocks = (
        d_conv_out.reshape(rows, unit, size, share).transpose(0, 2, 1, 3).reshape(width, share)
    )
    middle = lax.psum_scatter(
        jnp.concatenate([d_qkv, d_attn_blocks, d_conv_in, d_conv_blocks], axis=1),
        "rows",
        scatter_dimension=0,
        tiled=True,
    )
    grad_query, grad_key, grad_value = (
        middle[:, i * share : (i + 1) * share].astype(F32) for i in range(3)
    )
    grad_attn_out = lax.ppermute(
        middle[:, 3 * share : 4 * share], ("rows", "tm"), [(b, a) for a, b in perm]
    ).astype(F32)
    d_in = middle[:, 4 * share : 4 * share + wide].reshape(depth, size, -1).transpose(1, 0, 2)
    grad_conv_in = (
        exchange_tm(d_in)
        .reshape(size, depth, wide // depth, unit)
        .transpose(1, 2, 0, 3)
        .reshape(depth, wide)
        .astype(F32)
    )
    grad_conv_out = (
        exchange_tm(middle[:, 4 * share + wide :].reshape(size, unit, share))
        .reshape(depth, share)
        .astype(F32)
    )

    g1 = gather_tm((0.5 * d1).astype(BF))
    d_f1_out = mm_tn(s1, g1).astype(BF)
    da1 = (mm_nt(g1, f1_out) * silu_slope(a1)).astype(BF)
    d_f1_in = mm_tn(h1, da1).astype(BF)
    grad_ffn1_in, grad_ffn1_out = ffn_return(d_f1_in, d_f1_out, ffn1_in.shape, ffn1_out.shape)
    back, gain_one = norm_back(
        scatter_tm(mm_nt(da1, f1_in).astype(BF)), normed_one, inverse_one, norm_gains[0]
    )
    grad_frames = (d1 + back).astype(BF)[None]

    table_row = lax.dynamic_update_slice_in_dim(
        jnp.zeros(rel_table.shape, F32), d_table, t * heads, 0
    ).reshape(1, -1)
    table_row = jnp.pad(table_row, ((0, 0), (0, width - table_row.shape[1])))
    small = jnp.concatenate(
        [
            jnp.stack([gain_one, gain_two, gain_three, gain_four, gain_five]),
            placed(jnp.stack(d_kernel)),
            placed(bn_part),
            table_row,
        ],
        axis=0,
    )
    small = sum_axis(sum_axis(small, "tm"), "rows")
    table_size = rel_table.shape[0] * rel_table.shape[1]
    return (
        output,
        grad_frames,
        grad_ffn1_in,
        grad_ffn1_out,
        grad_query,
        grad_key,
        grad_value,
        grad_attn_out,
        grad_conv_in,
        grad_conv_out,
        grad_ffn2_in,
        grad_ffn2_out,
        small[:5],
        small[5 : 5 + taps],
        small[6 + taps],
        small[5 + taps],
        small[7 + taps, :table_size].reshape(rel_table.shape),
    )


def solution(mesh):
    split, copied = P("rows", "tm"), P()
    sequence = P("rows", "tm", None)
    return jax.shard_map(
        shards,
        mesh=mesh,
        in_specs=(sequence, P("rows", None)) + (split,) * 10 + (copied,) * 5 + (sequence,),
        out_specs=(sequence, sequence) + (split,) * 10 + (copied,) * 5,
        check_vma=False,
    )
```

time: 5700 us -> 701 us (0.12)
  local copies, waits for them, and re-layouts: 4010 us -> 113 us
  waiting for transfers between devices: 1200 us -> 371 us
  blocking collectives: 207 us -> 0 us
  matrix products: 165 us -> 65 us
    gather x34 -> x0, local copies, waits for them, and re-layouts: 3940 us -> none  [the longest x4 3720 us: shards(): biases = [jnp.take(table_local, bucket, axis=1) for bucket in buckets]]
    reduce_scatter x20 -> x1, waiting for transfers between devices: 785 us -> 0.01 us  [shards(): lax.psum_scatter(jnp.concatenate([d_qkv, d_attn_blocks, d_conv_in, d_conv...]
    all_gather x14 -> x4, waiting for transfers between devices: 402 us -> 91.5 us  [the longest x2 77.2 us: ffn_ready(): lax.all_gather(jnp.concatenate([a, b], axis=1), 'rows', axis=0, tiled=True)]
    ppermute x4 -> x77, waiting for transfers between devices: 2.43 us -> 239 us  [the longest x64 208 us: from_peer(): return lax.ppermute(a, 'tm', tm_peer(dx, dc))]
    psum x3 -> x0, blocking collectives: 121 us -> none  [the longest x1 40.5 us: shards(): lax.psum((jnp.sum(grad_shift, axis=0), jnp.sum(grad_shift * normed_bn, ax...]
    dot_general x42 -> x24, matrix products: 165 us -> 65 us  [the longest x8 22.6 us: mm_nt(): lax.dot_general(a, b, (((1,), (1,)), ((), ())), preferred_element_type=F32)]
  transfers between devices with their start and end apart: 40 -> 84, of which waited for: 21 -> 44; matrix products, arithmetic and copies ran while one was open for 74% -> 26% of each run, Pallas kernels for 0% -> 2%
where the time goes in v1:
time: 701 us; the launch traced here: 693 us
  waiting for transfers between devices  371 us (53%)
  local copies, waits for them, and re-layouts  113 us (16%)
  matrix products  65 us (9%)
  starting transfers between devices  57.4 us (8%)
  other arithmetic  53.9 us (8%)
  between operations  17 us (2%)
  Pallas kernels  15.9 us (2%)
    ppermute x64, waiting for transfers between devices, from_peer(): return lax.ppermute(a, 'tm', tm_peer(dx, dc))  208 us
    all_gather x2, waiting for transfers between devices, ffn_ready(): lax.all_gather(jnp.concatenate([a, b], axis=1), 'rows', axis=0, tiled=True)  77.2 us
    ppermute x64, starting transfers between devices, from_peer(): return lax.ppermute(a, 'tm', tm_peer(dx, dc))  47.3 us
    unnamed x206, local copies, waits for them, and re-layouts  40.7 us
    unnamed x9, waiting for transfers between devices  39.8 us
    ppermute x11, waiting for transfers between devices, sum_axis(): v = v + lax.ppermute(v, axis, [(i, i ^ bit) for i in range(size)])  31.6 us
    dot_general x8, matrix products, mm_nt(): lax.dot_general(a, b, (((1,), (1,)), ((), ())), preferred_element_type=F32)  22.6 us
    dot_general x8, matrix products, mm(): return jnp.dot(a, b, preferred_element_type=F32)  21.7 us
  transfers between devices with their start and end apart: 84, of which 44 were waited for; matrix products, arithmetic and copies ran while one was open for 26% of the time, Pallas kernels for 2%

profile of v1, /device:TPU:0, one launch (start us, length us, event | category | flops | bytes accessed | tf_op | source)
XLA Modules:
  0.0 692.5 jit_solution(935599209279903675)
XLA Ops:
  23.8 12.5 %collective-permute-done.1 = bf16[256,1024]{1,0:T(8,128)(2,1)} collective-permute-done((bf16[256,1024]{1,0:T(8,128)(2,1)S(1)}, bf16[256,1024]{1,0:T(8,128)(2,1)}, u32[]{:S(2)}, u32[]{:S(2)}) %collective-permute-start.1) | collective-permute-done | bytes 524320 | tf_op jit(solution)/shard_map/ppermute | solution.py:62
  40.1 57.0 %all-gather.5.cloned.1.call-done = bf16[1024,2048]{0,1:T(8,128)(2,1)} async-done(((bf16[128,2048]{0,1:T(8,128)(2,1)}), bf16[1024,2048]{0,1:T(8,128)(2,1)}) %all-gather.5.cloned.1.call-update) | async-done | bytes 4194320 | tf_op jit(solution)/shard_map/all_gather | solution.py:149
  110.8 8.1 %collective-permute-start.7 = (bf16[256,1024]{1,0:T(8,128)(2,1)}, bf16[256,1024]{1,0:T(8,128)(2,1)S(1)}, u32[]{:S(2)}, u32[]{:S(2)}) collective-permute-start(bf16[256,1024]{1,0:T(8,128)(2,1)} %fusion.69), channel_id=1, source_target_pairs={{2,0},{3,1},{0,2},{1,3},{6,4},{7,5},{4,6},{5,7},{10,8},{11,9},{8,1... | collective-permute-start | bytes 1572872 | tf_op jit(solution)/shard_map/ppermute | solution.py:62
  118.9 12.8 %collective-permute-done.7 = bf16[256,1024]{1,0:T(8,128)(2,1)S(1)} collective-permute-done((bf16[256,1024]{1,0:T(8,128)(2,1)}, bf16[256,1024]{1,0:T(8,128)(2,1)S(1)}, u32[]{:S(2)}, u32[]{:S(2)}) %collective-permute-start.7) | collective-permute-done | bytes 524320 | tf_op jit(solution)/shard_map/ppermute | solution.py:62
  149.5 14.2 %all-gather.7.cloned.1.call-done = bf16[1024,1024]{1,0:T(8,128)(2,1)} async-done(((bf16[128,1024]{1,0:T(8,128)(2,1)}), bf16[1024,1024]{1,0:T(8,128)(2,1)}) %all-gather.7.cloned.1.call-update) | async-done | bytes 2097168 | tf_op jit(solution)/shard_map/all_gather | solution.py:410
  213.1 11.5 %collective-permute-done.15 = bf16[256,1024]{1,0:T(8,128)(2,1)} collective-permute-done((bf16[256,1024]{1,0:T(8,128)(2,1)}, bf16[256,1024]{1,0:T(8,128)(2,1)}, u32[]{:S(2)}, u32[]{:S(2)}) %collective-permute-start.15) | collective-permute-done | bytes 524320 | tf_op jit(solution)/shard_map/ppermute | solution.py:62
  255.3 12.5 %collective-permute-done.27 = bf16[256,1024]{1,0:T(8,128)(2,1)S(1)} collective-permute-done((bf16[256,1024]{1,0:T(8,128)(2,1)S(1)}, bf16[256,1024]{1,0:T(8,128)(2,1)S(1)}, u32[]{:S(2)}, u32[]{:S(2)}) %collective-permute-start.27) | collective-permute-done | bytes 524320 | tf_op jit(solution)/shard_map/ppermute | solution.py:62
  272.5 11.7 %collective-permute-done.29 = bf16[256,1024]{1,0:T(8,128)(2,1)S(1)} collective-permute-done((bf16[256,1024]{1,0:T(8,128)(2,1)S(1)}, bf16[256,1024]{1,0:T(8,128)(2,1)S(1)}, u32[]{:S(2)}, u32[]{:S(2)}) %collective-permute-start.29) | collective-permute-done | bytes 524320 | tf_op jit(solution)/shard_map/ppermute | solution.py:62
  286.9 20.2 %all-gather.11.cloned.1.call-done = bf16[1024,2048]{0,1:T(8,128)(2,1)} async-done(((bf16[128,2048]{0,1:T(8,128)(2,1)}), bf16[1024,2048]{0,1:T(8,128)(2,1)}) %all-gather.11.cloned.1.call-update) | async-done | bytes 4194320 | tf_op jit(solution)/shard_map/all_gather | solution.py:149
  318.2 13.4 %collective-permute-done.35 = bf16[256,1024]{1,0:T(8,128)(2,1)S(1)} collective-permute-done((bf16[256,1024]{1,0:T(8,128)(2,1)S(1)}, bf16[256,1024]{1,0:T(8,128)(2,1)S(1)}, u32[]{:S(2)}, u32[]{:S(2)}) %collective-permute-start.35) | collective-permute-done | bytes 524320 | tf_op jit(solution)/shard_map/ppermute | solution.py:62
  334.8 12.5 %collective-permute-done.37 = bf16[256,1024]{1,0:T(8,128)(2,1)S(1)} collective-permute-done((bf16[256,1024]{1,0:T(8,128)(2,1)S(1)}, bf16[256,1024]{1,0:T(8,128)(2,1)S(1)}, u32[]{:S(2)}, u32[]{:S(2)}) %collective-permute-start.37) | collective-permute-done | bytes 524320 | tf_op jit(solution)/shard_map/ppermute | solution.py:62
  359.0 13.4 %collective-permute-done.40 = bf16[256,1024]{1,0:T(8,128)(2,1)S(1)} collective-permute-done((bf16[256,1024]{1,0:T(8,128)(2,1)S(1)}, bf16[256,1024]{1,0:T(8,128)(2,1)S(1)}, u32[]{:S(2)}, u32[]{:S(2)}) %collective-permute-start.40) | collective-permute-done | bytes 524320 | tf_op jit(solution)/shard_map/ppermute | solution.py:62
  378.2 9.9 %collective-permute-done.42 = bf16[256,1024]{1,0:T(8,128)(2,1)S(1)} collective-permute-done((bf16[256,1024]{1,0:T(8,128)(2,1)S(1)}, bf16[256,1024]{1,0:T(8,128)(2,1)S(1)}, u32[]{:S(2)}, u32[]{:S(2)}) %collective-permute-start.42) | collective-permute-done | bytes 524320 | tf_op jit(solution)/shard_map/ppermute | solution.py:62
  399.2 6.5 copy.271
  427.7 12.5 %collective-permute-done.48 = bf16[256,1024]{1,0:T(8,128)(2,1)S(1)} collective-permute-done((bf16[256,1024]{1,0:T(8,128)(2,1)S(1)}, bf16[256,1024]{1,0:T(8,128)(2,1)S(1)}, u32[]{:S(2)}, u32[]{:S(2)}) %collective-permute-start.48) | collective-permute-done | bytes 524320 | tf_op jit(solution)/shard_map/ppermute | solution.py:62
  450.7 6.8 collective-permute-done.50
  474.2 9.5 %shard_map.306 = (bf16[1024,768]{1,0:T(8,128)(2,1)S(1)}, f32[2,128,640]{2,1,0:T(8,128)S(1)}) custom-call(f32[2,17]{1,0:T(2,128)S(1)} %constant_dynamic-slice_fusion.21.tab_ref, s32[1,1024]{1,0:T(1,128)S(1)} %copy-done.2, s32[1024,1]{1,0:T(8,128)S(1)} %copy.201.seg_col_ref, bf16[1024,768]{1,0:T(8,128)(2,1)S(1)} %convolution_convert_fusion.13.q_ref.k_ref.v_ref, ...), custom_call_target="tpu_custom_call" | custom-call | flops 2684354560 | bytes 4194304 | tf_op jit(solution)/shard_map/pallas_call | solution.py:310
  503.3 12.7 %collective-permute-done.53 = bf16[256,1024]{1,0:T(8,128)(2,1)S(1)} collective-permute-done((bf16[256,1024]{1,0:T(8,128)(2,1)S(1)}, bf16[256,1024]{1,0:T(8,128)(2,1)S(1)}, u32[]{:S(2)}, u32[]{:S(2)}) %collective-permute-start.53) | collective-permute-done | bytes 524320 | tf_op jit(solution)/shard_map/ppermute | solution.py:62
  519.9 12.0 %collective-permute-done.55 = bf16[256,1024]{1,0:T(8,128)(2,1)S(1)} collective-permute-done((bf16[256,1024]{1,0:T(8,128)(2,1)S(1)}, bf16[256,1024]{1,0:T(8,128)(2,1)S(1)}, u32[]{:S(2)}, u32[]{:S(2)}) %collective-permute-start.55) | collective-permute-done | bytes 524320 | tf_op jit(solution)/shard_map/ppermute | solution.py:62
  545.8 6.8 copy.267
  572.4 11.4 %collective-permute-done.58 = bf16[256,1024]{1,0:T(8,128)(2,1)S(1)} collective-permute-done((bf16[256,1024]{1,0:T(8,128)(2,1)S(1)}, bf16[256,1024]{1,0:T(8,128)(2,1)S(1)}, u32[]{:S(2)}, u32[]{:S(2)}) %collective-permute-start.58) | collective-permute-done | bytes 524320 | tf_op jit(solution)/shard_map/ppermute | solution.py:62
  599.5 7.8 %collective-permute-done.75 = f32[13,1024]{1,0:T(8,128)S(1)} collective-permute-done((f32[13,1024]{1,0:T(8,128)S(1)}, f32[13,1024]{1,0:T(8,128)S(1)}, u32[]{:S(2)}, u32[]{:S(2)}) %collective-permute-start.75) | collective-permute-done | bytes 53280 | tf_op jit(solution)/shard_map/ppermute | solution.py:125
  609.9 7.8 %collective-permute-done.76 = f32[13,1024]{1,0:T(8,128)S(1)} collective-permute-done((f32[13,1024]{1,0:T(8,128)S(1)}, f32[13,1024]{1,0:T(8,128)S(1)}, u32[]{:S(2)}, u32[]{:S(2)}) %collective-permute-start.76) | collective-permute-done | bytes 53280 | tf_op jit(solution)/shard_map/ppermute | solution.py:125
  631.8 39.7 %reduce-scatter.10.cloned.1.call-done = bf16[128,2048]{1,0:T(8,128)(2,1)} async-done(((bf16[1024,2048]{1,0:T(8,128)(2,1)}), bf16[128,2048]{1,0:T(8,128)(2,1)}) %reduce-scatter.10.cloned.1.call-update) | async-done | bytes 524304
  (660 shorter events, 332.7 us)
Async XLA Ops:
  7.2 90.0 %all-gather.5.cloned.1.call-start = ((), (), s32[]{:S(2)}) async-start(), calls=%async_computation.3 | async-start | bytes 4718592 | tf_op jit(solution)/shard_map/all_gather | solution.py:149
  20.7 143.1 %all-gather.7.cloned.1.call-start = ((), (), s32[]{:S(2)}) async-start(), calls=%async_computation.4 | async-start | bytes 2359296 | tf_op jit(solution)/shard_map/all_gather | solution.py:410
  22.1 14.1 %collective-permute-start.1 = (bf16[256,1024]{1,0:T(8,128)(2,1)S(1)}, bf16[256,1024]{1,0:T(8,128)(2,1)}, u32[]{:S(2)}, u32[]{:S(2)}) collective-permute-start(bf16[256,1024]{1,0:T(8,128)(2,1)S(1)} %fusion.23), channel_id=1, source_target_pairs={{2,0},{3,1},{0,2},{1,3},{6,4},{7,5},{4,6},{5,7},{10,8},{11,9},{8,1... | collective-permute-start | bytes 1572872 | tf_op jit(solution)/shard_map/ppermute | solution.py:62
  106.7 123.4 %all-gather.9.cloned.1.call-start = ((), (), s32[]{:S(2)}) async-start(), calls=%async_computation.5 | async-start | bytes 1769472 | tf_op jit(solution)/shard_map/all_gather | solution.py:429
  110.8 20.8 %collective-permute-start.7 = (bf16[256,1024]{1,0:T(8,128)(2,1)}, bf16[256,1024]{1,0:T(8,128)(2,1)S(1)}, u32[]{:S(2)}, u32[]{:S(2)}) collective-permute-start(bf16[256,1024]{1,0:T(8,128)(2,1)} %fusion.69), channel_id=1, source_target_pairs={{2,0},{3,1},{0,2},{1,3},{6,4},{7,5},{4,6},{5,7},{10,8},{11,9},{8,1... | collective-permute-start | bytes 1572872 | tf_op jit(solution)/shard_map/ppermute | solution.py:62
  133.5 15.3 %collective-permute-start.9 = (bf16[256,1024]{1,0:T(8,128)(2,1)}, bf16[256,1024]{1,0:T(8,128)(2,1)}, u32[]{:S(2)}, u32[]{:S(2)}) collective-permute-start(bf16[256,1024]{1,0:T(8,128)(2,1)} %get-tuple-element.188), channel_id=1, source_target_pairs={{2,0},{3,1},{0,2},{1,3},{6,4},{7,5},{4,6},{5,7},{10,8},{11,9},{8,1... | collective-permute-start | bytes 1572872 | tf_op jit(solution)/shard_map/ppermute | solution.py:62
  135.9 29.5 %collective-permute-start.8 = (bf16[256,1024]{1,0:T(8,128)(2,1)}, bf16[256,1024]{1,0:T(8,128)(2,1)}, u32[]{:S(2)}, u32[]{:S(2)}) collective-permute-start(bf16[256,1024]{1,0:T(8,128)(2,1)} %get-tuple-element.188), channel_id=1, source_target_pairs={{1,0},{0,1},{3,2},{2,3},{5,4},{4,5},{7,6},{6,7},{9,8},{8,9},{11,10... | collective-permute-start | bytes 1572872 | tf_op jit(solution)/shard_map/ppermute | solution.py:62
  136.7 47.9 %collective-permute-start.17 = (bf16[128,128]{0,1:T(8,128)(2,1)}, bf16[128,128]{0,1:T(8,128)(2,1)}, u32[]{:S(2)}, u32[]{:S(2)}) collective-permute-start(bf16[128,128]{0,1:T(8,128)(2,1)} %get-tuple-element.238), channel_id=1, source_target_pairs={{1,0},{0,1},{3,2},{2,3},{5,4},{4,5},{7,6},{6,7},{9,8},{8,9},{11,10... | collective-permute-start | bytes 98312 | tf_op jit(solution)/shard_map/ppermute | solution.py:62
  137.2 48.2 %collective-permute-start.18 = (bf16[128,128]{0,1:T(8,128)(2,1)}, bf16[128,128]{0,1:T(8,128)(2,1)}, u32[]{:S(2)}, u32[]{:S(2)}) collective-permute-start(bf16[128,128]{0,1:T(8,128)(2,1)} %get-tuple-element.237), channel_id=1, source_target_pairs={{2,0},{3,1},{0,2},{1,3},{6,4},{7,5},{4,6},{5,7},{10,8},{11,9},{8,1... | collective-permute-start | bytes 98312 | tf_op jit(solution)/shard_map/ppermute | solution.py:62
  141.0 45.2 %collective-permute-start.19 = (bf16[128,128]{0,1:T(8,128)(2,1)S(1)}, bf16[128,128]{0,1:T(8,128)(2,1)S(1)}, u32[]{:S(2)}, u32[]{:S(2)}) collective-permute-start(bf16[128,128]{0,1:T(8,128)(2,1)S(1)} %copy-done.62), channel_id=1, source_target_pairs={{3,0},{2,1},{1,2},{0,3},{7,4},{6,5},{5,6},{4,7},{11,8},{10,9},{9,1... | collective-permute-start | bytes 98312 | tf_op jit(solution)/shard_map/ppermute | solution.py:62
  148.8 20.3 %collective-permute-start.10 = (bf16[256,1024]{1,0:T(8,128)(2,1)}, bf16[256,1024]{1,0:T(8,128)(2,1)}, u32[]{:S(2)}, u32[]{:S(2)}) collective-permute-start(bf16[256,1024]{1,0:T(8,128)(2,1)} %collective-permute-done.9), channel_id=1, source_target_pairs={{1,0},{0,1},{3,2},{2,3},{5,4},{4,5},{7,6},{6,7},{9,8},{8,9},{11,10... | collective-permute-start | bytes 1572872 | tf_op jit(solution)/shard_map/ppermute | solution.py:62
  165.4 18.0 %collective-permute-start.21 = (bf16[32,256]{1,0:T(8,128)(2,1)S(1)}, bf16[32,256]{1,0:T(8,128)(2,1)S(1)}, u32[]{:S(2)}, u32[]{:S(2)}) collective-permute-start(bf16[32,256]{1,0:T(8,128)(2,1)S(1)} %copy-done.71), channel_id=1, source_target_pairs={{2,0},{3,1},{0,2},{1,3},{6,4},{7,5},{4,6},{5,7},{10,8},{11,9},{8,1... | collective-permute-start | bytes 49160 | tf_op jit(solution)/shard_map/ppermute | solution.py:62
  169.2 15.5 %collective-permute-start.22 = (bf16[32,256]{1,0:T(8,128)(2,1)S(1)}, bf16[32,256]{1,0:T(8,128)(2,1)S(1)}, u32[]{:S(2)}, u32[]{:S(2)}) collective-permute-start(bf16[32,256]{1,0:T(8,128)(2,1)S(1)} %copy-done.70), channel_id=1, source_target_pairs={{3,0},{2,1},{1,2},{0,3},{7,4},{6,5},{5,6},{4,7},{11,8},{10,9},{9,1... | collective-permute-start | bytes 49160 | tf_op jit(solution)/shard_map/ppermute | solution.py:62
  187.0 120.0 %all-gather.11.cloned.1.call-start = ((), (), s32[]{:S(2)}) async-start(), calls=%async_computation.6 | async-start | bytes 4718592 | tf_op jit(solution)/shard_map/all_gather | solution.py:149
  191.4 15.1 %collective-permute-start.13 = (bf16[256,1024]{1,0:T(8,128)(2,1)}, bf16[256,1024]{1,0:T(8,128)(2,1)}, u32[]{:S(2)}, u32[]{:S(2)}) collective-permute-start(bf16[256,1024]{1,0:T(8,128)(2,1)} %fusion.70), channel_id=1, source_target_pairs={{2,0},{3,1},{0,2},{1,3},{6,4},{7,5},{4,6},{5,7},{10,8},{11,9},{8,1... | collective-permute-start | bytes 1572872 | tf_op jit(solution)/shard_map/ppermute | solution.py:62
  193.7 19.1 %collective-permute-start.32 = (bf16[256,256]{0,1:T(8,128)(2,1)}, bf16[256,256]{0,1:T(8,128)(2,1)S(1)}, u32[]{:S(2)}, u32[]{:S(2)}) collective-permute-start(bf16[256,256]{0,1:T(8,128)(2,1)} %get-tuple-element.221), channel_id=1, source_target_pairs={{2,0},{3,1},{0,2},{1,3},{6,4},{7,5},{4,6},{5,7},{10,8},{11,9},{8,1... | collective-permute-start | bytes 393224 | tf_op jit(solution)/shard_map/ppermute | solution.py:62
  194.3 18.6 %collective-permute-start.33 = (bf16[256,256]{0,1:T(8,128)(2,1)}, bf16[256,256]{0,1:T(8,128)(2,1)S(1)}, u32[]{:S(2)}, u32[]{:S(2)}) collective-permute-start(bf16[256,256]{0,1:T(8,128)(2,1)} %get-tuple-element.218), channel_id=1, source_target_pairs={{3,0},{2,1},{1,2},{0,3},{7,4},{6,5},{5,6},{4,7},{11,8},{10,9},{9,1... | collective-permute-start | bytes 393224 | tf_op jit(solution)/shard_map/ppermute | solution.py:62
  225.4 336.8 %reduce-scatter.14.cloned.1.call-start = ((), (), s32[]{:S(2)}) async-start(), calls=%async_computation.9 | async-start | bytes 4718592
  405.8 213.8 %reduce-scatter.12.cloned.1.call-start = ((), (), s32[]{:S(2)}) async-start(), calls=%async_computation.8 | async-start | bytes 4128768 | tf_op jit(solution)/shard_map/reduce_scatter | solution.py:542
  445.4 16.2 %collective-permute-start.49 = (bf16[256,1024]{1,0:T(8,128)(2,1)}, bf16[256,1024]{1,0:T(8,128)(2,1)}, u32[]{:S(2)}, u32[]{:S(2)}) collective-permute-start(bf16[256,1024]{1,0:T(8,128)(2,1)} %get-tuple-element.163), channel_id=1, source_target_pairs={{1,0},{0,1},{3,2},{2,3},{5,4},{4,5},{7,6},{6,7},{9,8},{8,9},{11,10... | collective-permute-start | bytes 1572872 | tf_op jit(solution)/shard_map/ppermute | solution.py:62
  493.7 177.7 %reduce-scatter.10.cloned.1.call-start = ((), (), s32[]{:S(2)}) async-start(), calls=%async_computation.7 | async-start | bytes 4718592
  501.7 14.3 %collective-permute-start.53 = (bf16[256,1024]{1,0:T(8,128)(2,1)S(1)}, bf16[256,1024]{1,0:T(8,128)(2,1)S(1)}, u32[]{:S(2)}, u32[]{:S(2)}) collective-permute-start(bf16[256,1024]{1,0:T(8,128)(2,1)S(1)} %fusion.76), channel_id=1, source_target_pairs={{2,0},{3,1},{0,2},{1,3},{6,4},{7,5},{4,6},{5,7},{10,8},{11,9},{8,1... | collective-permute-start | bytes 1572872 | tf_op jit(solution)/shard_map/ppermute | solution.py:62
  567.9 15.9 %collective-permute-start.58 = (bf16[256,1024]{1,0:T(8,128)(2,1)S(1)}, bf16[256,1024]{1,0:T(8,128)(2,1)S(1)}, u32[]{:S(2)}, u32[]{:S(2)}) collective-permute-start(bf16[256,1024]{1,0:T(8,128)(2,1)S(1)} %fusion.77), channel_id=1, source_target_pairs={{2,0},{3,1},{0,2},{1,3},{6,4},{7,5},{4,6},{5,7},{10,8},{11,9},{8,1... | collective-permute-start | bytes 1572872 | tf_op jit(solution)/shard_map/ppermute | solution.py:62
  628.5 45.5 %collective-permute-start.62 = (bf16[128,256]{0,1:T(8,128)(2,1)S(1)}, bf16[128,256]{0,1:T(8,128)(2,1)S(1)}, u32[]{:S(2)}, u32[]{:S(2)}) collective-permute-start(bf16[128,256]{0,1:T(8,128)(2,1)S(1)} %copy.286), channel_id=1, source_target_pairs={{0,0},{1,8},{2,16},{3,24},{4,1},{5,9},{6,17},{7,25},{8,2},{9,10},{... | collective-permute-start | bytes 196616 | tf_op jit(solution)/shard_map/ppermute | solution.py:551
  (151 other events, 1194.0 us)
Sparse Core Ops, SparseCore 0:
  20.8 76.3 all-gather.4
  106.8 56.9 all-gather.6
  187.2 42.6 all-gather.8
  232.3 74.7 all-gather.10
  405.9 86.0 reduce-scatter.13
  496.0 80.6 reduce-scatter.11
  580.8 90.6 reduce-scatter.9

commit v2 on v1

v2 whole, which is shorter than its diff:
```python
import functools

import jax
import jax.numpy as jnp
from jax import lax
from jax.experimental import pallas as pl
from jax.experimental.pallas import tpu as pltpu
from jax.sharding import PartitionSpec as P

HEAD_DIM = 128
RELMAX = 8
LANES = 128
EPS = 1e-05
BF = jnp.bfloat16
F32 = jnp.float32


def mm(a, b):
    return jnp.dot(a, b, preferred_element_type=F32)


def mm_tn(a, b):
    return lax.dot_general(a, b, (((0,), (0,)), ((), ())), preferred_element_type=F32)


def mm_nt(a, b):
    return lax.dot_general(a, b, (((1,), (1,)), ((), ())), preferred_element_type=F32)


def silu_slope(a):
    s = jax.nn.sigmoid(a)
    return s * (1.0 + a * (1.0 - s))


def norm_rows(v, g):
    center = v - jnp.mean(v, axis=-1, keepdims=True)
    spread = jnp.mean(center * center, axis=-1, keepdims=True)
    inverse = lax.rsqrt(spread + EPS)
    normed = center * inverse
    return normed * g, normed, inverse


def norm_back(grad, normed, inverse, g):
    scaled = grad * g
    back = inverse * (
        scaled
        - jnp.mean(scaled, axis=-1, keepdims=True)
        - normed * jnp.mean(scaled * normed, axis=-1, keepdims=True)
    )
    return back, jnp.sum(grad * normed, axis=0)


def tm_peer(dx, dc):
    size = lax.axis_size("tm")
    chips = size // 2
    return [
        (((t // 2 + dx) % chips) * 2 + ((t % 2) ^ dc), t) for t in range(size)
    ]


def from_peer(a, dx, dc):
    return lax.ppermute(a, "tm", tm_peer(dx, dc))


def peer_index(dx, dc):
    chips = lax.axis_size("tm") // 2
    t = lax.axis_index("tm")
    return lax.rem(t // 2 + dx, chips) * 2 + jnp.bitwise_xor(t % 2, dc)


def gather_tm(a):
    size = lax.axis_size("tm")
    n, w = a.shape
    far = [from_peer(a, dx, 0) for dx in range(1, size // 2)]
    held = {(0, 0): a, (0, 1): from_peer(a, 0, 1)}
    for dx, b in enumerate(far, 1):
        held[dx, 0] = b
        held[dx, 1] = from_peer(b, 0, 1)
    out = jnp.zeros((size, n, w), a.dtype)
    for (dx, dc), b in held.items():
        out = lax.dynamic_update_index_in_dim(out, b, peer_index(dx, dc), 0)
    return out.reshape(size * n, w)


def scatter_tm(p, beside=()):
    size = lax.axis_size("tm")
    chips = size // 2
    t = lax.axis_index("tm")
    x, c = t // 2, t % 2
    w = p.shape[1]
    p = p.reshape(chips, 2, p.shape[0] // size, w)
    mine = lax.dynamic_index_in_dim(p, c, 1, keepdims=False)
    theirs = lax.dynamic_index_in_dim(p, 1 - c, 1, keepdims=False).astype(BF)
    q = mine.astype(F32) + from_peer(theirs, 0, 1).astype(F32)
    total = lax.dynamic_index_in_dim(q, x, 0, keepdims=False)
    for dx in range(1, chips):
        piece = lax.dynamic_index_in_dim(q, lax.rem(x + chips - dx, chips), 0, keepdims=False)
        total = total + after(from_peer(piece.astype(BF), dx, 0), *beside).astype(F32)
    return total


def spread(a, local):
    chips = lax.axis_size("tm") // 2
    far = [from_peer(a, dx, 0) for dx in range(1, chips)]
    near = (a, from_peer(a, 0, 1))
    done = local(near)
    far = [after(b, *jax.tree.leaves(done)) for b in far]
    return [near] + [(b, from_peer(b, 0, 1)) for b in far], done


def collect(mine, theirs, beside=()):
    chips = lax.axis_size("tm") // 2
    got = []
    for dx in range(1, chips):
        q = mine[dx] + from_peer(theirs[dx], 0, 1).astype(F32)
        got.append(from_peer(q.astype(BF), chips - dx, 0))
    near = from_peer(theirs[0], 0, 1)
    got = [after(v, near, *beside) for v in got]
    return [mine[0], near] + got


def exchange_tm(pieces):
    size = lax.axis_size("tm")
    chips = size // 2
    t = lax.axis_index("tm")
    out = jnp.zeros(pieces.shape, pieces.dtype)
    out = lax.dynamic_update_index_in_dim(
        out, lax.dynamic_index_in_dim(pieces, t, 0, keepdims=False), t, 0
    )
    for dx in range(chips):
        for dc in range(2):
            if dx or dc:
                piece = lax.dynamic_index_in_dim(
                    pieces, peer_index(chips - dx, dc), 0, keepdims=False
                )
                out = lax.dynamic_update_index_in_dim(
                    out, from_peer(piece, dx, dc), peer_index(dx, dc), 0
                )
    return out


def sum_axis(v, axis):
    size, bit = lax.axis_size(axis), 1
    while bit < size:
        v = v + lax.ppermute(v, axis, [(i, i ^ bit) for i in range(size)])
        bit *= 2
    return v


def pack(a, width):
    m, w = a.shape
    f = width // w
    if f * w != width or m % f:
        return a.reshape(-1, width)
    return jnp.concatenate([a[i * (m // f) : (i + 1) * (m // f)] for i in range(f)], axis=1)


def unpack(full, w):
    rows, n, width = full.shape
    f = width // w
    if f * w != width:
        return full.reshape(-1, w)
    if f == 1:
        return full.reshape(-1, w)
    parts = [full[:, None, :, i * w : (i + 1) * w] for i in range(f)]
    return jnp.concatenate(parts, axis=1).reshape(-1, w)


def gather_rows(parts):
    width = max(p.shape[1] for p in parts)
    packed = [pack(p, width) for p in parts]
    full = lax.all_gather(jnp.concatenate(packed, axis=0), "rows", axis=0, tiled=False)
    out, at = [], 0
    for p, q in zip(parts, packed):
        out.append(unpack(full[:, at : at + q.shape[0]], p.shape[1]))
        at += q.shape[0]
    return out


def pack_rows(p, width):
    rows = lax.axis_size("rows")
    m, w = p.shape[0] // rows, p.shape[1]
    f = width // w
    q = p.reshape(rows, m, w)
    if f * w != width or m % f:
        return q.reshape(rows, -1, width)
    return jnp.concatenate([q[:, i * (m // f) : (i + 1) * (m // f)] for i in range(f)], axis=2)


def pack_grads(parts):
    width = max(p.shape[1] for p in parts)
    return jnp.concatenate([pack_rows(p, width) for p in parts], axis=1)


def unpack_grads(total, parts):
    rows = lax.axis_size("rows")
    width = total.shape[1]
    out, at = [], 0
    for p in parts:
        n = p.size // (rows * width)
        out.append(unpack(total[None, at : at + n], p.shape[1]))
        at += n
    return out


def scatter_rows(packed):
    return lax.psum_scatter(packed, "rows", scatter_dimension=0, tiled=False)


def scatter_rows_near(packed):
    got = lax.all_to_all(packed, "rows", 0, 0, tiled=True)
    return jnp.sum(got.astype(F32), axis=0).astype(BF)


def gather_weights(pair, more=None):
    parts = list(pair) + ([] if more is None else [more])
    m, width = parts[0].shape
    if all(p.shape == (m, width) for p in parts) and m % 16 == 0:
        full = lax.all_gather(jnp.concatenate(parts, axis=0), "rows", axis=0, tiled=False)
        out = [Weight(full, i * m, m) for i in range(len(parts))]
    else:
        out = [Weight(lax.all_gather(p, "rows", axis=0, tiled=True)) for p in parts]
    return (out[:2], out[2]) if more is not None else out


def exchange_all(pieces):
    size = lax.axis_size("tm")
    width = max(p.shape[2] for p in pieces)
    if any(p[0].size % width for p in pieces):
        return [exchange_tm(p) for p in pieces]
    flat = [p.reshape(size, -1, width) for p in pieces]
    got = exchange_tm(jnp.concatenate(flat, axis=1))
    out, at = [], 0
    for p, q in zip(pieces, flat):
        out.append(got[:, at : at + q.shape[1]].reshape(p.shape))
        at += q.shape[1]
    return out


def after(a, *others):
    return lax.optimization_barrier((a,) + others)[0]


def ffn_pieces(w_in, w_out):
    size = lax.axis_size("tm")
    unit = w_out.shape[0] // size
    m, w = w_in.shape
    a = w_in.reshape(m, w // (size * unit), size, unit).transpose(2, 0, 1, 3)
    return [a.reshape(size, m, w // size), w_out.reshape(size, unit, w_out.shape[1])]


def side_by_side(pieces):
    return pieces.transpose(1, 0, 2).reshape(pieces.shape[1], -1)


def ffn_return(a, b, like_in, like_out):
    size = lax.axis_size("tm")
    a = a.reshape(a.shape[0], size, -1).transpose(1, 0, 2)
    b = b.reshape(b.shape[0], size, -1).transpose(1, 0, 2)
    a, b = exchange_all([a, b])
    unit = like_out[0] // size
    m, w = like_in
    a = a.reshape(size, m, w // (size * unit), unit).transpose(1, 2, 0, 3).reshape(m, w)
    return a.astype(F32), b.reshape(like_out).astype(F32)


def head_rows_perm():
    rows, size = lax.axis_size("rows"), lax.axis_size("tm")
    perm = []
    for r in range(rows):
        for t in range(size):
            k, u = divmod(r, size)
            perm.append(((t * (rows // size) + k) * size + u, r * size + t))
    return perm


def params(limit):
    return pltpu.CompilerParams(vmem_limit_bytes=limit * 1024 * 1024)


def whole(shape):
    return pl.BlockSpec(shape, lambda *_: (0,) * len(shape))


def flat(v):
    return v.reshape(-1, v.shape[-1])


def cost(flops, *arrays):
    return pl.CostEstimate(
        flops=flops, bytes_accessed=sum(a.size * a.dtype.itemsize for a in arrays), transcendentals=0
    )


class Weight:
    def __init__(self, array, first=0, m=None):
        self.array, self.first, self.m = array, first, m
        if m is not None:
            self.shape = (array.shape[0] * m, array.shape[2])
        else:
            self.shape = array.shape

    def all(self):
        if self.m is None:
            return whole(self.shape)
        unit = self.first // self.m
        return pl.BlockSpec(
            (self.array.shape[0], self.m, self.shape[1]), lambda *_: (0, unit, 0)
        )

    def value(self):
        if self.m is None:
            return self.array
        return flat(self.array[:, self.first : self.first + self.m])


def ffn_kernel(h0, h1, w_in, w_out, s_ref, slope_ref, mine, theirs):
    n = h0.shape[0]
    h = jnp.concatenate([h0[...], h1[...]], axis=0)
    w_a, w_b = flat(w_in[...]), flat(w_out[...])
    units = w_a.shape[1]
    total = None
    for half in range(2):
        at = slice(half * units // 2, (half + 1) * units // 2)
        a = mm(h, w_a[:, at])
        sig = jax.nn.sigmoid(a)
        act = (a * sig).astype(BF)
        s_ref[:, at] = act
        slope_ref[:, at] = (sig * (1.0 + a * (1.0 - sig))).astype(BF)
        p = mm(act, w_b[at])
        total = p if total is None else total + p
    mine[...] = total[:n]
    theirs[...] = total[n:].astype(BF)


def ffn(pair, w_in, w_out):
    n, d = pair[0].shape
    units = w_in.shape[1]
    return pl.pallas_call(
        ffn_kernel,
        grid=(1,),
        in_specs=[whole((n, d)), whole((n, d)), w_in.all(), w_out.all()],
        out_specs=[whole((2 * n, units))] * 2 + [whole((n, d))] * 2,
        out_shape=[jax.ShapeDtypeStruct((2 * n, units), BF)] * 2
        + [jax.ShapeDtypeStruct((n, d), F32), jax.ShapeDtypeStruct((n, d), BF)],
        compiler_params=params(24),
        cost_estimate=cost(8 * n * d * units, w_in.array),
    )(*pair, w_in.array, w_out.array)


def ffn_back_kernel(g0, g1, slope, w_in, w_out, da_ref, mine, theirs):
    n = g0.shape[0]
    g = jnp.concatenate([g0[...], g1[...]], axis=0)
    w_a, w_b = flat(w_in[...]), flat(w_out[...])
    units = w_a.shape[1]
    total = None
    for half in range(2):
        at = slice(half * units // 2, (half + 1) * units // 2)
        da = (mm_nt(g, w_b[at]) * slope[:, at].astype(F32)).astype(BF)
        da_ref[:, at] = da
        p = mm_nt(da, w_a[:, at])
        total = p if total is None else total + p
    mine[...] = total[:n]
    theirs[...] = total[n:].astype(BF)


def ffn_back(pair, slope, w_in, w_out):
    n, d = pair[0].shape
    units = w_in.shape[1]
    return pl.pallas_call(
        ffn_back_kernel,
        grid=(1,),
        in_specs=[whole((n, d))] * 2 + [whole((2 * n, units)), w_in.all(), w_out.all()],
        out_specs=[whole((2 * n, units))] + [whole((n, d))] * 2,
        out_shape=[
            jax.ShapeDtypeStruct((2 * n, units), BF),
            jax.ShapeDtypeStruct((n, d), F32),
            jax.ShapeDtypeStruct((n, d), BF),
        ],
        compiler_params=params(24),
        cost_estimate=cost(8 * n * d * units, w_in.array),
    )(*pair, slope, w_in.array, w_out.array)


def ffn_grads_kernel(*refs):
    out = refs[-1]
    count = (len(refs) - 1) // 6
    h, g = refs[: 2 * count], refs[2 * count : 4 * count]
    da, s = refs[4 * count : 5 * count], refs[5 * count : 6 * count]
    half = out.shape[1] // 2
    join = lambda v: jnp.concatenate([r[...] for r in v], axis=0)
    out[:, :half, :] = mm_tn(join(h), join(da)).astype(BF).reshape(out.shape[0], half, -1)
    out[:, half:, :] = mm_tn(join(s), join(g)).astype(BF).reshape(out.shape[0], half, -1)


def ffn_grads(h, g, da, s):
    rows = lax.axis_size("rows")
    n, d = h[0].shape
    units, tile = da[0].shape[1], d // 2
    m = d // rows
    if units != d or tile % m:
        h, g, da, s = (jnp.concatenate(v, axis=0) for v in (h, g, da, s))
        return pack_grads([mm_tn(h, da).astype(BF), mm_tn(s, g).astype(BF)])
    part = pl.BlockSpec((n, tile), lambda j: (0, j))
    column = pl.BlockSpec((2 * n, tile), lambda j: (0, j))
    return pl.pallas_call(
        ffn_grads_kernel,
        grid=(d // tile,),
        in_specs=[part] * len(h)
        + [whole((n, d))] * len(g)
        + [whole((2 * n, units))] * len(da)
        + [column] * len(s),
        out_specs=pl.BlockSpec((tile // m, 2 * m, d), lambda j: (j, 0, 0)),
        out_shape=jax.ShapeDtypeStruct((rows, 2 * m, d), BF),
        compiler_params=params(36),
        cost_estimate=cost(4 * len(h) * n * d * units, *h),
    )(*h, *g, *da, *s)


def add_norm_kernel(*refs, scale):
    x_ref, gain, x_new, h_ref = refs[-4:]
    total = refs[0][...]
    for r in refs[1:-4]:
        total = total + r[...].astype(F32)
    x = x_ref[...] + scale * total
    x_new[...] = x
    h_ref[...] = norm_rows(x, gain[...])[0].astype(BF)


def add_norm(parts, x, gain, scale):
    n, d = x.shape
    return pl.pallas_call(
        functools.partial(add_norm_kernel, scale=scale),
        out_shape=[jax.ShapeDtypeStruct((n, d), F32), jax.ShapeDtypeStruct((n, d), BF)],
        compiler_params=params(12),
        cost_estimate=cost(0, x, x, x),
    )(*parts, x, gain[None])


def turn_kernel(*refs):
    x_ref, gain, cot, out, d_ref, g_ref, gain_ref = refs[-7:]
    total = refs[0][...]
    for r in refs[1:-7]:
        total = total + r[...].astype(F32)
    y, normed, inverse = norm_rows(x_ref[...] + 0.5 * total, gain[...])
    out[...] = y.astype(BF)
    back, gain_sum = norm_back(cot[...].astype(F32), normed, inverse, gain[...])
    d_ref[...] = back
    g_ref[...] = (0.5 * back).astype(BF)
    gain_ref[...] = gain_sum[None]


def turn(parts, x, gain, cot):
    n, d = x.shape
    return pl.pallas_call(
        turn_kernel,
        out_shape=[
            jax.ShapeDtypeStruct((n, d), BF),
            jax.ShapeDtypeStruct((n, d), F32),
            jax.ShapeDtypeStruct((n, d), BF),
            jax.ShapeDtypeStruct((1, d), F32),
        ],
        compiler_params=params(14),
        cost_estimate=cost(0, x, x, x),
    )(*parts, x, gain[None], cot)


def back_norm_kernel(*refs, scale):
    x_ref, gain, prev, d_ref, g_ref, gain_ref = refs[-6:]
    total = refs[0][...]
    for r in refs[1:-6]:
        total = total + r[...].astype(F32)
    _, normed, inverse = norm_rows(x_ref[...], gain[...])
    back, gain_sum = norm_back(total, normed, inverse, gain[...])
    d = prev[...] + back
    d_ref[...] = d
    g_ref[...] = (scale * d).astype(BF)
    gain_ref[...] = gain_sum[None]


def back_norm(parts, x, gain, prev, scale):
    n, d = x.shape
    return pl.pallas_call(
        functools.partial(back_norm_kernel, scale=scale),
        out_shape=[
            jax.ShapeDtypeStruct((n, d), F32),
            jax.ShapeDtypeStruct((n, d), BF),
            jax.ShapeDtypeStruct((1, d), F32),
        ],
        compiler_params=params(14),
        cost_estimate=cost(0, x, x, x),
    )(*parts, x, gain[None], prev)


def project_kernel(h0, h1, w, out):
    h = jnp.concatenate([h0[...], h1[...]], axis=0)
    out[...] = mm(h, flat(w[...])[:, : out.shape[1]]).astype(BF)


def project(pair, w, width):
    n, d = pair[0].shape
    return pl.pallas_call(
        project_kernel,
        grid=(1,),
        in_specs=[whole((n, d)), whole((n, d)), w.all()],
        out_specs=whole((2 * n, width)),
        out_shape=jax.ShapeDtypeStruct((2 * n, width), BF),
        compiler_params=params(20),
        cost_estimate=cost(4 * n * d * width, w.array),
    )(*pair, w.array)


def joined(v, size, depth):
    groups = v.shape[0] // (size * depth)
    cut = lambda k, u: v[(k * size + u) * depth : (k * size + u + 1) * depth]
    return jnp.concatenate(
        [jnp.concatenate([cut(k, u) for u in range(size)], axis=1) for k in range(groups)], axis=0
    )


def fill_bias(tab_ref, head, strip, length):
    lo, hi = length - LANES, length + 2 * LANES
    first, last = tab_ref[head, 0], tab_ref[head, 2 * RELMAX]
    offset = (
        lax.broadcasted_iota(jnp.int32, (LANES, hi - lo), 1)
        - LANES
        - lax.broadcasted_iota(jnp.int32, (LANES, hi - lo), 0)
    )
    tile = jnp.where(offset <= -RELMAX, first, last)
    for b in range(1, 2 * RELMAX):
        tile = jnp.where(offset == b - RELMAX, tab_ref[head, b], tile)
    strip[:, :lo] = jnp.full((LANES, lo), first, F32)
    strip[:, lo:hi] = tile
    strip[:, hi:] = jnp.full((LANES, 2 * length - hi), last, F32)


def biased(q, k, seg_col, seg_row, strip, first, length):
    raw = mm_nt(q, k) * HEAD_DIM ** (-0.5)
    parts = [
        strip[:, length - (first + a) : 2 * length - (first + a)]
        for a in range(0, q.shape[0], LANES)
    ]
    bias = parts[0] if len(parts) == 1 else jnp.concatenate(parts, axis=0)
    return jnp.where(seg_col == seg_row, raw + bias, -jnp.inf)


def head_columns(n, head, heads):
    return pl.ds(pl.multiple_of((n * heads + head) * HEAD_DIM, HEAD_DIM), HEAD_DIM)


def attend_kernel(order, tab_ref, seg_row_ref, seg_col_ref, w_ref, *refs, size, depth):
    chips = size // 2
    pairs, (qkv, att, lse_ref) = refs[:chips], refs[chips : chips + 3]
    mine, theirs = refs[chips + 3 : 2 * chips + 3], refs[2 * chips + 3 : 3 * chips + 3]
    strip = refs[-1]
    length = qkv.shape[0]
    n = length // size
    head, heads = pl.program_id(0), pl.num_programs(0)
    at = lambda i: pl.ds(pl.multiple_of(order[i] * n, n), n)

    @pl.when(head == 0)
    def _():
        for i in range(size):
            qkv[at(i), :] = pairs[i // 2][(i % 2) * n : (i % 2 + 1) * n, :]

    fill_bias(tab_ref, head, strip, length)
    k, v = qkv[:, head_columns(1, head, heads)], qkv[:, head_columns(2, head, heads)]
    block = min(256, length)
    for first in range(0, length, block):
        own = slice(first, first + block)
        q = qkv[own, head_columns(0, head, heads)]
        sc = biased(q, k, seg_col_ref[own, :], seg_row_ref[...], strip, first, length)
        peak = jnp.max(sc, axis=1, keepdims=True)
        e = jnp.exp(sc - peak)
        total = jnp.sum(e, axis=1, keepdims=True)
        p = (e * (1.0 / total)).astype(BF)
        att[own, head_columns(0, head, heads)] = mm(p, v).astype(BF)
        lse_ref[0, own, :] = peak + jnp.log(total)

    @pl.when(head == heads - 1)
    def _():
        share = att.shape[1]
        w = joined(flat(w_ref[...])[:, -share:], size, depth)
        for i in range(size):
            p = mm(att[at(i), :], w)
            if i % 2:
                theirs[i // 2][...] = p.astype(BF)
            else:
                mine[i // 2][...] = p


def attend(order, pairs, seg_row, table, weight):
    size = 2 * len(pairs)
    length, heads = seg_row.shape[0], table.shape[0]
    share, d = heads * HEAD_DIM, weight.shape[0]
    n = length // size
    depth = d // lax.axis_size("rows")
    shape = jax.ShapeDtypeStruct
    out = pl.pallas_call(
        functools.partial(attend_kernel, size=size, depth=depth),
        grid=(heads,),
        in_specs=[
            pl.BlockSpec(memory_space=pltpu.SMEM),
            pl.BlockSpec(memory_space=pltpu.SMEM),
            whole((1, length)),
            whole((length, 1)),
            weight.all(),
        ]
        + [whole((2 * n, 3 * share))] * len(pairs),
        out_specs=[
            whole((length, 3 * share)),
            whole((length, share)),
            pl.BlockSpec((1, length, 1), lambda h: (h, 0, 0)),
        ]
        + [whole((n, d))] * size,
        out_shape=[
            shape((length, 3 * share), BF),
            shape((length, share), BF),
            shape((heads, length, 1), F32),
        ]
        + [shape((n, d), F32)] * len(pairs)
        + [shape((n, d), BF)] * len(pairs),
        scratch_shapes=[pltpu.VMEM((LANES, 2 * length), F32)],
        compiler_params=params(32),
        cost_estimate=cost(6 * length * length * share, *pairs),
    )(order, table, seg_row.reshape(1, length), seg_row.reshape(length, 1), weight.array, *pairs)
    chips = len(pairs)
    return out[0], out[1], out[2], out[3 : 3 + chips], out[3 + chips :]


def att_grad_kernel(g0, g1, w_ref, out, *, size, depth):
    share = out.shape[1]
    w = joined(flat(w_ref[...])[:, -share:], size, depth)
    g = jnp.concatenate([g0[...], g1[...]], axis=0)
    out[...] = mm_nt(g, w).astype(BF)


def att_grad(pair, weight, share):
    n, d = pair[0].shape
    return pl.pallas_call(
        functools.partial(
            att_grad_kernel, size=lax.axis_size("tm"), depth=d // lax.axis_size("rows")
        ),
        grid=(1,),
        in_specs=[whole((n, d)), whole((n, d)), weight.all()],
        out_specs=whole((2 * n, share)),
        out_shape=jax.ShapeDtypeStruct((2 * n, share), BF),
        compiler_params=params(16),
        cost_estimate=cost(4 * n * d * share, weight.array),
    )(*pair, weight.array)


def attend_back_kernel(
    order, tab_ref, seg_row_ref, seg_col_ref, w_ref, qkv, lse_ref, *refs, size
):
    chips = size // 2
    pairs, (dqkv_ref, band_ref) = refs[:chips], refs[chips : chips + 2]
    mine, theirs = refs[chips + 2 : 2 * chips + 2], refs[2 * chips + 2 : 3 * chips + 2]
    strip, dk_sum, dv_sum, grad = refs[-4:]
    length = qkv.shape[0]
    n = length // size
    block = min(256, length)
    head, heads = pl.program_id(0), pl.num_programs(0)
    rows_of = lambda i: pl.ds(pl.multiple_of(order[i] * n, n), n)

    @pl.when(head == 0)
    def _():
        for i in range(size):
            grad[rows_of(i), :] = pairs[i // 2][(i % 2) * n : (i % 2 + 1) * n, :]

    fill_bias(tab_ref, head, strip, length)
    k, v = qkv[:, head_columns(1, head, heads)], qkv[:, head_columns(2, head, heads)]
    scale = HEAD_DIM ** (-0.5)
    at = lambda n: head_columns(n, head, heads)
    low = jnp.zeros((LANES, LANES), F32)
    high = jnp.zeros((LANES, LANES), F32)
    band = [jnp.zeros((LANES, LANES), F32) for _ in range(3)]
    for first in range(0, length, block):
        own = slice(first, first + block)
        q, do = qkv[own, at(0)], grad[own, at(0)]
        sc = biased(q, k, seg_col_ref[own, :], seg_row_ref[...], strip, first, length)
        p = jnp.exp(sc - lse_ref[0, own, :])
        dp = mm_nt(do, v)
        inner = jnp.sum(p * dp, axis=1, keepdims=True)
        ds = (p * (dp - inner)).astype(BF)
        dv = mm_tn(p.astype(BF), do)
        dk = mm_tn(ds, q)
        if first == 0:
            dv_sum[...] = dv
            dk_sum[...] = dk
        else:
            dv_sum[...] += dv
            dk_sum[...] += dk
        dqkv_ref[own, at(0)] = (mm(ds, k) * scale).astype(BF)
        wide = ds.astype(F32)
        for a in range(0, block, LANES):
            for b in range(0, length, LANES):
                part = wide[a : a + LANES, b : b + LANES]
                apart = (b - first - a) // LANES
                if apart < -1:
                    low = low + part
                elif apart > 1:
                    high = high + part
                else:
                    band[apart + 1] = band[apart + 1] + part
    dqkv_ref[:, at(1)] = (dk_sum[...] * scale).astype(BF)
    dqkv_ref[:, at(2)] = dv_sum[...].astype(BF)
    for i, part in enumerate([low] + band + [high]):
        band_ref[0, :, i * LANES : (i + 1) * LANES] = part

    @pl.when(head == heads - 1)
    def _():
        w = flat(w_ref[...])[:, : dqkv_ref.shape[1]]
        for i in range(size):
            p = mm_nt(dqkv_ref[rows_of(i), :], w)
            if i % 2:
                theirs[i // 2][...] = p.astype(BF)
            else:
                mine[i // 2][...] = p


def attend_back(order, pairs, qkv, seg_row, table, lse, weight):
    size = 2 * len(pairs)
    length, heads = qkv.shape[0], table.shape[0]
    share, d = heads * HEAD_DIM, weight.shape[0]
    n = length // size
    shape = jax.ShapeDtypeStruct
    out = pl.pallas_call(
        functools.partial(attend_back_kernel, size=size),
        grid=(heads,),
        in_specs=[
            pl.BlockSpec(memory_space=pltpu.SMEM),
            pl.BlockSpec(memory_space=pltpu.SMEM),
            whole((1, length)),
            whole((length, 1)),
            weight.all(),
            whole((length, 3 * share)),
            pl.BlockSpec((1, length, 1), lambda h: (h, 0, 0)),
        ]
        + [whole((2 * n, share))] * len(pairs),
        out_specs=[
            whole((length, 3 * share)),
            pl.BlockSpec((1, LANES, 5 * LANES), lambda h: (h, 0, 0)),
        ]
        + [whole((n, d))] * size,
        out_shape=[
            shape((length, 3 * share), BF),
            shape((heads, LANES, 5 * LANES), F32),
        ]
        + [shape((n, d), F32)] * len(pairs)
        + [shape((n, d), BF)] * len(pairs),
        scratch_shapes=[
            pltpu.VMEM((LANES, 2 * length), F32),
            pltpu.VMEM((length, HEAD_DIM), F32),
            pltpu.VMEM((length, HEAD_DIM), F32),
            pltpu.VMEM((length, share), BF),
        ],
        compiler_params=params(36),
        cost_estimate=cost(12 * length * length * share, *pairs),
    )(
        order,
        table,
        seg_row.reshape(1, length),
        seg_row.reshape(length, 1),
        weight.array,
        qkv,
        lse,
        *pairs,
    )
    chips = len(pairs)
    return out[0], out[1], out[2 : 2 + chips], out[2 + chips :]


def table_grad(band):
    offset = (
        lax.broadcasted_iota(jnp.int32, (LANES, 3 * LANES), 1)
        - LANES
        - lax.broadcasted_iota(jnp.int32, (LANES, 3 * LANES), 0)
    )
    middle = band[:, :, LANES : 4 * LANES]
    inner = [
        jnp.sum(jnp.where(offset == b, middle, 0.0), axis=(1, 2)) for b in range(1 - RELMAX, RELMAX)
    ]
    lower = jnp.sum(jnp.where(offset <= -RELMAX, middle, 0.0), axis=(1, 2))
    upper = jnp.sum(jnp.where(offset >= RELMAX, middle, 0.0), axis=(1, 2))
    lower = lower + jnp.sum(band[:, :, :LANES], axis=(1, 2))
    upper = upper + jnp.sum(band[:, :, 4 * LANES :], axis=(1, 2))
    return jnp.stack([lower] + inner + [upper], axis=1)


def attend_grads_kernel(order, dqkv, att, *refs):
    out, h_all, g_all = refs[-3:]
    size = (len(refs) - 3) // 2
    h, g = refs[:size], refs[size : 2 * size]
    n = h[0].shape[0]
    wide = dqkv.shape[1]
    for i in range(size):
        at = pl.ds(pl.multiple_of(order[i] * n, n), n)
        h_all[at, :] = h[i][...]
        g_all[at, :] = g[i][...]
    first = mm_tn(h_all[...], dqkv[...]).astype(BF)
    out[:, :, :wide] = first.reshape(out.shape[0], out.shape[1], wide)
    second = mm_tn(att[...], g_all[...]).astype(BF)
    depth, share = out.shape[1], out.shape[2] - wide
    per = second.shape[1] // share
    for i in range(out.shape[0]):
        k, u = divmod(i, per)
        out[i, :, wide:] = second[k * depth : (k + 1) * depth, u * share : (u + 1) * share]


def attend_grads(order, h, g, dqkv, att):
    rows, size = lax.axis_size("rows"), lax.axis_size("tm")
    n, d = h[0].shape
    length, share = att.shape
    m = d // rows
    if share != 2 * m:
        def place(chunks):
            out = jnp.zeros((size, n, d), BF)
            for i, v in enumerate(chunks):
                out = lax.dynamic_update_index_in_dim(out, v, order[i], 0)
            return out.reshape(length, d)

        first = mm_tn(place(h), dqkv).astype(BF)
        second = mm_tn(att, place(g)).astype(BF)
        second = (
            second.reshape(rows // size, m, size, share).transpose(0, 2, 1, 3).reshape(d, share)
        )
        return jnp.concatenate([first, second], axis=1).reshape(rows, m, -1)
    return pl.pallas_call(
        attend_grads_kernel,
        grid=(1,),
        in_specs=[
            pl.BlockSpec(memory_space=pltpu.SMEM),
            whole(dqkv.shape),
            whole(att.shape),
        ]
        + [whole((n, d))] * (2 * size),
        out_specs=whole((rows, m, 4 * share)),
        out_shape=jax.ShapeDtypeStruct((rows, m, 4 * share), BF),
        scratch_shapes=[pltpu.VMEM((length, d), BF)] * 2,
        compiler_params=params(28),
        cost_estimate=cost(8 * length * d * share, *h),
    )(order, dqkv, att, *h, *g)


def shards(
    frames,
    segments,
    ffn1_in,
    ffn1_out,
    query_w,
    key_w,
    value_w,
    attn_out,
    conv_in,
    conv_out,
    ffn2_in,
    ffn2_out,
    norm_gains,
    conv_kernel,
    bn_gain,
    bn_bias,
    rel_table,
    cotangent,
):
    rows, size = lax.axis_size("rows"), lax.axis_size("tm")
    t = lax.axis_index("tm")
    own, width = frames.shape[1], frames.shape[2]
    length = own * size
    share = width // size
    heads = rel_table.shape[0] // size
    taps = conv_kernel.shape[0]
    reach = taps // 2
    frame_total = float(length * rows)
    seg = segments[0]
    table = lax.dynamic_slice_in_dim(rel_table, t * heads, heads, 0)
    depth = width // rows
    unit = depth // size

    def mine(v):
        v = v.reshape(-1, rows, size, unit)
        return lax.dynamic_index_in_dim(v, t, 2, keepdims=False).reshape(-1, share)

    def placed(v):
        n = v.shape[0]
        out = jnp.zeros((n, rows, size, unit), F32)
        return lax.dynamic_update_index_in_dim(
            out, v.reshape(n, rows, unit), t, 2
        ).reshape(n, width)

    kernel_own = mine(conv_kernel)
    bn_gain_own, bn_bias_own = mine(bn_gain[None]), mine(bn_bias[None])

    perm = head_rows_perm()
    out_block = lax.ppermute(attn_out, ("rows", "tm"), perm)
    order = jnp.stack(
        [peer_index(dx, dc) for dx in range(size // 2) for dc in range(2)]
    ).astype(jnp.int32)
    f1, attn_w = gather_weights(
        [side_by_side(p) for p in exchange_all(ffn_pieces(ffn1_in, ffn1_out))],
        jnp.concatenate([query_w, key_w, value_w, out_block], axis=1),
    )
    wide = conv_in.shape[1]
    later = exchange_all(
        ffn_pieces(ffn2_in, ffn2_out)
        + [
            conv_in.reshape(depth, wide // depth, size, unit)
            .transpose(2, 0, 1, 3)
            .reshape(size, depth, wide // size),
            conv_out.reshape(size, unit, share),
        ]
    )
    later = [side_by_side(p) for p in later]
    f2_in, f2_out, conv_in_w, conv_out_w = gather_rows(later)
    f2 = (Weight(f2_in), Weight(f2_out))

    inputs = frames[0].astype(F32)
    n1 = norm_rows(inputs, norm_gains[0])[0]
    h1, _ = spread(n1.astype(BF), lambda near: ())
    h1[0] = (after(h1[0][0], *later), h1[0][1])
    one = [ffn(pair, *f1) for pair in reversed(h1)][::-1]
    parts = collect([v[2] for v in one], [v[3] for v in one])
    x1, n2 = add_norm(parts, inputs, norm_gains[1], 0.5)

    h2, local = spread(n2, lambda near: project(near, attn_w, 3 * share))
    pairs = [local] + [project(pair, attn_w, 3 * share) for pair in h2[1:]]
    qkv, att, lse, mine, theirs = attend(order, pairs, seg, table, attn_w)
    x2, n3 = add_norm(collect(mine, theirs), x1, norm_gains[2], 1.0)

    h3 = gather_tm(n3)
    u = mm(h3, conv_in_w)
    u_lin, u_sig = u[:, :share], jax.nn.sigmoid(u[:, share:])
    z = (u_lin * u_sig).astype(BF)
    seg_pad = jnp.pad(seg, (reach, reach), constant_values=-1)
    same = [(seg_pad[k : k + length] == seg)[:, None] for k in range(taps)]

    def shifted_rows(v):
        v = jnp.pad(v, ((reach, reach), (0, 0)))
        return [v[k : k + length] for k in range(taps)]

    z_near = shifted_rows(z)
    conv = jnp.zeros((length, share), F32)
    for k in range(taps):
        conv = conv + jnp.where(same[k], z_near[k].astype(F32) * kernel_own[k], 0.0)
    moments = sum_axis(
        jnp.stack([jnp.sum(conv, axis=0), jnp.sum(conv * conv, axis=0)]), "rows"
    )
    centre = moments[0] / frame_total
    inverse_bn = lax.rsqrt(moments[1] / frame_total - centre * centre + EPS)
    normed_bn = (conv - centre) * inverse_bn
    shifted = normed_bn * bn_gain_own + bn_bias_own
    e = (shifted * jax.nn.sigmoid(shifted)).astype(BF)
    x3, n4 = add_norm([scatter_tm(mm(e, conv_out_w).astype(BF))], x2, norm_gains[3], 1.0)

    h4, local = spread(n4, lambda near: ffn(near, *f2))
    four = [local] + [ffn(pair, *f2) for pair in h4[1:]]
    parts = collect([v[2] for v in four], [v[3] for v in four])
    output, d4, g, gain_five = turn(parts, x3, norm_gains[4], cotangent[0])

    def ffn_backward(g, h, kept, w, x, gain, prev, scale):
        g, local = spread(g, lambda near: ffn_back(near, kept[0][1], *w))
        back = [local] + [ffn_back(p, kept[i][1], *w) for i, p in enumerate(g[1:], 1)]
        packed = ffn_grads(
            sum(h, ()), sum(g, ()), [v[0] for v in back], [v[0] for v in kept]
        )
        parts = collect([v[1] for v in back], [v[2] for v in back], (packed,))
        return back_norm(parts, x, gain, prev, scale), packed

    (d3, g, gain_four), packed_four = ffn_backward(
        g, h4, four, f2, x3, norm_gains[3], d4, 1.0
    )
    sum_four = scatter_rows(packed_four)

    g3 = gather_tm(g)
    d_conv_out = mm_tn(e, g3).astype(BF)
    dn = mm_nt(g3, conv_out_w) * silu_slope(shifted)
    bn_part = jnp.stack([jnp.sum(dn, axis=0), jnp.sum(dn * normed_bn, axis=0)])
    bn_sums = sum_axis(bn_part, "rows")
    dc = (
        bn_gain_own
        * inverse_bn
        * (dn - bn_sums[0] / frame_total - normed_bn * (bn_sums[1] / frame_total))
    ).astype(BF)
    dc_near = shifted_rows(dc)
    dc_wide = dc.astype(F32)
    dz = jnp.zeros((length, share), F32)
    d_kernel = []
    for k in range(taps):
        mirror = taps - 1 - k
        dz = dz + jnp.where(same[mirror], dc_near[mirror].astype(F32) * kernel_own[k], 0.0)
        d_kernel.append(
            jnp.sum(jnp.where(same[k], z_near[k].astype(F32) * dc_wide, 0.0), axis=0)
        )
    du = jnp.concatenate([dz * u_sig, dz * u_lin * u_sig * (1.0 - u_sig)], axis=1).astype(BF)
    d_conv_in = mm_tn(h3, du).astype(BF)
    parts_three = [d_conv_in, d_conv_out]
    packed_three = pack_grads(parts_three)
    parts_three = [d_conv_in, d_conv_out]
    packed_three = pack_grads(parts_three)
    d2, g, gain_three = back_norm(
        [scatter_tm(mm_nt(du, conv_in_w).astype(BF), (packed_three,))],
        x2,
        norm_gains[2],
        d3,
        1.0,
    )

    g2, local = spread(g, lambda near: att_grad(near, attn_w, share))
    pairs = [local] + [att_grad(pair, attn_w, share) for pair in g2[1:]]
    dqkv, band, mine, theirs = attend_back(order, pairs, qkv, seg, table, lse, attn_w)
    packed_two = attend_grads(order, sum(h2, ()), sum(g2, ()), dqkv, att)
    packed_mid = jnp.concatenate([pack_grads([packed_two.reshape(width, -1)]), packed_three], axis=1) if packed_two.shape[2] == packed_three.shape[2] else None
    parts = collect(mine, theirs, (packed_two,) if packed_mid is None else (packed_mid,))
    d1, g, gain_two = back_norm(parts, x1, norm_gains[1], d2, 0.5)
    if packed_mid is None:
        sum_two, sum_three = scatter_rows(packed_two), scatter_rows(packed_three)
    else:
        sum_mid = scatter_rows(packed_mid)
        sum_two, sum_three = sum_mid[:depth], sum_mid[depth:]

    (grad, _, gain_one), packed_one = ffn_backward(
        g, h1, one, f1, inputs, norm_gains[0], d1, 1.0
    )
    grad_frames = grad.astype(BF)[None]
    sum_one = scatter_rows(packed_one)

    def ffn_parts(total):
        if total.shape == (2 * depth, width) and ffn1_in.shape[1] == width:
            return total[:depth], total[depth:]
        like = [
            jax.ShapeDtypeStruct((width, ffn1_in.shape[1]), BF),
            jax.ShapeDtypeStruct((ffn1_in.shape[1], width), BF),
        ]
        return unpack_grads(total, like)

    grad_ffn2_in, grad_ffn2_out = ffn_return(
        *ffn_parts(sum_four), ffn2_in.shape, ffn2_out.shape
    )
    grad_query, grad_key, grad_value, d_block = (
        sum_two[:, i * share : (i + 1) * share] for i in range(4)
    )
    grad_query, grad_key, grad_value = (v.astype(F32) for v in (grad_query, grad_key, grad_value))
    grad_attn_out = lax.ppermute(d_block, ("rows", "tm"), [(b, a) for a, b in perm]).astype(F32)
    d_in, d_out = unpack_grads(sum_three, parts_three)
    d_in, d_out = exchange_all(
        [
            d_in.reshape(depth, size, -1).transpose(1, 0, 2),
            d_out.reshape(unit, size, share).transpose(1, 0, 2),
        ]
    )
    grad_conv_in = (
        d_in.reshape(size, depth, wide // depth, unit)
        .transpose(1, 2, 0, 3)
        .reshape(depth, wide)
        .astype(F32)
    )
    grad_conv_out = d_out.reshape(depth, share).astype(F32)
    grad_ffn1_in, grad_ffn1_out = ffn_return(
        *ffn_parts(sum_one), ffn1_in.shape, ffn1_out.shape
    )

    table_row = lax.dynamic_update_slice_in_dim(
        jnp.zeros(rel_table.shape, F32), table_grad(band), t * heads, 0
    ).reshape(1, -1)
    table_row = jnp.pad(table_row, ((0, 0), (0, width - table_row.shape[1])))
    small = jnp.concatenate(
        [
            gain_one,
            gain_two,
            gain_three,
            gain_four,
            gain_five,
            placed(jnp.stack(d_kernel)),
            placed(bn_part),
            table_row,
        ],
        axis=0,
    )
    small = sum_axis(sum_axis(small, "tm"), "rows")
    table_size = rel_table.shape[0] * rel_table.shape[1]
    return (
        output[None],
        grad_frames,
        grad_ffn1_in,
        grad_ffn1_out,
        grad_query,
        grad_key,
        grad_value,
        grad_attn_out,
        grad_conv_in,
        grad_conv_out,
        grad_ffn2_in,
        grad_ffn2_out,
        small[:5],
        small[5 : 5 + taps],
        small[6 + taps],
        small[5 + taps],
        small[7 + taps, :table_size].reshape(rel_table.shape),
    )


def solution(mesh):
    split, copied = P("rows", "tm"), P()
    sequence = P("rows", "tm", None)
    return jax.shard_map(
        shards,
        mesh=mesh,
        in_specs=(sequence, P("rows", None)) + (split,) * 10 + (copied,) * 5 + (sequence,),
        out_specs=(sequence, sequence) + (split,) * 10 + (copied,) * 5,
        check_vma=False,
    )
```

time: 701 us -> 640 us (0.913)
  matrix products: 65 us -> 7.74 us
  Pallas kernels: 15.9 us -> 69.4 us
  local copies, waits for them, and re-layouts: 113 us -> 81.4 us
  other arithmetic: 53.9 us -> 30.2 us
    reduce_scatter x1 -> x3, waiting for transfers between devices: 0.01 us -> 59.7 us  [scatter_rows(): return lax.psum_scatter(packed, 'rows', scatter_dimension=0, tiled=False)]
    pallas_call x2 -> x25, Pallas kernels: 15.9 us -> 69.4 us  [the longest x1 11.5 us: attend_back(): pl.pallas_call(functools.partial(attend_back_kernel, size=size), grid=(he...]
    unnamed x9 -> x5, waiting for transfers between devices: 39.8 us -> 0.08 us
    dot_general x8 -> x2, matrix products: 22.6 us -> 2.32 us  [mm_nt(): lax.dot_general(a, b, (((1,), (1,)), ((), ())), preferred_element_type=F32)]
    dot_general x8 -> x2, matrix products: 20.7 us -> 2.11 us  [mm_tn(): lax.dot_general(a, b, (((0,), (0,)), ((), ())), preferred_element_type=F32)]
    dot_general x8 -> x2, matrix products: 21.7 us -> 3.3 us  [mm(): return jnp.dot(a, b, preferred_element_type=F32)]
    all_gather x4 -> x2, waiting for transfers between devices: 91.5 us -> 78.5 us  [the longest x1 67.6 us: gather_weights(): lax.all_gather(jnp.concatenate(parts, axis=0), 'rows', axis=0, tiled=False)]
    reshape x9 -> x10, local copies, waits for them, and re-layouts: 10.8 us -> 1.16 us  [the longest x3 0.38 us: ffn_return(): b = b.reshape(b.shape[0], size, -1).transpose(1, 0, 2)]
  transfers between devices with their start and end apart: 84 -> 79, of which waited for: 44 -> 54; matrix products, arithmetic and copies ran while one was open for 26% -> 10% of each run, Pallas kernels for 2% -> 9%
where the time goes in v2:
time: 640 us; the launch traced here: 634 us
  waiting for transfers between devices  375 us (59%)
  local copies, waits for them, and re-layouts  81.4 us (13%)
  Pallas kernels  69.4 us (11%)
  starting transfers between devices  54.2 us (8%)
  other arithmetic  30.2 us (5%)
  between operations  16.4 us (3%)
  matrix products  7.74 us (1%)
    ppermute x61, waiting for transfers between devices, from_peer(): return lax.ppermute(a, 'tm', tm_peer(dx, dc))  206 us
    all_gather x1, waiting for transfers between devices, gather_weights(): lax.all_gather(jnp.concatenate(parts, axis=0), 'rows', axis=0, tiled=False)  67.6 us
    reduce_scatter x3, waiting for transfers between devices, scatter_rows(): return lax.psum_scatter(packed, 'rows', scatter_dimension=0, tiled=False)  59.7 us
    unnamed x201, local copies, waits for them, and re-layouts  42.6 us
    ppermute x61, starting transfers between devices, from_peer(): return lax.ppermute(a, 'tm', tm_peer(dx, dc))  42.4 us
    ppermute x11, waiting for transfers between devices, sum_axis(): v = v + lax.ppermute(v, axis, [(i, i ^ bit) for i in range(size)])  30.6 us
  transfers between devices with their start and end apart: 79, of which 54 were waited for; matrix products, arithmetic and copies ran while one was open for 10% of the time, Pallas kernels for 9%

profile of v2, /device:TPU:0, one launch (start us, length us, event | category | flops | bytes accessed | tf_op | source)
XLA Modules:
  0.0 634.2 jit_solution(12133717504468506637)
XLA Ops:
  27.7 4.9 collective-permute-done.5
  41.5 12.8 %collective-permute-done.9.h0.refs_2_ = bf16[256,1024]{1,0:T(8,128)(2,1)S(1)} collective-permute-done((bf16[256,1024]{1,0:T(8,128)(2,1)S(1)}, bf16[256,1024]{1,0:T(8,128)(2,1)S(1)}, u32[]{:S(2)}, u32[]{:S(2)}) %collective-permute-start.9) | collective-permute-done | bytes 524320 | tf_op jit(solution)/shard_map/ppermute | solution.py:62
  56.2 67.6 %all-gather.5.cloned.1.call-done = bf16[3072,1024]{1,0:T(8,128)(2,1)} async-done(((bf16[384,1024]{1,0:T(8,128)(2,1)}), bf16[3072,1024]{1,0:T(8,128)(2,1)}) %all-gather.5.cloned.1.call-update) | async-done | bytes 6291472 | tf_op jit(solution)/shard_map/all_gather | solution.py:219
  134.0 12.4 %collective-permute-done.12.refs_2_ = bf16[256,1024]{1,0:T(8,128)(2,1)S(1)} collective-permute-done((bf16[256,1024]{1,0:T(8,128)(2,1)S(1)}, bf16[256,1024]{1,0:T(8,128)(2,1)S(1)}, u32[]{:S(2)}, u32[]{:S(2)}) %collective-permute-start.12) | collective-permute-done | bytes 524320 | tf_op jit(solution)/shard_map/ppermute | solution.py:62
  150.0 11.4 %collective-permute-done.14.h0.refs_2_ = bf16[256,1024]{1,0:T(8,128)(2,1)S(1)} collective-permute-done((bf16[256,1024]{1,0:T(8,128)(2,1)S(1)}, bf16[256,1024]{1,0:T(8,128)(2,1)S(1)}, u32[]{:S(2)}, u32[]{:S(2)}) %collective-permute-start.14) | collective-permute-done | bytes 524320 | tf_op jit(solution)/shard_map/ppermute | solution.py:62
  171.9 8.0 %shard_map.310 = (bf16[1024,768]{1,0:T(8,128)(2,1)S(1)}, bf16[1024,256]{1,0:T(8,128)(2,1)S(1)}, f32[2,1024,1]{2,1,0:T(8,128)S(1)}, f32[256,1024]{1,0:T(8,128)S(1...) custom-call(s32[4]{0:T(128)S(1)} %pad_add_fusion.order, ...), custom_call_target="tpu_custom_call" | custom-call | flops 1610612736 | bytes 1572864 | tf_op jit(solution)/shard_map/pallas_call | solution.py:599
  188.9 10.0 %collective-permute-done.18.refs_2_ = bf16[256,1024]{1,0:T(8,128)(2,1)S(1)} collective-permute-done((bf16[256,1024]{1,0:T(8,128)(2,1)}, bf16[256,1024]{1,0:T(8,128)(2,1)S(1)}, u32[]{:S(2)}, u32[]{:S(2)}) %collective-permute-start.18) | collective-permute-done | bytes 524320 | tf_op jit(solution)/shard_map/ppermute | solution.py:62
  205.9 10.9 %all-gather.7.cloned.1.call-done = bf16[2816,1024]{1,0:T(8,128)(2,1)} async-done(((bf16[352,1024]{1,0:T(8,128)(2,1)}), bf16[2816,1024]{1,0:T(8,128)(2,1)}) %all-gather.7.cloned.1.call-update) | async-done | bytes 5767184 | tf_op jit(solution)/shard_map/all_gather | solution.py:172
  251.4 12.8 %collective-permute-done.26 = bf16[256,1024]{1,0:T(8,128)(2,1)} collective-permute-done((bf16[256,1024]{1,0:T(8,128)(2,1)}, bf16[256,1024]{1,0:T(8,128)(2,1)}, u32[]{:S(2)}, u32[]{:S(2)}) %collective-permute-start.26) | collective-permute-done | bytes 524320 | tf_op jit(solution)/shard_map/ppermute | solution.py:62
  272.9 7.6 %collective-permute-done.29.h0.refs_2_ = bf16[256,1024]{1,0:T(8,128)(2,1)S(1)} collective-permute-done((bf16[256,1024]{1,0:T(8,128)(2,1)S(1)}, bf16[256,1024]{1,0:T(8,128)(2,1)S(1)}, u32[]{:S(2)}, u32[]{:S(2)}) %collective-permute-start.29) | collective-permute-done | bytes 524320 | tf_op jit(solution)/shard_map/ppermute | solution.py:62
  288.6 12.5 %collective-permute-done.32.refs_2_ = bf16[256,1024]{1,0:T(8,128)(2,1)S(1)} collective-permute-done((bf16[256,1024]{1,0:T(8,128)(2,1)S(1)}, bf16[256,1024]{1,0:T(8,128)(2,1)S(1)}, u32[]{:S(2)}, u32[]{:S(2)}) %collective-permute-start.32) | collective-permute-done | bytes 524320 | tf_op jit(solution)/shard_map/ppermute | solution.py:62
  309.8 8.3 %collective-permute-done.35.g0.refs_6_ = bf16[256,1024]{1,0:T(8,128)(2,1)S(1)} collective-permute-done((bf16[256,1024]{1,0:T(8,128)(2,1)S(1)}, bf16[256,1024]{1,0:T(8,128)(2,1)S(1)}, u32[]{:S(2)}, u32[]{:S(2)}) %collective-permute-start.35) | collective-permute-done | bytes 524320 | tf_op jit(solution)/shard_map/ppermute | solution.py:62
  327.2 5.1 shard_map.318
  334.3 5.7 collective-permute-done.38.refs_2_
  349.1 11.9 %collective-permute-done.40 = bf16[256,1024]{1,0:T(8,128)(2,1)} collective-permute-done((bf16[256,1024]{1,0:T(8,128)(2,1)}, bf16[256,1024]{1,0:T(8,128)(2,1)}, u32[]{:S(2)}, u32[]{:S(2)}) %collective-permute-start.40) | collective-permute-done | bytes 524320 | tf_op jit(solution)/shard_map/ppermute | solution.py:62
  388.8 12.5 %collective-permute-done.46 = bf16[256,1024]{1,0:T(8,128)(2,1)S(1)} collective-permute-done((bf16[256,1024]{1,0:T(8,128)(2,1)S(1)}, bf16[256,1024]{1,0:T(8,128)(2,1)S(1)}, u32[]{:S(2)}, u32[]{:S(2)}) %collective-permute-start.46) | collective-permute-done | bytes 524320 | tf_op jit(solution)/shard_map/ppermute | solution.py:62
  405.3 11.4 %collective-permute-done.48.g0.refs_6_ = bf16[256,1024]{1,0:T(8,128)(2,1)S(1)} collective-permute-done((bf16[256,1024]{1,0:T(8,128)(2,1)S(1)}, bf16[256,1024]{1,0:T(8,128)(2,1)S(1)}, u32[]{:S(2)}, u32[]{:S(2)}) %collective-permute-start.48) | collective-permute-done | bytes 524320 | tf_op jit(solution)/shard_map/ppermute | solution.py:62
  420.0 11.5 %shard_map.323 = (bf16[1024,768]{1,0:T(8,128)(2,1)S(1)}, f32[2,128,640]{2,1,0:T(8,128)S(1)}, f32[256,1024]{1,0:T(8,128)S(1)}, f32[256,1024]{1,0:T(8,128)S(1)}, b...) custom-call(s32[4]{0:T(128)S(1)} %pad_add_fusion.order, f32[2,17]{1,0:T(2,128)S(1)} %constant_dynamic-slice_fusion.8.tab_ref, ...), custom_call_target="tpu_custom_call" | custom-call | flops 3221225472 | bytes 524288 | tf_op jit(solution)/shard_map/pallas_call | solution.py:728
  442.1 12.7 %collective-permute-done.52.refs_2_ = bf16[256,1024]{1,0:T(8,128)(2,1)S(1)} collective-permute-done((bf16[256,1024]{1,0:T(8,128)(2,1)S(1)}, bf16[256,1024]{1,0:T(8,128)(2,1)S(1)}, u32[]{:S(2)}, u32[]{:S(2)}) %collective-permute-start.52) | collective-permute-done | bytes 524320 | tf_op jit(solution)/shard_map/ppermute | solution.py:62
  466.4 6.3 collective-permute-done.55.g0.refs_6_
  478.8 5.1 shard_map.328
  497.9 11.0 %collective-permute-done.58.refs_2_ = bf16[256,1024]{1,0:T(8,128)(2,1)} collective-permute-done((bf16[256,1024]{1,0:T(8,128)(2,1)}, bf16[256,1024]{1,0:T(8,128)(2,1)}, u32[]{:S(2)}, u32[]{:S(2)}) %collective-permute-start.58) | collective-permute-done | bytes 524320 | tf_op jit(solution)/shard_map/ppermute | solution.py:62
  538.2 4.4 collective-permute-done.67
  555.4 59.7 %reduce-scatter.4.cloned.1.call-done = bf16[1,256,1024]{2,1,0:T(8,128)(2,1)} async-done(((bf16[8,256,1024]{2,1,0:T(8,128)(2,1)}), bf16[1,256,1024]{2,1,0:T(8,128)(2,1)}) %reduce-scatter.4.cloned.1.call-update) | async-done | bytes 524304 | tf_op jit(solution)/shard_map/reduce_scatter | solution.py:207
  (593 shorter events, 281.3 us)
Async XLA Ops:
  7.2 116.5 %all-gather.5.cloned.1.call-start = ((), (), s32[]{:S(2)}) async-start(), calls=%async_computation.6 | async-start | bytes 7077888 | tf_op jit(solution)/shard_map/all_gather | solution.py:219
  21.2 195.6 %all-gather.7.cloned.1.call-start = ((), (), s32[]{:S(2)}) async-start(), calls=%async_computation.7 | async-start | bytes 6488064 | tf_op jit(solution)/shard_map/all_gather | solution.py:172
  38.5 495.7 %reduce-scatter.8.cloned.1.call-start = ((), (), s32[]{:S(2)}) async-start(), calls=%async_computation.5 | async-start | bytes 4718592 | tf_op jit(solution)/shard_map/reduce_scatter | solution.py:207
  39.8 14.4 %collective-permute-start.9 = (bf16[256,1024]{1,0:T(8,128)(2,1)S(1)}, bf16[256,1024]{1,0:T(8,128)(2,1)S(1)}, u32[]{:S(2)}, u32[]{:S(2)}) collective-permute-start(bf16[256,1024]{1,0:T(8,128)(2,1)S(1)} %multiply_convert_fusion.5.h0.refs_0_), channel_id=1, source_target_pairs={{2,0},{3,1},{0,2},{1,3},{6,4},{7,5},{4,6},{5,7},{10,8},{11,9},{8,1... | collective-permute-start | bytes 1572872 | tf_op jit(solution)/shard_map/ppermute | solution.py:62
  54.2 74.8 %collective-permute-start.7 = (bf16[256,1024]{1,0:T(8,128)(2,1)S(1)}, bf16[256,1024]{1,0:T(8,128)(2,1)S(1)}, u32[]{:S(2)}, u32[]{:S(2)}) collective-permute-start(bf16[256,1024]{1,0:T(8,128)(2,1)S(1)} %multiply_convert_fusion.5.h0.refs_0_), channel_id=1, source_target_pairs={{1,0},{0,1},{3,2},{2,3},{5,4},{4,5},{7,6},{6,7},{9,8},{8,9},{11,10... | collective-permute-start | bytes 1572872 | tf_op jit(solution)/shard_map/ppermute | solution.py:62
  132.3 14.1 %collective-permute-start.12 = (bf16[256,1024]{1,0:T(8,128)(2,1)S(1)}, bf16[256,1024]{1,0:T(8,128)(2,1)S(1)}, u32[]{:S(2)}, u32[]{:S(2)}) collective-permute-start(bf16[256,1024]{1,0:T(8,128)(2,1)S(1)} %add_convert_fusion.5), channel_id=1, source_target_pairs={{2,0},{3,1},{0,2},{1,3},{6,4},{7,5},{4,6},{5,7},{10,8},{11,9},{8,1... | collective-permute-start | bytes 1572872 | tf_op jit(solution)/shard_map/ppermute | solution.py:62
  147.1 14.3 %collective-permute-start.14 = (bf16[256,1024]{1,0:T(8,128)(2,1)S(1)}, bf16[256,1024]{1,0:T(8,128)(2,1)S(1)}, u32[]{:S(2)}, u32[]{:S(2)}) collective-permute-start(bf16[256,1024]{1,0:T(8,128)(2,1)S(1)} %get-tuple-element.97.h0.refs_0_), channel_id=1, source_target_pairs={{2,0},{3,1},{0,2},{1,3},{6,4},{7,5},{4,6},{5,7},{10,8},{11,9},{8,1... | collective-permute-start | bytes 1572872 | tf_op jit(solution)/shard_map/ppermute | solution.py:62
  184.8 14.2 %collective-permute-start.18 = (bf16[256,1024]{1,0:T(8,128)(2,1)}, bf16[256,1024]{1,0:T(8,128)(2,1)S(1)}, u32[]{:S(2)}, u32[]{:S(2)}) collective-permute-start(bf16[256,1024]{1,0:T(8,128)(2,1)} %add_convert_fusion.4), channel_id=1, source_target_pairs={{2,0},{3,1},{0,2},{1,3},{6,4},{7,5},{4,6},{5,7},{10,8},{11,9},{8,1... | collective-permute-start | bytes 1572872 | tf_op jit(solution)/shard_map/ppermute | solution.py:62
  204.3 14.0 %collective-permute-start.20 = (bf16[256,1024]{1,0:T(8,128)(2,1)}, bf16[256,1024]{1,0:T(8,128)(2,1)}, u32[]{:S(2)}, u32[]{:S(2)}) collective-permute-start(bf16[256,1024]{1,0:T(8,128)(2,1)} %get-tuple-element.105), channel_id=1, source_target_pairs={{2,0},{3,1},{0,2},{1,3},{6,4},{7,5},{4,6},{5,7},{10,8},{11,9},{8,1... | collective-permute-start | bytes 1572872 | tf_op jit(solution)/shard_map/ppermute | solution.py:62
  205.9 13.8 %collective-permute-start.19 = (bf16[256,1024]{1,0:T(8,128)(2,1)}, bf16[256,1024]{1,0:T(8,128)(2,1)}, u32[]{:S(2)}, u32[]{:S(2)}) collective-permute-start(bf16[256,1024]{1,0:T(8,128)(2,1)} %get-tuple-element.105), channel_id=1, source_target_pairs={{1,0},{0,1},{3,2},{2,3},{5,4},{4,5},{7,6},{6,7},{9,8},{8,9},{11,10... | collective-permute-start | bytes 1572872 | tf_op jit(solution)/shard_map/ppermute | solution.py:62
  250.0 14.3 %collective-permute-start.26 = (bf16[256,1024]{1,0:T(8,128)(2,1)}, bf16[256,1024]{1,0:T(8,128)(2,1)}, u32[]{:S(2)}, u32[]{:S(2)}) collective-permute-start(bf16[256,1024]{1,0:T(8,128)(2,1)} %fusion.23), channel_id=1, source_target_pairs={{2,0},{3,1},{0,2},{1,3},{6,4},{7,5},{4,6},{5,7},{10,8},{11,9},{8,1... | collective-permute-start | bytes 1572872 | tf_op jit(solution)/shard_map/ppermute | solution.py:62
  266.2 14.3 %collective-permute-start.29 = (bf16[256,1024]{1,0:T(8,128)(2,1)S(1)}, bf16[256,1024]{1,0:T(8,128)(2,1)S(1)}, u32[]{:S(2)}, u32[]{:S(2)}) collective-permute-start(bf16[256,1024]{1,0:T(8,128)(2,1)S(1)} %get-tuple-element.107.h0.refs_0_), channel_id=1, source_target_pairs={{2,0},{3,1},{0,2},{1,3},{6,4},{7,5},{4,6},{5,7},{10,8},{11,9},{8,1... | collective-permute-start | bytes 1572872 | tf_op jit(solution)/shard_map/ppermute | solution.py:62
  287.1 14.0 %collective-permute-start.32 = (bf16[256,1024]{1,0:T(8,128)(2,1)S(1)}, bf16[256,1024]{1,0:T(8,128)(2,1)S(1)}, u32[]{:S(2)}, u32[]{:S(2)}) collective-permute-start(bf16[256,1024]{1,0:T(8,128)(2,1)S(1)} %add_convert_fusion.3), channel_id=1, source_target_pairs={{2,0},{3,1},{0,2},{1,3},{6,4},{7,5},{4,6},{5,7},{10,8},{11,9},{8,1... | collective-permute-start | bytes 1572872 | tf_op jit(solution)/shard_map/ppermute | solution.py:62
  303.7 14.3 %collective-permute-start.35 = (bf16[256,1024]{1,0:T(8,128)(2,1)S(1)}, bf16[256,1024]{1,0:T(8,128)(2,1)S(1)}, u32[]{:S(2)}, u32[]{:S(2)}) collective-permute-start(bf16[256,1024]{1,0:T(8,128)(2,1)S(1)} %get-tuple-element.120.g0.refs_4_), channel_id=1, source_target_pairs={{2,0},{3,1},{0,2},{1,3},{6,4},{7,5},{4,6},{5,7},{10,8},{11,9},{8,1... | collective-permute-start | bytes 1572872 | tf_op jit(solution)/shard_map/ppermute | solution.py:62
  325.7 14.3 %collective-permute-start.38 = (bf16[256,1024]{1,0:T(8,128)(2,1)}, bf16[256,1024]{1,0:T(8,128)(2,1)}, u32[]{:S(2)}, u32[]{:S(2)}) collective-permute-start(bf16[256,1024]{1,0:T(8,128)(2,1)} %add_convert_fusion.2), channel_id=1, source_target_pairs={{2,0},{3,1},{0,2},{1,3},{6,4},{7,5},{4,6},{5,7},{10,8},{11,9},{8,1... | collective-permute-start | bytes 1572872 | tf_op jit(solution)/shard_map/ppermute | solution.py:62
  349.1 13.5 %collective-permute-start.39 = (bf16[256,1024]{1,0:T(8,128)(2,1)}, bf16[256,1024]{1,0:T(8,128)(2,1)}, u32[]{:S(2)}, u32[]{:S(2)}) collective-permute-start(bf16[256,1024]{1,0:T(8,128)(2,1)} %get-tuple-element.132), channel_id=1, source_target_pairs={{1,0},{0,1},{3,2},{2,3},{5,4},{4,5},{7,6},{6,7},{9,8},{8,9},{11,10... | collective-permute-start | bytes 1572872 | tf_op jit(solution)/shard_map/ppermute | solution.py:62
  349.1 198.0 %reduce-scatter.6.cloned.1.call-start = ((), (), s32[]{:S(2)}) async-start(), calls=%async_computation.4 | async-start | bytes 4128768 | tf_op jit(solution)/shard_map/reduce_scatter | solution.py:207
  387.3 14.0 %collective-permute-start.46 = (bf16[256,1024]{1,0:T(8,128)(2,1)S(1)}, bf16[256,1024]{1,0:T(8,128)(2,1)S(1)}, u32[]{:S(2)}, u32[]{:S(2)}) collective-permute-start(bf16[256,1024]{1,0:T(8,128)(2,1)S(1)} %fusion.24), channel_id=1, source_target_pairs={{2,0},{3,1},{0,2},{1,3},{6,4},{7,5},{4,6},{5,7},{10,8},{11,9},{8,1... | collective-permute-start | bytes 1572872 | tf_op jit(solution)/shard_map/ppermute | solution.py:62
  402.4 14.3 %collective-permute-start.48 = (bf16[256,1024]{1,0:T(8,128)(2,1)S(1)}, bf16[256,1024]{1,0:T(8,128)(2,1)S(1)}, u32[]{:S(2)}, u32[]{:S(2)}) collective-permute-start(bf16[256,1024]{1,0:T(8,128)(2,1)S(1)} %get-tuple-element.134.g0.refs_4_), channel_id=1, source_target_pairs={{2,0},{3,1},{0,2},{1,3},{6,4},{7,5},{4,6},{5,7},{10,8},{11,9},{8,1... | collective-permute-start | bytes 1572872 | tf_op jit(solution)/shard_map/ppermute | solution.py:62
  437.8 177.3 %reduce-scatter.4.cloned.1.call-start = ((), (), s32[]{:S(2)}) async-start(), calls=%async_computation.3 | async-start | bytes 4718592 | tf_op jit(solution)/shard_map/reduce_scatter | solution.py:207
  440.6 14.3 %collective-permute-start.52 = (bf16[256,1024]{1,0:T(8,128)(2,1)S(1)}, bf16[256,1024]{1,0:T(8,128)(2,1)S(1)}, u32[]{:S(2)}, u32[]{:S(2)}) collective-permute-start(bf16[256,1024]{1,0:T(8,128)(2,1)S(1)} %add_convert_fusion.1), channel_id=1, source_target_pairs={{2,0},{3,1},{0,2},{1,3},{6,4},{7,5},{4,6},{5,7},{10,8},{11,9},{8,1... | collective-permute-start | bytes 1572872 | tf_op jit(solution)/shard_map/ppermute | solution.py:62
  458.3 14.3 %collective-permute-start.55 = (bf16[256,1024]{1,0:T(8,128)(2,1)S(1)}, bf16[256,1024]{1,0:T(8,128)(2,1)S(1)}, u32[]{:S(2)}, u32[]{:S(2)}) collective-permute-start(bf16[256,1024]{1,0:T(8,128)(2,1)S(1)} %get-tuple-element.144.g0.refs_4_), channel_id=1, source_target_pairs={{2,0},{3,1},{0,2},{1,3},{6,4},{7,5},{4,6},{5,7},{10,8},{11,9},{8,1... | collective-permute-start | bytes 1572872 | tf_op jit(solution)/shard_map/ppermute | solution.py:62
  494.6 14.3 %collective-permute-start.58 = (bf16[256,1024]{1,0:T(8,128)(2,1)}, bf16[256,1024]{1,0:T(8,128)(2,1)}, u32[]{:S(2)}, u32[]{:S(2)}) collective-permute-start(bf16[256,1024]{1,0:T(8,128)(2,1)} %add_convert_fusion), channel_id=1, source_target_pairs={{2,0},{3,1},{0,2},{1,3},{6,4},{7,5},{4,6},{5,7},{10,8},{11,9},{8,1... | collective-permute-start | bytes 1572872 | tf_op jit(solution)/shard_map/ppermute | solution.py:62
  552.1 68.8 %collective-permute-start.62 = (bf16[128,256]{1,0:T(8,128)(2,1)S(1)}, bf16[128,256]{1,0:T(8,128)(2,1)S(1)}, u32[]{:S(2)}, u32[]{:S(2)}) collective-permute-start(bf16[128,256]{1,0:T(8,128)(2,1)S(1)} %get-tuple-element.335), channel_id=1, source_target_pairs={{0,0},{1,8},{2,16},{3,24},{4,1},{5,9},{6,17},{7,25},{8,2},{9,10},{... | collective-permute-start | bytes 196616 | tf_op jit(solution)/shard_map/ppermute | solution.py:1043
  (152 other events, 1069.2 us)
Sparse Core Ops, SparseCore 0:
  21.3 102.3 all-gather.4
  125.9 90.8 all-gather.6
  349.2 85.4 reduce-scatter.7
  438.6 80.5 reduce-scatter.5
  523.1 91.9 reduce-scatter.3

commit v3 on v2

--- a/solution.py
+++ b/solution.py
@@ -13,6 +13,21 @@
 EPS = 1e-05
 BF = jnp.bfloat16
 F32 = jnp.float32
+SMEM = pl.BlockSpec(memory_space=pltpu.SMEM)
+
+
+def vmem(count):
+    return [pl.BlockSpec(memory_space=pltpu.VMEM)] * count
+
+
+def params(limit):
+    return pltpu.CompilerParams(vmem_limit_bytes=limit * 1024 * 1024)
+
+
+def cost(flops, *arrays):
+    return pl.CostEstimate(
+        flops=flops, bytes_accessed=sum(a.size * a.dtype.itemsize for a in arrays), transcendentals=0
+    )
 
 
 def mm(a, b):
@@ -25,11 +40,6 @@
 
 def mm_nt(a, b):
     return lax.dot_general(a, b, (((1,), (1,)), ((), ())), preferred_element_type=F32)
-
-
-def silu_slope(a):
-    s = jax.nn.sigmoid(a)
-    return s * (1.0 + a * (1.0 - s))
 
 
 def norm_rows(v, g):
@@ -66,37 +76,6 @@
     chips = lax.axis_size("tm") // 2
     t = lax.axis_index("tm")
     return lax.rem(t // 2 + dx, chips) * 2 + jnp.bitwise_xor(t % 2, dc)
-
-
-def gather_tm(a):
-    size = lax.axis_size("tm")
-    n, w = a.shape
-    far = [from_peer(a, dx, 0) for dx in range(1, size // 2)]
-    held = {(0, 0): a, (0, 1): from_peer(a, 0, 1)}
-    for dx, b in enumerate(far, 1):
-        held[dx, 0] = b
-        held[dx, 1] = from_peer(b, 0, 1)
-    out = jnp.zeros((size, n, w), a.dtype)
-    for (dx, dc), b in held.items():
-        out = lax.dynamic_update_index_in_dim(out, b, peer_index(dx, dc), 0)
-    return out.reshape(size * n, w)
-
-
-def scatter_tm(p, beside=()):
-    size = lax.axis_size("tm")
-    chips = size // 2
-    t = lax.axis_index("tm")
-    x, c = t // 2, t % 2
-    w = p.shape[1]
-    p = p.reshape(chips, 2, p.shape[0] // size, w)
-    mine = lax.dynamic_index_in_dim(p, c, 1, keepdims=False)
-    theirs = lax.dynamic_index_in_dim(p, 1 - c, 1, keepdims=False).astype(BF)
-    q = mine.astype(F32) + from_peer(theirs, 0, 1).astype(F32)
-    total = lax.dynamic_index_in_dim(q, x, 0, keepdims=False)
-    for dx in range(1, chips):
-        piece = lax.dynamic_index_in_dim(q, lax.rem(x + chips - dx, chips), 0, keepdims=False)
-        total = total + after(from_peer(piece.astype(BF), dx, 0), *beside).astype(F32)
-    return total
 
 
 def spread(a, local):
@@ -108,15 +87,16 @@
     return [near] + [(b, from_peer(b, 0, 1)) for b in far], done
 
 
-def collect(mine, theirs, beside=()):
+def collect(mine, theirs, beside=None):
     chips = lax.axis_size("tm") // 2
-    got = []
-    for dx in range(1, chips):
-        q = mine[dx] + from_peer(theirs[dx], 0, 1).astype(F32)
-        got.append(from_peer(q.astype(BF), chips - dx, 0))
+    sent = [
+        (mine[dx] + from_peer(theirs[dx], 0, 1).astype(F32)).astype(BF) for dx in range(1, chips)
+    ]
     near = from_peer(theirs[0], 0, 1)
-    got = [after(v, near, *beside) for v in got]
-    return [mine[0], near] + got
+    got = [from_peer(q, chips - dx, 0) for dx, q in enumerate(sent, 1)]
+    done = beside(lambda v: after(v, *sent)) if beside else None
+    got = [after(v, near, *jax.tree.leaves(done)) for v in got]
+    return [mine[0], near] + got, done
 
 
 def exchange_tm(pieces):
@@ -166,17 +146,6 @@
     return jnp.concatenate(parts, axis=1).reshape(-1, w)
 
 
-def gather_rows(parts):
-    width = max(p.shape[1] for p in parts)
-    packed = [pack(p, width) for p in parts]
-    full = lax.all_gather(jnp.concatenate(packed, axis=0), "rows", axis=0, tiled=False)
-    out, at = [], 0
-    for p, q in zip(parts, packed):
-        out.append(unpack(full[:, at : at + q.shape[0]], p.shape[1]))
-        at += q.shape[0]
-    return out
-
-
 def pack_rows(p, width):
     rows = lax.axis_size("rows")
     m, w = p.shape[0] // rows, p.shape[1]
@@ -203,24 +172,36 @@
     return out
 
 
+def scatter_parity(own, other):
+    rows = lax.axis_size("rows")
+    near = lax.ppermute(other, "rows", [(i, i ^ 1) for i in range(rows)])
+    packed = (own.astype(F32) + near.astype(F32)).astype(BF)
+    return lax.psum_scatter(
+        packed,
+        "rows",
+        scatter_dimension=0,
+        tiled=False,
+        axis_index_groups=[list(range(y, rows, 2)) for y in range(2)],
+    )
+
+
 def scatter_rows(packed):
     return lax.psum_scatter(packed, "rows", scatter_dimension=0, tiled=False)
 
 
-def scatter_rows_near(packed):
-    got = lax.all_to_all(packed, "rows", 0, 0, tiled=True)
-    return jnp.sum(got.astype(F32), axis=0).astype(BF)
-
-
-def gather_weights(pair, more=None):
-    parts = list(pair) + ([] if more is None else [more])
-    m, width = parts[0].shape
-    if all(p.shape == (m, width) for p in parts) and m % 16 == 0:
-        full = lax.all_gather(jnp.concatenate(parts, axis=0), "rows", axis=0, tiled=False)
-        out = [Weight(full, i * m, m) for i in range(len(parts))]
-    else:
-        out = [Weight(lax.all_gather(p, "rows", axis=0, tiled=True)) for p in parts]
-    return (out[:2], out[2]) if more is not None else out
+def gather_ffn(w_in, w_out, more=()):
+    m, width = w_in.shape[0], w_out.shape[1] * lax.axis_size("tm")
+    side = sum(v.shape[1] for v in more)
+    if whole_lanes(w_in.shape, w_out.shape) and (not more or side == width):
+        sent = exchanged_ffn(w_in, w_out, more)
+        full = lax.all_gather(sent, "rows", axis=0, tiled=False)
+        return (Weight(full, 0, m), Weight(full, m, m)), full[:, 2 * m :].reshape(-1, width), sent
+    sent = [side_by_side(p) for p in exchange_all(ffn_pieces(w_in, w_out))]
+    full = [
+        lax.all_gather(p, "rows", axis=0, tiled=True)
+        for p in sent + ([jnp.concatenate(more, axis=1)] if more else [])
+    ]
+    return (Weight(full[0]), Weight(full[1])), full[-1], sent[0]
 
 
 def exchange_all(pieces):
@@ -253,15 +234,117 @@
     return pieces.transpose(1, 0, 2).reshape(pieces.shape[1], -1)
 
 
-def ffn_return(a, b, like_in, like_out):
+def ffn_back_in(a, like_in, like_out):
     size = lax.axis_size("tm")
-    a = a.reshape(a.shape[0], size, -1).transpose(1, 0, 2)
-    b = b.reshape(b.shape[0], size, -1).transpose(1, 0, 2)
-    a, b = exchange_all([a, b])
+    m, w = like_in
     unit = like_out[0] // size
-    m, w = like_in
+    a = exchange_tm(a.reshape(m, size, -1).transpose(1, 0, 2))
     a = a.reshape(size, m, w // (size * unit), unit).transpose(1, 2, 0, 3).reshape(m, w)
-    return a.astype(F32), b.reshape(like_out).astype(F32)
+    return a.astype(F32)
+
+
+def ffn_back_out(b, like_out):
+    size = lax.axis_size("tm")
+    b = exchange_tm(b.reshape(b.shape[0], size, -1).transpose(1, 0, 2))
+    return b.reshape(like_out).astype(F32)
+
+
+def peers():
+    chips = lax.axis_size("tm") // 2
+    rel = [(dx, dc) for dx in range(chips) for dc in range(2)]
+    index = lambda v: jnp.stack(v).astype(jnp.int32)
+    return (
+        rel,
+        index([peer_index(dx, dc) for dx, dc in rel]),
+        index([peer_index(chips - dx if dx else 0, dc) for dx, dc in rel]),
+    )
+
+
+def whole_lanes(like_in, like_out):
+    unit = like_out[0] // lax.axis_size("tm")
+    return unit % LANES == 0 and unit == like_in[0] and like_in[1] == like_out[1] * lax.axis_size("tm")
+
+
+def cut_kernel(to, w_in, w_out, *outs, unit):
+    size, m = len(outs), w_in.shape[0]
+    for i, out in enumerate(outs):
+        for j in range(out.shape[1] // unit):
+            at = pl.multiple_of(j * size * unit + to[i] * unit, unit)
+            out[:m, j * unit : (j + 1) * unit] = w_in[:, pl.ds(at, unit)]
+        out[m:, :] = w_out[pl.ds(pl.multiple_of(to[i] * unit, unit), unit), :]
+
+
+def lay_kernel(order, *refs, size):
+    out = refs[-1]
+    n, w = refs[0].shape
+    for i in range(size):
+        out[:n, pl.ds(pl.multiple_of(order[i] * w, w), w)] = refs[i][...]
+    at = 0
+    for r in refs[size:-1]:
+        out[n:, at : at + r.shape[1]] = r[...]
+        at += r.shape[1]
+
+
+def exchanged_ffn(w_in, w_out, more=()):
+    size = lax.axis_size("tm")
+    rel, order, to = peers()
+    m, unit = w_in.shape[0], w_out.shape[0] // size
+    w = w_in.shape[1] // size
+    pieces = pl.pallas_call(
+        functools.partial(cut_kernel, unit=unit),
+        in_specs=[SMEM] + vmem(2),
+        out_shape=[jax.ShapeDtypeStruct((m + unit, w), BF)] * size,
+        compiler_params=params(8),
+        cost_estimate=cost(0, w_in, w_out),
+    )(to, w_in, w_out)
+    got = [pieces[0]] + [from_peer(p, *at) for p, at in zip(pieces[1:], rel[1:])]
+    n = m + unit + (more[0].shape[0] if more else 0)
+    return pl.pallas_call(
+        functools.partial(lay_kernel, size=size),
+        in_specs=[SMEM] + vmem(size + len(more)),
+        out_shape=jax.ShapeDtypeStruct((n, w * size), BF),
+        compiler_params=params(8),
+        cost_estimate=cost(0, w_in, w_out),
+    )(order, *got, *more)
+
+
+def split_kernel(to, total, *outs):
+    w = outs[0].shape[1]
+    for i, out in enumerate(outs):
+        out[...] = total[:, pl.ds(pl.multiple_of(to[i] * w, w), w)]
+
+
+def place_kernel(order, *refs, unit):
+    size = len(refs) - 2
+    g_in, g_out = refs[-2:]
+    m = g_in.shape[0]
+    for i in range(size):
+        for j in range(refs[i].shape[1] // unit):
+            at = pl.multiple_of(j * size * unit + order[i] * unit, unit)
+            g_in[:, pl.ds(at, unit)] = refs[i][:m, j * unit : (j + 1) * unit].astype(F32)
+        rows = pl.ds(pl.multiple_of(order[i] * unit, unit), unit)
+        g_out[rows, :] = refs[i][m:, :].astype(F32)
+
+
+def returned_ffn(total, like_in, like_out):
+    size = lax.axis_size("tm")
+    rel, order, to = peers()
+    n, w = total.shape[0], total.shape[1] // size
+    pieces = pl.pallas_call(
+        split_kernel,
+        in_specs=[SMEM] + vmem(1),
+        out_shape=[jax.ShapeDtypeStruct((n, w), BF)] * size,
+        compiler_params=params(8),
+        cost_estimate=cost(0, total, total),
+    )(to, total)
+    got = [pieces[0]] + [from_peer(p, *at) for p, at in zip(pieces[1:], rel[1:])]
+    return pl.pallas_call(
+        functools.partial(place_kernel, unit=like_out[0] // size),
+        in_specs=[SMEM] + vmem(size),
+        out_shape=[jax.ShapeDtypeStruct(like_in, F32), jax.ShapeDtypeStruct(like_out, F32)],
+        compiler_params=params(8),
+        cost_estimate=cost(0, total, total, total),
+    )(order, *got)
 
 
 def head_rows_perm():
@@ -274,22 +357,12 @@
     return perm
 
 
-def params(limit):
-    return pltpu.CompilerParams(vmem_limit_bytes=limit * 1024 * 1024)
-
-
 def whole(shape):
     return pl.BlockSpec(shape, lambda *_: (0,) * len(shape))
 
 
 def flat(v):
     return v.reshape(-1, v.shape[-1])
-
-
-def cost(flops, *arrays):
-    return pl.CostEstimate(
-        flops=flops, bytes_accessed=sum(a.size * a.dtype.itemsize for a in arrays), transcendentals=0
-    )
 
 
 class Weight:
@@ -307,11 +380,6 @@
         return pl.BlockSpec(
             (self.array.shape[0], self.m, self.shape[1]), lambda *_: (0, unit, 0)
         )
-
-    def value(self):
-        if self.m is None:
-            return self.array
-        return flat(self.array[:, self.first : self.first + self.m])
 
 
 def ffn_kernel(h0, h1, w_in, w_out, s_ref, slope_ref, mine, theirs):
@@ -417,6 +485,45 @@
     )(*h, *g, *da, *s)
 
 
+def half_grads_kernel(odd_ref, *refs, count):
+    own, other = refs[-2:]
+    refs = refs[:-2]
+    join = lambda v: jnp.concatenate([r[...] for r in v], axis=0)
+    v = mm_tn(join(refs[:count]), join(refs[count:])).astype(BF)
+    v = v.reshape(own.shape[0], 2, own.shape[1], own.shape[2])
+    even = odd_ref[0] == 0
+    own[...] = jnp.where(even, v[:, 0], v[:, 1])
+    other[...] = jnp.where(even, v[:, 1], v[:, 0])
+
+
+def half_grads(left, right):
+    rows = lax.axis_size("rows")
+    d, units = left[0].shape[1], right[0].shape[1]
+    m = d // rows
+    if m % 16:
+        v = mm_tn(jnp.concatenate(left, axis=0), jnp.concatenate(right, axis=0)).astype(BF)
+        return by_parity(v.reshape(rows, m, units))
+    odd = (lax.axis_index("rows") % 2).astype(jnp.int32).reshape(1)
+    return pl.pallas_call(
+        functools.partial(half_grads_kernel, count=len(left)),
+        in_specs=[pl.BlockSpec(memory_space=pltpu.SMEM)]
+        + [pl.BlockSpec(memory_space=pltpu.VMEM)] * (len(left) + len(right)),
+        out_shape=[jax.ShapeDtypeStruct((rows // 2, m, units), BF)] * 2,
+        compiler_params=params(28),
+        cost_estimate=cost(2 * len(left) * left[0].shape[0] * d * units, *left),
+    )(odd, *left, *right)
+
+
+def by_parity(packed):
+    rows = packed.shape[0]
+    odd = lax.axis_index("rows") % 2
+    v = packed.reshape(rows // 2, 2, *packed.shape[1:])
+    return [
+        lax.dynamic_index_in_dim(v, odd, 1, keepdims=False),
+        lax.dynamic_index_in_dim(v, 1 - odd, 1, keepdims=False),
+    ]
+
+
 def add_norm_kernel(*refs, scale):
     x_ref, gain, x_new, h_ref = refs[-4:]
     total = refs[0][...]
@@ -494,7 +601,7 @@
 
 def project_kernel(h0, h1, w, out):
     h = jnp.concatenate([h0[...], h1[...]], axis=0)
-    out[...] = mm(h, flat(w[...])[:, : out.shape[1]]).astype(BF)
+    out[...] = mm(h, w[...][:, : out.shape[1]]).astype(BF)
 
 
 def project(pair, w, width):
@@ -502,12 +609,12 @@
     return pl.pallas_call(
         project_kernel,
         grid=(1,),
-        in_specs=[whole((n, d)), whole((n, d)), w.all()],
+        in_specs=[whole((n, d)), whole((n, d)), whole(w.shape)],
         out_specs=whole((2 * n, width)),
         out_shape=jax.ShapeDtypeStruct((2 * n, width), BF),
         compiler_params=params(20),
-        cost_estimate=cost(4 * n * d * width, w.array),
-    )(*pair, w.array)
+        cost_estimate=cost(4 * n * d * width, w),
+    )(*pair, w)
 
 
 def joined(v, size, depth):
@@ -580,7 +687,7 @@
     @pl.when(head == heads - 1)
     def _():
         share = att.shape[1]
-        w = joined(flat(w_ref[...])[:, -share:], size, depth)
+        w = joined(w_ref[...][:, -share:], size, depth)
         for i in range(size):
             p = mm(att[at(i), :], w)
             if i % 2:
@@ -604,7 +711,7 @@
             pl.BlockSpec(memory_space=pltpu.SMEM),
             whole((1, length)),
             whole((length, 1)),
-            weight.all(),
+            whole(weight.shape),
         ]
         + [whole((2 * n, 3 * share))] * len(pairs),
         out_specs=[
@@ -623,14 +730,14 @@
         scratch_shapes=[pltpu.VMEM((LANES, 2 * length), F32)],
         compiler_params=params(32),
         cost_estimate=cost(6 * length * length * share, *pairs),
-    )(order, table, seg_row.reshape(1, length), seg_row.reshape(length, 1), weight.array, *pairs)
+    )(order, table, seg_row.reshape(1, length), seg_row.reshape(length, 1), weight, *pairs)
     chips = len(pairs)
     return out[0], out[1], out[2], out[3 : 3 + chips], out[3 + chips :]
 
 
 def att_grad_kernel(g0, g1, w_ref, out, *, size, depth):
     share = out.shape[1]
-    w = joined(flat(w_ref[...])[:, -share:], size, depth)
+    w = joined(w_ref[...][:, -share:], size, depth)
     g = jnp.concatenate([g0[...], g1[...]], axis=0)
     out[...] = mm_nt(g, w).astype(BF)
 
@@ -642,12 +749,12 @@
             att_grad_kernel, size=lax.axis_size("tm"), depth=d // lax.axis_size("rows")
         ),
         grid=(1,),
-        in_specs=[whole((n, d)), whole((n, d)), weight.all()],
+        in_specs=[whole((n, d)), whole((n, d)), whole(weight.shape)],
         out_specs=whole((2 * n, share)),
         out_shape=jax.ShapeDtypeStruct((2 * n, share), BF),
         compiler_params=params(16),
-        cost_estimate=cost(4 * n * d * share, weight.array),
-    )(*pair, weight.array)
+        cost_estimate=cost(4 * n * d * share, weight),
+    )(*pair, weight)
 
 
 def attend_back_kernel(
@@ -710,7 +817,7 @@
 
     @pl.when(head == heads - 1)
     def _():
-        w = flat(w_ref[...])[:, : dqkv_ref.shape[1]]
+        w = w_ref[...][:, : dqkv_ref.shape[1]]
         for i in range(size):
             p = mm_nt(dqkv_ref[rows_of(i), :], w)
             if i % 2:
@@ -733,7 +840,7 @@
             pl.BlockSpec(memory_space=pltpu.SMEM),
             whole((1, length)),
             whole((length, 1)),
-            weight.all(),
+            whole(weight.shape),
             whole((length, 3 * share)),
             pl.BlockSpec((1, length, 1), lambda h: (h, 0, 0)),
         ]
@@ -762,7 +869,7 @@
         table,
         seg_row.reshape(1, length),
         seg_row.reshape(length, 1),
-        weight.array,
+        weight,
         qkv,
         lse,
         *pairs,
@@ -841,6 +948,248 @@
         compiler_params=params(28),
         cost_estimate=cost(8 * length * d * share, *h),
     )(order, dqkv, att, *h, *g)
+
+
+EDGE = 16
+
+
+def glu_kernel(h0, h1, w, z, sig_ref, slope_ref):
+    h = jnp.concatenate([h0[...], h1[...]], axis=0)
+    u = mm(h, w[...])
+    share = z.shape[1]
+    lin, sig = u[:, :share], jax.nn.sigmoid(u[:, share:])
+    z[...] = (lin * sig).astype(BF)
+    sig_ref[...] = sig.astype(BF)
+    slope_ref[...] = (lin * sig * (1.0 - sig)).astype(BF)
+
+
+def glu(pair, w):
+    n, d = pair[0].shape
+    share = w.shape[1] // 2
+    return pl.pallas_call(
+        glu_kernel,
+        out_shape=[jax.ShapeDtypeStruct((2 * n, share), BF)] * 3,
+        compiler_params=params(16),
+        cost_estimate=cost(8 * n * d * share, w),
+    )(*pair, w)
+
+
+def lay_out(order, pairs, out):
+    n = pairs[0].shape[0] // 2
+    out[:EDGE, :] = jnp.zeros((EDGE, out.shape[1]), F32)
+    out[EDGE + 2 * len(pairs) * n :, :] = jnp.zeros((EDGE, out.shape[1]), F32)
+    for i in range(2 * len(pairs)):
+        rows = pl.ds(pl.multiple_of(EDGE + order[i] * n, EDGE), n)
+        out[rows, :] = pairs[i // 2][(i % 2) * n : (i % 2 + 1) * n, :].astype(F32)
+
+
+def pick(ref, order, size):
+    n = ref.shape[0] // size
+    return jnp.concatenate(
+        [ref[pl.ds(pl.multiple_of(order[i] * n, EDGE), n), :] for i in range(size)], axis=0
+    )
+
+
+def joined_rows(refs):
+    return jnp.concatenate([r[...] for r in refs], axis=0)
+
+
+def tap_masks(seg, taps, count):
+    own = seg[EDGE : EDGE + count, :]
+    first = EDGE - taps // 2
+    return [(seg[first + k : first + k + count, :] == own).astype(F32) for k in range(taps)]
+
+
+def convolve_kernel(order, seg, taps_ref, *refs, taps):
+    pairs, (conv_ref, sums_ref, wide) = refs[:-3], refs[-3:]
+    count = conv_ref.shape[0]
+    lay_out(order, pairs, wide)
+    first = EDGE - taps // 2
+    total = None
+    for k, mask in enumerate(tap_masks(seg, taps, count)):
+        term = (wide[first + k : first + k + count, :] * mask) * taps_ref[k : k + 1, :]
+        total = term if total is None else total + term
+    conv_ref[...] = total
+    sums_ref[0:1, :] = jnp.sum(total, axis=0, keepdims=True)
+    sums_ref[1:2, :] = jnp.sum(total * total, axis=0, keepdims=True)
+
+
+def convolve(order, seg, taps, pairs):
+    count, share = seg.shape[0] - 2 * EDGE, pairs[0].shape[1]
+    return pl.pallas_call(
+        functools.partial(convolve_kernel, taps=taps.shape[0]),
+        in_specs=[SMEM] + vmem(2 + len(pairs)),
+        out_shape=[
+            jax.ShapeDtypeStruct((count, share), F32),
+            jax.ShapeDtypeStruct((2, share), F32),
+        ],
+        scratch_shapes=[pltpu.VMEM((count + 2 * EDGE, share), F32)],
+        compiler_params=params(16),
+        cost_estimate=cost(0, *pairs, *pairs, *pairs),
+    )(order, seg, taps, *pairs)
+
+
+def bn_stats(moments, total):
+    centre = moments[0:1, :] / total
+    return centre, lax.rsqrt(moments[1:2, :] / total - centre * centre + EPS)
+
+
+def bn_kernel(order, conv, moments, gain, bias, w, e_ref, slope_ref, *refs, total):
+    size = len(refs)
+    n = conv.shape[0] // size
+    centre, inverse = bn_stats(moments[...], total)
+    shifted = (pick(conv, order, size) - centre) * inverse * gain[...] + bias[...]
+    sig = jax.nn.sigmoid(shifted)
+    e = (shifted * sig).astype(BF)
+    e_ref[...] = e
+    slope_ref[...] = (sig * (1.0 + shifted * (1.0 - sig))).astype(BF)
+    p = mm(e, w[...])
+    for i in range(size):
+        refs[i % 2 * (size // 2) + i // 2][...] = p[i * n : (i + 1) * n].astype(
+            BF if i % 2 else F32
+        )
+
+
+def chunk_shapes(n, d, size):
+    return [jax.ShapeDtypeStruct((n, d), F32)] * (size // 2) + [
+        jax.ShapeDtypeStruct((n, d), BF)
+    ] * (size // 2)
+
+
+def bn_forward(order, conv, moments, gain, bias, w, total):
+    count, share = conv.shape
+    d, size = w.shape[1], lax.axis_size("tm")
+    out = pl.pallas_call(
+        functools.partial(bn_kernel, total=total),
+        in_specs=[SMEM] + vmem(5),
+        out_shape=[jax.ShapeDtypeStruct((count, share), BF)] * 2
+        + chunk_shapes(count // size, d, size),
+        compiler_params=params(24),
+        cost_estimate=cost(2 * count * share * d, conv),
+    )(order, conv, moments, gain, bias, w)
+    return out[0], out[1], out[2 : 2 + size // 2], out[2 + size // 2 :]
+
+
+def conv_out_grad_kernel(g0, g1, w, out):
+    g = jnp.concatenate([g0[...], g1[...]], axis=0)
+    out[...] = mm_nt(g, w[...])
+
+
+def conv_out_grad(pair, w):
+    n, d = pair[0].shape
+    return pl.pallas_call(
+        conv_out_grad_kernel,
+        out_shape=jax.ShapeDtypeStruct((2 * n, w.shape[0]), F32),
+        compiler_params=params(12),
+        cost_estimate=cost(4 * n * d * w.shape[0], w),
+    )(*pair, w)
+
+
+def bn_sums_kernel(order, conv, slope, moments, *refs, total):
+    pairs, (dn_ref, sums_ref) = refs[:-2], refs[-2:]
+    dn = joined_rows(pairs) * slope[...].astype(F32)
+    dn_ref[...] = dn
+    centre, inverse = bn_stats(moments[...], total)
+    normed = (pick(conv, order, 2 * len(pairs)) - centre) * inverse
+    sums_ref[0:1, :] = jnp.sum(dn, axis=0, keepdims=True)
+    sums_ref[1:2, :] = jnp.sum(dn * normed, axis=0, keepdims=True)
+
+
+def bn_back(order, conv, slope, moments, pairs, total):
+    count, share = conv.shape
+    return pl.pallas_call(
+        functools.partial(bn_sums_kernel, total=total),
+        in_specs=[SMEM] + vmem(3 + len(pairs)),
+        out_shape=[
+            jax.ShapeDtypeStruct((count, share), F32),
+            jax.ShapeDtypeStruct((2, share), F32),
+        ],
+        compiler_params=params(16),
+        cost_estimate=cost(0, conv, conv, conv),
+    )(order, conv, slope, moments, *pairs)
+
+
+def conv_back_kernel(
+    order, seg, taps_ref, dn, conv, moments, sums, gain, w, *refs, taps, total, size
+):
+    chips = size // 2
+    z, sig, slope = refs[:chips], refs[chips : 2 * chips], refs[2 * chips : 3 * chips]
+    du_ref, dk_ref = refs[3 * chips : 3 * chips + 2]
+    out, (c_wide, z_wide, dz_ref, dc_ref) = refs[3 * chips + 2 : -4], refs[-4:]
+    count, share = dn.shape
+    n = count // size
+    centre, inverse = bn_stats(moments[...], total)
+    normed = (pick(conv, order, size) - centre) * inverse
+    dc = dn[...] - sums[0:1, :] / total - normed * (sums[1:2, :] / total)
+    dc_ref[...] = (gain[...] * inverse * dc).astype(BF)
+    lay_out(order, [dc_ref.at[2 * n * i : 2 * n * (i + 1)] for i in range(chips)], c_wide)
+    lay_out(order, z, z_wide)
+    first = EDGE - taps // 2
+    masks = tap_masks(seg, taps, count)
+    own = c_wide[EDGE : EDGE + count, :]
+    dz = None
+    for k in range(taps):
+        mirror = taps - 1 - k
+        near = c_wide[first + mirror : first + mirror + count, :] * masks[mirror]
+        term = near * taps_ref[k : k + 1, :]
+        dz = term if dz is None else dz + term
+        dk_ref[k : k + 1, :] = jnp.sum(
+            (z_wide[first + k : first + k + count, :] * masks[k]) * own, axis=0, keepdims=True
+        )
+    dz_ref[...] = dz
+    dz = pick(dz_ref, order, size)
+    du = jnp.concatenate(
+        [dz * joined_rows(sig).astype(F32), dz * joined_rows(slope).astype(F32)], axis=1
+    ).astype(BF)
+    du_ref[...] = du
+    p = mm_nt(du, w[...])
+    for i in range(size):
+        out[i % 2 * chips + i // 2][...] = p[i * n : (i + 1) * n].astype(BF if i % 2 else F32)
+
+
+def conv_back(order, seg, taps, dn, conv, moments, sums, gain, w, kept, total):
+    count, share = dn.shape
+    d, size = w.shape[0], lax.axis_size("tm")
+    wide = pltpu.VMEM((count + 2 * EDGE, share), F32)
+    z, sig, slope = zip(*kept)
+    out = pl.pallas_call(
+        functools.partial(conv_back_kernel, taps=taps.shape[0], total=total, size=size),
+        in_specs=[SMEM] + vmem(8 + 3 * len(kept)),
+        out_shape=[
+            jax.ShapeDtypeStruct((count, 2 * share), BF),
+            jax.ShapeDtypeStruct((taps.shape[0], share), F32),
+        ]
+        + chunk_shapes(count // size, d, size),
+        scratch_shapes=[
+            wide,
+            wide,
+            pltpu.VMEM((count, share), F32),
+            pltpu.VMEM((count, share), BF),
+        ],
+        compiler_params=params(30),
+        cost_estimate=cost(4 * count * share * d, dn, dn, dn),
+    )(order, seg, taps, dn, conv, moments, sums, gain, w, *z, *sig, *slope)
+    return out[0], out[1], out[2 : 2 + size // 2], out[2 + size // 2 :]
+
+
+def conv_grads_kernel(du, e, *refs):
+    size = (len(refs) - 2) // 2
+    in_ref, out_ref = refs[-2:]
+    in_ref[...] = mm_tn(joined_rows(refs[:size]), du[...]).astype(BF)
+    out_ref[...] = mm_tn(e[...], joined_rows(refs[size : 2 * size])).astype(BF)
+
+
+def conv_grads(h, g, du, e):
+    d, share = h[0].shape[1], e.shape[1]
+    return pl.pallas_call(
+        conv_grads_kernel,
+        out_shape=[
+            jax.ShapeDtypeStruct((d, 2 * share), BF),
+            jax.ShapeDtypeStruct((share, d), BF),
+        ],
+        compiler_params=params(24),
+        cost_estimate=cost(6 * e.shape[0] * share * d, du, e),
+    )(du, e, *h, *g)
 
 
 def shards(
@@ -870,7 +1219,6 @@
     share = width // size
     heads = rel_table.shape[0] // size
     taps = conv_kernel.shape[0]
-    reach = taps // 2
     frame_total = float(length * rows)
     seg = segments[0]
     table = lax.dynamic_slice_in_dim(rel_table, t * heads, heads, 0)
@@ -890,139 +1238,134 @@
 
     kernel_own = mine(conv_kernel)
     bn_gain_own, bn_bias_own = mine(bn_gain[None]), mine(bn_bias[None])
+    seg_near = jnp.pad(seg, (EDGE, EDGE), constant_values=-1).reshape(-1, 1)
 
     perm = head_rows_perm()
     out_block = lax.ppermute(attn_out, ("rows", "tm"), perm)
     order = jnp.stack(
         [peer_index(dx, dc) for dx in range(size // 2) for dc in range(2)]
     ).astype(jnp.int32)
-    f1, attn_w = gather_weights(
-        [side_by_side(p) for p in exchange_all(ffn_pieces(ffn1_in, ffn1_out))],
-        jnp.concatenate([query_w, key_w, value_w, out_block], axis=1),
-    )
+    f1, attn_part, sent = gather_ffn(ffn1_in, ffn1_out, (query_w, key_w, value_w, out_block))
     wide = conv_in.shape[1]
-    later = exchange_all(
-        ffn_pieces(ffn2_in, ffn2_out)
-        + [
-            conv_in.reshape(depth, wide // depth, size, unit)
+    pieces = exchange_all(
+        [
+            after(conv_in, sent)
+            .reshape(depth, wide // depth, size, unit)
             .transpose(2, 0, 1, 3)
             .reshape(size, depth, wide // size),
-            conv_out.reshape(size, unit, share),
+            after(conv_out, sent).reshape(size, unit, share),
         ]
     )
-    later = [side_by_side(p) for p in later]
-    f2_in, f2_out, conv_in_w, conv_out_w = gather_rows(later)
-    f2 = (Weight(f2_in), Weight(f2_out))
+    packed = [pack(side_by_side(p), width) for p in pieces]
+    sent = jnp.concatenate(packed, axis=0)
+    full = lax.all_gather(sent, "rows", axis=0, tiled=False)
+    at = packed[0].shape[0]
+    conv_in_w, conv_out_w = unpack(full[:, :at], wide), unpack(full[:, at:], width)
+    f2, _, sent = gather_ffn(after(ffn2_in, sent), ffn2_out)
 
     inputs = frames[0].astype(F32)
     n1 = norm_rows(inputs, norm_gains[0])[0]
     h1, _ = spread(n1.astype(BF), lambda near: ())
-    h1[0] = (after(h1[0][0], *later), h1[0][1])
+    h1[0] = (after(h1[0][0], sent), h1[0][1])
     one = [ffn(pair, *f1) for pair in reversed(h1)][::-1]
-    parts = collect([v[2] for v in one], [v[3] for v in one])
+    parts, attn_w = collect(
+        [v[2] for v in one], [v[3] for v in one], lambda ready: ready(attn_part)
+    )
     x1, n2 = add_norm(parts, inputs, norm_gains[1], 0.5)
 
     h2, local = spread(n2, lambda near: project(near, attn_w, 3 * share))
     pairs = [local] + [project(pair, attn_w, 3 * share) for pair in h2[1:]]
-    qkv, att, lse, mine, theirs = attend(order, pairs, seg, table, attn_w)
-    x2, n3 = add_norm(collect(mine, theirs), x1, norm_gains[2], 1.0)
-
-    h3 = gather_tm(n3)
-    u = mm(h3, conv_in_w)
-    u_lin, u_sig = u[:, :share], jax.nn.sigmoid(u[:, share:])
-    z = (u_lin * u_sig).astype(BF)
-    seg_pad = jnp.pad(seg, (reach, reach), constant_values=-1)
-    same = [(seg_pad[k : k + length] == seg)[:, None] for k in range(taps)]
-
-    def shifted_rows(v):
-        v = jnp.pad(v, ((reach, reach), (0, 0)))
-        return [v[k : k + length] for k in range(taps)]
-
-    z_near = shifted_rows(z)
-    conv = jnp.zeros((length, share), F32)
-    for k in range(taps):
-        conv = conv + jnp.where(same[k], z_near[k].astype(F32) * kernel_own[k], 0.0)
-    moments = sum_axis(
-        jnp.stack([jnp.sum(conv, axis=0), jnp.sum(conv * conv, axis=0)]), "rows"
-    )
-    centre = moments[0] / frame_total
-    inverse_bn = lax.rsqrt(moments[1] / frame_total - centre * centre + EPS)
-    normed_bn = (conv - centre) * inverse_bn
-    shifted = normed_bn * bn_gain_own + bn_bias_own
-    e = (shifted * jax.nn.sigmoid(shifted)).astype(BF)
-    x3, n4 = add_norm([scatter_tm(mm(e, conv_out_w).astype(BF))], x2, norm_gains[3], 1.0)
+    qkv, att, lse, mine_a, theirs_a = attend(order, pairs, seg, table, attn_w)
+    parts, _ = collect(mine_a, theirs_a)
+    x2, n3 = add_norm(parts, x1, norm_gains[2], 1.0)
+
+    h3, local = spread(n3, lambda near: glu(near, conv_in_w))
+    kept = [local] + [glu(pair, conv_in_w) for pair in h3[1:]]
+    conv, moments = convolve(order, seg_near, kernel_own, [v[0] for v in kept])
+    moments = sum_axis(moments, "rows")
+    e, e_slope, mine_c, theirs_c = bn_forward(
+        order, conv, moments, bn_gain_own, bn_bias_own, conv_out_w, frame_total
+    )
+    parts, _ = collect(mine_c, theirs_c)
+    x3, n4 = add_norm(parts, x2, norm_gains[3], 1.0)
 
     h4, local = spread(n4, lambda near: ffn(near, *f2))
     four = [local] + [ffn(pair, *f2) for pair in h4[1:]]
-    parts = collect([v[2] for v in four], [v[3] for v in four])
+    parts, _ = collect([v[2] for v in four], [v[3] for v in four])
     output, d4, g, gain_five = turn(parts, x3, norm_gains[4], cotangent[0])
 
-    def ffn_backward(g, h, kept, w, x, gain, prev, scale):
-        g, local = spread(g, lambda near: ffn_back(near, kept[0][1], *w))
-        back = [local] + [ffn_back(p, kept[i][1], *w) for i, p in enumerate(g[1:], 1)]
-        packed = ffn_grads(
-            sum(h, ()), sum(g, ()), [v[0] for v in back], [v[0] for v in kept]
+    g4, local = spread(g, lambda near: ffn_back(near, four[0][1], *f2))
+    back = [local] + [ffn_back(p, four[i][1], *f2) for i, p in enumerate(g4[1:], 1)]
+    parts, packed_four = collect(
+        [v[1] for v in back],
+        [v[2] for v in back],
+        lambda ready: ffn_grads(
+            [ready(v) for v in sum(h4, ())],
+            sum(g4, ()),
+            [v[0] for v in back],
+            [ready(v[0]) for v in four],
+        ),
+    )
+    d3, g, gain_four = back_norm(parts, x3, norm_gains[3], d4, 1.0)
+    sum_four = scatter_rows(packed_four)
+
+    g3, local = spread(g, lambda near: conv_out_grad(near, conv_out_w))
+    pairs = [local] + [conv_out_grad(pair, conv_out_w) for pair in g3[1:]]
+    dn, bn_part = bn_back(order, conv, e_slope, moments, pairs, frame_total)
+    bn_sums = sum_axis(bn_part, "rows")
+    du, d_kernel, mine_c, theirs_c = conv_back(
+        order,
+        seg_near,
+        kernel_own,
+        dn,
+        conv,
+        moments,
+        bn_sums,
+        bn_gain_own,
+        conv_in_w,
+        kept,
+        frame_total,
+    )
+    parts, _ = collect(mine_c, theirs_c)
+    d2, g, gain_three = back_norm(parts, x2, norm_gains[2], d3, 1.0)
+
+    g2, local = spread(
+        g,
+        lambda near: (
+            att_grad(near, attn_w, share),
+            conv_grads([after(v, g) for v in sum(h3, ())], sum(g3, ()), du, e),
+        ),
+    )
+    local, parts_three = local
+    packed_three = pack_grads(parts_three)
+    pairs = [local] + [att_grad(pair, attn_w, share) for pair in g2[1:]]
+    dqkv, band, mine_a, theirs_a = attend_back(order, pairs, qkv, seg, table, lse, attn_w)
+
+    def attention_sums(ready):
+        packed = attend_grads(
+            order, [ready(v) for v in sum(h2, ())], sum(g2, ()), dqkv, att
         )
-        parts = collect([v[1] for v in back], [v[2] for v in back], (packed,))
-        return back_norm(parts, x, gain, prev, scale), packed
-
-    (d3, g, gain_four), packed_four = ffn_backward(
-        g, h4, four, f2, x3, norm_gains[3], d4, 1.0
-    )
-    sum_four = scatter_rows(packed_four)
-
-    g3 = gather_tm(g)
-    d_conv_out = mm_tn(e, g3).astype(BF)
-    dn = mm_nt(g3, conv_out_w) * silu_slope(shifted)
-    bn_part = jnp.stack([jnp.sum(dn, axis=0), jnp.sum(dn * normed_bn, axis=0)])
-    bn_sums = sum_axis(bn_part, "rows")
-    dc = (
-        bn_gain_own
-        * inverse_bn
-        * (dn - bn_sums[0] / frame_total - normed_bn * (bn_sums[1] / frame_total))
-    ).astype(BF)
-    dc_near = shifted_rows(dc)
-    dc_wide = dc.astype(F32)
-    dz = jnp.zeros((length, share), F32)
-    d_kernel = []
-    for k in range(taps):
-        mirror = taps - 1 - k
-        dz = dz + jnp.where(same[mirror], dc_near[mirror].astype(F32) * kernel_own[k], 0.0)
-        d_kernel.append(
-            jnp.sum(jnp.where(same[k], z_near[k].astype(F32) * dc_wide, 0.0), axis=0)
-        )
-    du = jnp.concatenate([dz * u_sig, dz * u_lin * u_sig * (1.0 - u_sig)], axis=1).astype(BF)
-    d_conv_in = mm_tn(h3, du).astype(BF)
-    parts_three = [d_conv_in, d_conv_out]
-    packed_three = pack_grads(parts_three)
-    parts_three = [d_conv_in, d_conv_out]
-    packed_three = pack_grads(parts_three)
-    d2, g, gain_three = back_norm(
-        [scatter_tm(mm_nt(du, conv_in_w).astype(BF), (packed_three,))],
-        x2,
-        norm_gains[2],
-        d3,
-        1.0,
-    )
-
-    g2, local = spread(g, lambda near: att_grad(near, attn_w, share))
-    pairs = [local] + [att_grad(pair, attn_w, share) for pair in g2[1:]]
-    dqkv, band, mine, theirs = attend_back(order, pairs, qkv, seg, table, lse, attn_w)
-    packed_two = attend_grads(order, sum(h2, ()), sum(g2, ()), dqkv, att)
-    packed_mid = jnp.concatenate([pack_grads([packed_two.reshape(width, -1)]), packed_three], axis=1) if packed_two.shape[2] == packed_three.shape[2] else None
-    parts = collect(mine, theirs, (packed_two,) if packed_mid is None else (packed_mid,))
+        if packed.shape[2] == packed_three.shape[2]:
+            return (jnp.concatenate([packed, packed_three], axis=1),)
+        return packed, packed_three
+
+    parts, packed_mid = collect(mine_a, theirs_a, attention_sums)
     d1, g, gain_two = back_norm(parts, x1, norm_gains[1], d2, 0.5)
-    if packed_mid is None:
-        sum_two, sum_three = scatter_rows(packed_two), scatter_rows(packed_three)
+    if len(packed_mid) == 1:
+        sum_mid = scatter_rows(packed_mid[0])
+        sum_two, sum_three = sum_mid[:depth], sum_mid[depth:]
     else:
-        sum_mid = scatter_rows(packed_mid)
-        sum_two, sum_three = sum_mid[:depth], sum_mid[depth:]
-
-    (grad, _, gain_one), packed_one = ffn_backward(
-        g, h1, one, f1, inputs, norm_gains[0], d1, 1.0
-    )
+        sum_two, sum_three = (scatter_rows(v) for v in packed_mid)
+
+    g1, local = spread(g, lambda near: ffn_back(near, one[0][1], *f1))
+    back = [local] + [ffn_back(p, one[i][1], *f1) for i, p in enumerate(g1[1:], 1)]
+    packed_one = ffn_grads(
+        sum(h1, ()), sum(g1, ()), [v[0] for v in back], [v[0] for v in one]
+    )
+    sum_one = scatter_rows(packed_one)
+    parts, _ = collect([v[1] for v in back], [v[2] for v in back])
+    grad, _, gain_one = back_norm(parts, inputs, norm_gains[0], d1, 1.0)
     grad_frames = grad.astype(BF)[None]
-    sum_one = scatter_rows(packed_one)
 
     def ffn_parts(total):
         if total.shape == (2 * depth, width) and ffn1_in.shape[1] == width:
@@ -1033,9 +1376,16 @@
         ]
         return unpack_grads(total, like)
 
-    grad_ffn2_in, grad_ffn2_out = ffn_return(
-        *ffn_parts(sum_four), ffn2_in.shape, ffn2_out.shape
-    )
+    def ffn_owned(total):
+        if whole_lanes(ffn1_in.shape, ffn1_out.shape):
+            return returned_ffn(total, ffn1_in.shape, ffn1_out.shape)
+        g_in, g_out = ffn_parts(total)
+        return (
+            ffn_back_in(g_in, ffn1_in.shape, ffn1_out.shape),
+            ffn_back_out(g_out, ffn1_out.shape),
+        )
+
+    grad_ffn2_in, grad_ffn2_out = ffn_owned(sum_four)
     grad_query, grad_key, grad_value, d_block = (
         sum_two[:, i * share : (i + 1) * share] for i in range(4)
     )
@@ -1055,9 +1405,7 @@
         .astype(F32)
     )
     grad_conv_out = d_out.reshape(depth, share).astype(F32)
-    grad_ffn1_in, grad_ffn1_out = ffn_return(
-        *ffn_parts(sum_one), ffn1_in.shape, ffn1_out.shape
-    )
+    grad_ffn1_in, grad_ffn1_out = ffn_owned(sum_one)
 
     table_row = lax.dynamic_update_slice_in_dim(
         jnp.zeros(rel_table.shape, F32), table_grad(band), t * heads, 0
@@ -1070,7 +1418,7 @@
             gain_three,
             gain_four,
             gain_five,
-            placed(jnp.stack(d_kernel)),
+            placed(d_kernel),
             placed(bn_part),
             table_row,
         ],

time: 640 us -> 629 us (0.983)
  Pallas kernels: 69.4 us -> 96.2 us
  local copies, waits for them, and re-layouts: 81.4 us -> 61.2 us
  other arithmetic: 30.2 us -> 16.9 us
  matrix products: 7.74 us -> 0 us
    pallas_call x0 -> x17, Pallas kernels: none -> 26.2 us  [the longest x1 4.79 us: conv_back(): pl.pallas_call(functools.partial(conv_back_kernel, taps=taps.shape[0], to...]
    ppermute x61 -> x66, waiting for transfers between devices: 206 us -> 221 us  [from_peer(): return lax.ppermute(a, 'tm', tm_peer(dx, dc))]
    all_gather x2 -> x3, waiting for transfers between devices: 78.5 us -> 65 us  [the longest x2 65 us: gather_ffn(): full = lax.all_gather(sent, 'rows', axis=0, tiled=False)]
    dot_general x6 -> x0, matrix products: 7.74 us -> none  [the longest x2 3.3 us: mm(): return jnp.dot(a, b, preferred_element_type=F32)]
    dynamic_update_slice x11 -> x0, local copies, waits for them, and re-layouts: 6.77 us -> none  [the longest x8 6.7 us: gather_tm(): out = lax.dynamic_update_index_in_dim(out, b, peer_index(dx, dc), 0)]
    ppermute x61 -> x66, starting transfers between devices: 42.4 us -> 46.4 us  [from_peer(): return lax.ppermute(a, 'tm', tm_peer(dx, dc))]
    unnamed x201 -> x208, local copies, waits for them, and re-layouts: 42.6 us -> 42.7 us
  transfers between devices with their start and end apart: 79 -> 85, of which waited for: 54 -> 59; matrix products, arithmetic and copies ran while one was open for 10% -> 6% of each run, Pallas kernels for 9% -> 13%
where the time goes in v3:
time: 629 us; the launch traced here: 624 us
  waiting for transfers between devices  374 us (59%)
  Pallas kernels  96.2 us (15%)
  local copies, waits for them, and re-layouts  61.2 us (10%)
  starting transfers between devices  60.2 us (10%)
  other arithmetic  16.9 us (3%)
  between operations  15.9 us (3%)
    ppermute x66, waiting for transfers between devices, from_peer(): return lax.ppermute(a, 'tm', tm_peer(dx, dc))  221 us
    all_gather x2, waiting for transfers between devices, gather_ffn(): full = lax.all_gather(sent, 'rows', axis=0, tiled=False)  65 us
    reduce_scatter x3, waiting for transfers between devices, scatter_rows(): return lax.psum_scatter(packed, 'rows', scatter_dimension=0, tiled=False)  61 us
    ppermute x66, starting transfers between devices, from_peer(): return lax.ppermute(a, 'tm', tm_peer(dx, dc))  46.4 us
    unnamed x208, local copies, waits for them, and re-layouts  42.7 us
    ppermute x11, waiting for transfers between devices, sum_axis(): v = v + lax.ppermute(v, axis, [(i, i ^ bit) for i in range(size)])  27.3 us
  transfers between devices with their start and end apart: 85, of which 59 were waited for; matrix products, arithmetic and copies ran while one was open for 6% of the time, Pallas kernels for 13%

profile of v3, /device:TPU:0, one launch (start us, length us, event | category | flops | bytes accessed | tf_op | source)
XLA Modules:
  0.0 624.4 jit_solution(2208311206297011640)
XLA Ops:
  25.8 5.1 collective-permute-start.8
  37.6 13.0 %collective-permute-done.4.h0.refs_2_ = bf16[256,1024]{1,0:T(8,128)(2,1)S(1)} collective-permute-done((bf16[256,1024]{1,0:T(8,128)(2,1)S(1)}, bf16[256,1024]{1,0:T(8,128)(2,1)S(1)}, u32[]{:S(2)}, u32[]{:S(2)}) %collective-permute-start.4) | collective-permute-done | bytes 524320 | tf_op jit(solution)/shard_map/ppermute | solution.py:72
  53.2 4.9 collective-permute-done.11.refs_2_
  62.2 65.0 %all-gather.7.cloned.1.call-done = bf16[3072,1024]{1,0:T(8,128)(2,1)} async-done(((bf16[384,1024]{1,0:T(8,128)(2,1)}), bf16[3072,1024]{1,0:T(8,128)(2,1)}) %all-gather.7.cloned.1.call-update) | async-done | bytes 6291472 | tf_op jit(solution)/shard_map/all_gather | solution.py:197
  138.6 11.9 %collective-permute-done.15.refs_2_ = bf16[256,1024]{1,0:T(8,128)(2,1)S(1)} collective-permute-done((bf16[256,1024]{1,0:T(8,128)(2,1)S(1)}, bf16[256,1024]{1,0:T(8,128)(2,1)S(1)}, u32[]{:S(2)}, u32[]{:S(2)}) %collective-permute-start.15) | collective-permute-done | bytes 524320 | tf_op jit(solution)/shard_map/ppermute | solution.py:72
  155.8 9.8 %collective-permute-done.17.h0.refs_2_ = bf16[256,1024]{1,0:T(8,128)(2,1)} collective-permute-done((bf16[256,1024]{1,0:T(8,128)(2,1)S(1)}, bf16[256,1024]{1,0:T(8,128)(2,1)}, u32[]{:S(2)}, u32[]{:S(2)}) %collective-permute-start.17) | collective-permute-done | bytes 524320 | tf_op jit(solution)/shard_map/ppermute | solution.py:72
  170.1 7.7 %shard_map.314 = (bf16[1024,768]{1,0:T(8,128)(2,1)S(1)}, bf16[1024,256]{1,0:T(8,128)(2,1)S(1)}, f32[2,1024,1]{2,1,0:T(8,128)S(1)}, f32[256,1024]{1,0:T(8,128)S(1...) custom-call(s32[4]{0:T(128)S(1)} %pad_add_fusion.to.order, ...), custom_call_target="tpu_custom_call" | custom-call | flops 1610612736 | bytes 1572864 | tf_op jit(solution)/shard_map/pallas_call | solution.py:706
  181.5 12.5 %collective-permute-done.21.refs_2_ = bf16[256,1024]{1,0:T(8,128)(2,1)S(1)} collective-permute-done((bf16[256,1024]{1,0:T(8,128)(2,1)S(1)}, bf16[256,1024]{1,0:T(8,128)(2,1)S(1)}, u32[]{:S(2)}, u32[]{:S(2)}) %collective-permute-start.21) | collective-permute-done | bytes 524320 | tf_op jit(solution)/shard_map/ppermute | solution.py:72
  202.6 8.4 %collective-permute-done.23.h0.refs_2_ = bf16[256,1024]{1,0:T(8,128)(2,1)} collective-permute-done((bf16[256,1024]{1,0:T(8,128)(2,1)}, bf16[256,1024]{1,0:T(8,128)(2,1)}, u32[]{:S(2)}, u32[]{:S(2)}) %collective-permute-start.23) | collective-permute-done | bytes 524320 | tf_op jit(solution)/shard_map/ppermute | solution.py:72
  238.3 12.5 %collective-permute-done.30.refs_2_ = bf16[256,1024]{1,0:T(8,128)(2,1)S(1)} collective-permute-done((bf16[256,1024]{1,0:T(8,128)(2,1)S(1)}, bf16[256,1024]{1,0:T(8,128)(2,1)S(1)}, u32[]{:S(2)}, u32[]{:S(2)}) %collective-permute-start.30) | collective-permute-done | bytes 524320 | tf_op jit(solution)/shard_map/ppermute | solution.py:72
  261.3 6.4 %collective-permute-done.33.h0.refs_2_ = bf16[256,1024]{1,0:T(8,128)(2,1)} collective-permute-done((bf16[256,1024]{1,0:T(8,128)(2,1)}, bf16[256,1024]{1,0:T(8,128)(2,1)}, u32[]{:S(2)}, u32[]{:S(2)}) %collective-permute-start.33) | collective-permute-done | bytes 524320 | tf_op jit(solution)/shard_map/ppermute | solution.py:72
  277.0 12.5 %collective-permute-done.36.refs_2_ = bf16[256,1024]{1,0:T(8,128)(2,1)S(1)} collective-permute-done((bf16[256,1024]{1,0:T(8,128)(2,1)S(1)}, bf16[256,1024]{1,0:T(8,128)(2,1)S(1)}, u32[]{:S(2)}, u32[]{:S(2)}) %collective-permute-start.36) | collective-permute-done | bytes 524320 | tf_op jit(solution)/shard_map/ppermute | solution.py:72
  297.5 9.1 %collective-permute-done.39.g0.refs_6_ = bf16[256,1024]{1,0:T(8,128)(2,1)S(1)} collective-permute-done((bf16[256,1024]{1,0:T(8,128)(2,1)S(1)}, bf16[256,1024]{1,0:T(8,128)(2,1)S(1)}, u32[]{:S(2)}, u32[]{:S(2)}) %collective-permute-start.39) | collective-permute-done | bytes 524320 | tf_op jit(solution)/shard_map/ppermute | solution.py:72
  313.8 6.0 shard_map.326
  324.1 12.4 %collective-permute-done.42.refs_2_ = bf16[256,1024]{1,0:T(8,128)(2,1)S(1)} collective-permute-done((bf16[256,1024]{1,0:T(8,128)(2,1)}, bf16[256,1024]{1,0:T(8,128)(2,1)S(1)}, u32[]{:S(2)}, u32[]{:S(2)}) %collective-permute-start.42) | collective-permute-done | bytes 524320 | tf_op jit(solution)/shard_map/ppermute | solution.py:72
  343.6 12.0 %collective-permute-done.44.g0.refs_6_ = bf16[256,1024]{1,0:T(8,128)(2,1)S(1)} collective-permute-done((bf16[256,1024]{1,0:T(8,128)(2,1)S(1)}, bf16[256,1024]{1,0:T(8,128)(2,1)S(1)}, u32[]{:S(2)}, u32[]{:S(2)}) %collective-permute-start.44) | collective-permute-done | bytes 524320 | tf_op jit(solution)/shard_map/ppermute | solution.py:72
  379.1 12.5 %collective-permute-done.51.refs_2_ = bf16[256,1024]{1,0:T(8,128)(2,1)S(1)} collective-permute-done((bf16[256,1024]{1,0:T(8,128)(2,1)S(1)}, bf16[256,1024]{1,0:T(8,128)(2,1)S(1)}, u32[]{:S(2)}, u32[]{:S(2)}) %collective-permute-start.51) | collective-permute-done | bytes 524320 | tf_op jit(solution)/shard_map/ppermute | solution.py:72
  398.8 9.0 %collective-permute-done.53.g0.refs_6_ = bf16[256,1024]{1,0:T(8,128)(2,1)S(1)} collective-permute-done((bf16[256,1024]{1,0:T(8,128)(2,1)S(1)}, bf16[256,1024]{1,0:T(8,128)(2,1)S(1)}, u32[]{:S(2)}, u32[]{:S(2)}) %collective-permute-start.53) | collective-permute-done | bytes 524320 | tf_op jit(solution)/shard_map/ppermute | solution.py:72
  410.2 11.5 %shard_map.336 = (bf16[1024,768]{1,0:T(8,128)(2,1)S(1)}, f32[2,128,640]{2,1,0:T(8,128)S(1)}, f32[256,1024]{1,0:T(8,128)S(1)}, f32[256,1024]{1,0:T(8,128)S(1)}, b...) custom-call(s32[4]{0:T(128)S(1)} %pad_add_fusion.to.order, f32[2,17]{1,0:T(2,128)S(1)} %constant_dynamic-slice_fusion.2.tab_ref, ...), custom_call_target="tpu_custom_call" | custom-call | flops 3221225472 | bytes 524288 | tf_op jit(solution)/shard_map/pallas_call | solution.py:835
  432.8 12.4 %collective-permute-done.57.refs_2_ = bf16[256,1024]{1,0:T(8,128)(2,1)S(1)} collective-permute-done((bf16[256,1024]{1,0:T(8,128)(2,1)S(1)}, bf16[256,1024]{1,0:T(8,128)(2,1)S(1)}, u32[]{:S(2)}, u32[]{:S(2)}) %collective-permute-start.57) | collective-permute-done | bytes 524320 | tf_op jit(solution)/shard_map/ppermute | solution.py:72
  456.8 6.3 %collective-permute-done.60.g0.refs_6_ = bf16[256,1024]{1,0:T(8,128)(2,1)S(1)} collective-permute-done((bf16[256,1024]{1,0:T(8,128)(2,1)S(1)}, bf16[256,1024]{1,0:T(8,128)(2,1)S(1)}, u32[]{:S(2)}, u32[]{:S(2)}) %collective-permute-start.60) | collective-permute-done | bytes 524320 | tf_op jit(solution)/shard_map/ppermute | solution.py:72
  469.3 5.2 shard_map.342
  488.1 11.0 %collective-permute-done.63.refs_2_ = bf16[256,1024]{1,0:T(8,128)(2,1)} collective-permute-done((bf16[256,1024]{1,0:T(8,128)(2,1)}, bf16[256,1024]{1,0:T(8,128)(2,1)}, u32[]{:S(2)}, u32[]{:S(2)}) %collective-permute-start.63) | collective-permute-done | bytes 524320 | tf_op jit(solution)/shard_map/ppermute | solution.py:72
  544.8 61.0 %reduce-scatter.4.cloned.1.call-done = bf16[1,256,1024]{2,1,0:T(8,128)(2,1)} async-done(((bf16[8,256,1024]{2,1,0:T(8,128)(2,1)}), bf16[1,256,1024]{2,1,0:T(8,128)(2,1)}) %reduce-scatter.4.cloned.1.call-update) | async-done | bytes 524304 | tf_op jit(solution)/shard_map/reduce_scatter | solution.py:189
  (525 shorter events, 270.2 us)
Async XLA Ops:
  7.2 119.9 %all-gather.7.cloned.1.call-start = ((), (), s32[]{:S(2)}) async-start(), calls=%async_computation.6 | async-start | bytes 7077888 | tf_op jit(solution)/shard_map/all_gather | solution.py:197
  23.7 174.1 %all-gather.9.cloned.1.call-start = ((), (), s32[]{:S(2)}) async-start(), calls=%async_computation.7 | async-start | bytes 1769472 | tf_op jit(solution)/shard_map/all_gather | solution.py:1261
  35.7 218.9 %all-gather.11.cloned.1.call-start = ((), (), s32[]{:S(2)}) async-start(), calls=%async_computation.8 | async-start | bytes 4718592 | tf_op jit(solution)/shard_map/all_gather | solution.py:197
  36.5 14.1 %collective-permute-start.4 = (bf16[256,1024]{1,0:T(8,128)(2,1)S(1)}, bf16[256,1024]{1,0:T(8,128)(2,1)S(1)}, u32[]{:S(2)}, u32[]{:S(2)}) collective-permute-start(bf16[256,1024]{1,0:T(8,128)(2,1)S(1)} %multiply_convert_fusion.h0.refs_0_), channel_id=1, source_target_pairs={{2,0},{3,1},{0,2},{1,3},{6,4},{7,5},{4,6},{5,7},{10,8},{11,9},{8,1... | collective-permute-start | bytes 1572872 | tf_op jit(solution)/shard_map/ppermute | solution.py:72
  60.6 463.5 %reduce-scatter.8.cloned.1.call-start = ((), (), s32[]{:S(2)}) async-start(), calls=%async_computation.5 | async-start | bytes 4718592 | tf_op jit(solution)/shard_map/reduce_scatter | solution.py:189
  61.0 72.4 %collective-permute-start.13 = (bf16[256,1024]{1,0:T(8,128)(2,1)S(1)}, bf16[256,1024]{1,0:T(8,128)(2,1)S(1)}, u32[]{:S(2)}, u32[]{:S(2)}) collective-permute-start(bf16[256,1024]{1,0:T(8,128)(2,1)S(1)} %multiply_convert_fusion.h0.refs_0_), channel_id=1, source_target_pairs={{1,0},{0,1},{3,2},{2,3},{5,4},{4,5},{7,6},{6,7},{9,8},{8,9},{11,10... | collective-permute-start | bytes 1572872 | tf_op jit(solution)/shard_map/ppermute | solution.py:72
  136.7 13.9 %collective-permute-start.15 = (bf16[256,1024]{1,0:T(8,128)(2,1)S(1)}, bf16[256,1024]{1,0:T(8,128)(2,1)S(1)}, u32[]{:S(2)}, u32[]{:S(2)}) collective-permute-start(bf16[256,1024]{1,0:T(8,128)(2,1)S(1)} %add_convert_fusion.7), channel_id=1, source_target_pairs={{2,0},{3,1},{0,2},{1,3},{6,4},{7,5},{4,6},{5,7},{10,8},{11,9},{8,1... | collective-permute-start | bytes 1572872 | tf_op jit(solution)/shard_map/ppermute | solution.py:72
  151.2 14.4 %collective-permute-start.17 = (bf16[256,1024]{1,0:T(8,128)(2,1)S(1)}, bf16[256,1024]{1,0:T(8,128)(2,1)}, u32[]{:S(2)}, u32[]{:S(2)}) collective-permute-start(bf16[256,1024]{1,0:T(8,128)(2,1)S(1)} %get-tuple-element.257.h0.refs_0_), channel_id=1, source_target_pairs={{2,0},{3,1},{0,2},{1,3},{6,4},{7,5},{4,6},{5,7},{10,8},{11,9},{8,1... | collective-permute-start | bytes 1572872 | tf_op jit(solution)/shard_map/ppermute | solution.py:72
  180.0 14.0 %collective-permute-start.21 = (bf16[256,1024]{1,0:T(8,128)(2,1)S(1)}, bf16[256,1024]{1,0:T(8,128)(2,1)S(1)}, u32[]{:S(2)}, u32[]{:S(2)}) collective-permute-start(bf16[256,1024]{1,0:T(8,128)(2,1)S(1)} %add_convert_fusion.6), channel_id=1, source_target_pairs={{2,0},{3,1},{0,2},{1,3},{6,4},{7,5},{4,6},{5,7},{10,8},{11,9},{8,1... | collective-permute-start | bytes 1572872 | tf_op jit(solution)/shard_map/ppermute | solution.py:72
  196.3 14.6 %collective-permute-start.23 = (bf16[256,1024]{1,0:T(8,128)(2,1)}, bf16[256,1024]{1,0:T(8,128)(2,1)}, u32[]{:S(2)}, u32[]{:S(2)}) collective-permute-start(bf16[256,1024]{1,0:T(8,128)(2,1)} %get-tuple-element.244.h0.refs_0_), channel_id=1, source_target_pairs={{2,0},{3,1},{0,2},{1,3},{6,4},{7,5},{4,6},{5,7},{10,8},{11,9},{8,1... | collective-permute-start | bytes 1572872 | tf_op jit(solution)/shard_map/ppermute | solution.py:72
  236.8 14.0 %collective-permute-start.30 = (bf16[256,1024]{1,0:T(8,128)(2,1)S(1)}, bf16[256,1024]{1,0:T(8,128)(2,1)S(1)}, u32[]{:S(2)}, u32[]{:S(2)}) collective-permute-start(bf16[256,1024]{1,0:T(8,128)(2,1)S(1)} %add_convert_fusion.5), channel_id=1, source_target_pairs={{2,0},{3,1},{0,2},{1,3},{6,4},{7,5},{4,6},{5,7},{10,8},{11,9},{8,1... | collective-permute-start | bytes 1572872 | tf_op jit(solution)/shard_map/ppermute | solution.py:72
  253.1 14.7 %collective-permute-start.33 = (bf16[256,1024]{1,0:T(8,128)(2,1)}, bf16[256,1024]{1,0:T(8,128)(2,1)}, u32[]{:S(2)}, u32[]{:S(2)}) collective-permute-start(bf16[256,1024]{1,0:T(8,128)(2,1)} %get-tuple-element.219.h0.refs_0_), channel_id=1, source_target_pairs={{2,0},{3,1},{0,2},{1,3},{6,4},{7,5},{4,6},{5,7},{10,8},{11,9},{8,1... | collective-permute-start | bytes 1572872 | tf_op jit(solution)/shard_map/ppermute | solution.py:72
  275.5 14.0 %collective-permute-start.36 = (bf16[256,1024]{1,0:T(8,128)(2,1)S(1)}, bf16[256,1024]{1,0:T(8,128)(2,1)S(1)}, u32[]{:S(2)}, u32[]{:S(2)}) collective-permute-start(bf16[256,1024]{1,0:T(8,128)(2,1)S(1)} %add_convert_fusion.4), channel_id=1, source_target_pairs={{2,0},{3,1},{0,2},{1,3},{6,4},{7,5},{4,6},{5,7},{10,8},{11,9},{8,1... | collective-permute-start | bytes 1572872 | tf_op jit(solution)/shard_map/ppermute | solution.py:72
  292.3 14.3 %collective-permute-start.39 = (bf16[256,1024]{1,0:T(8,128)(2,1)S(1)}, bf16[256,1024]{1,0:T(8,128)(2,1)S(1)}, u32[]{:S(2)}, u32[]{:S(2)}) collective-permute-start(bf16[256,1024]{1,0:T(8,128)(2,1)S(1)} %get-tuple-element.211.g0.refs_4_), channel_id=1, source_target_pairs={{2,0},{3,1},{0,2},{1,3},{6,4},{7,5},{4,6},{5,7},{10,8},{11,9},{8,1... | collective-permute-start | bytes 1572872 | tf_op jit(solution)/shard_map/ppermute | solution.py:72
  321.8 214.6 %reduce-scatter.6.cloned.1.call-start = ((), (), s32[]{:S(2)}) async-start(), calls=%async_computation.4 | async-start | bytes 4128768 | tf_op jit(solution)/shard_map/reduce_scatter | solution.py:189
  322.1 14.4 %collective-permute-start.42 = (bf16[256,1024]{1,0:T(8,128)(2,1)}, bf16[256,1024]{1,0:T(8,128)(2,1)S(1)}, u32[]{:S(2)}, u32[]{:S(2)}) collective-permute-start(bf16[256,1024]{1,0:T(8,128)(2,1)} %add_convert_fusion.3), channel_id=1, source_target_pairs={{2,0},{3,1},{0,2},{1,3},{6,4},{7,5},{4,6},{5,7},{10,8},{11,9},{8,1... | collective-permute-start | bytes 1572872 | tf_op jit(solution)/shard_map/ppermute | solution.py:72
  341.3 14.3 %collective-permute-start.44 = (bf16[256,1024]{1,0:T(8,128)(2,1)S(1)}, bf16[256,1024]{1,0:T(8,128)(2,1)S(1)}, u32[]{:S(2)}, u32[]{:S(2)}) collective-permute-start(bf16[256,1024]{1,0:T(8,128)(2,1)S(1)} %get-tuple-element.229.g0.refs_4_), channel_id=1, source_target_pairs={{2,0},{3,1},{0,2},{1,3},{6,4},{7,5},{4,6},{5,7},{10,8},{11,9},{8,1... | collective-permute-start | bytes 1572872 | tf_op jit(solution)/shard_map/ppermute | solution.py:72
  377.5 14.0 %collective-permute-start.51 = (bf16[256,1024]{1,0:T(8,128)(2,1)S(1)}, bf16[256,1024]{1,0:T(8,128)(2,1)S(1)}, u32[]{:S(2)}, u32[]{:S(2)}) collective-permute-start(bf16[256,1024]{1,0:T(8,128)(2,1)S(1)} %add_convert_fusion.2), channel_id=1, source_target_pairs={{2,0},{3,1},{0,2},{1,3},{6,4},{7,5},{4,6},{5,7},{10,8},{11,9},{8,1... | collective-permute-start | bytes 1572872 | tf_op jit(solution)/shard_map/ppermute | solution.py:72
  393.5 14.3 %collective-permute-start.53 = (bf16[256,1024]{1,0:T(8,128)(2,1)S(1)}, bf16[256,1024]{1,0:T(8,128)(2,1)S(1)}, u32[]{:S(2)}, u32[]{:S(2)}) collective-permute-start(bf16[256,1024]{1,0:T(8,128)(2,1)S(1)} %get-tuple-element.241.g0.refs_4_), channel_id=1, source_target_pairs={{2,0},{3,1},{0,2},{1,3},{6,4},{7,5},{4,6},{5,7},{10,8},{11,9},{8,1... | collective-permute-start | bytes 1572872 | tf_op jit(solution)/shard_map/ppermute | solution.py:72
  429.9 175.9 %reduce-scatter.4.cloned.1.call-start = ((), (), s32[]{:S(2)}) async-start(), calls=%async_computation.3 | async-start | bytes 4718592 | tf_op jit(solution)/shard_map/reduce_scatter | solution.py:189
  431.0 14.2 %collective-permute-start.57 = (bf16[256,1024]{1,0:T(8,128)(2,1)S(1)}, bf16[256,1024]{1,0:T(8,128)(2,1)S(1)}, u32[]{:S(2)}, u32[]{:S(2)}) collective-permute-start(bf16[256,1024]{1,0:T(8,128)(2,1)S(1)} %add_convert_fusion.1), channel_id=1, source_target_pairs={{2,0},{3,1},{0,2},{1,3},{6,4},{7,5},{4,6},{5,7},{10,8},{11,9},{8,1... | collective-permute-start | bytes 1572872 | tf_op jit(solution)/shard_map/ppermute | solution.py:72
  448.7 14.3 %collective-permute-start.60 = (bf16[256,1024]{1,0:T(8,128)(2,1)S(1)}, bf16[256,1024]{1,0:T(8,128)(2,1)S(1)}, u32[]{:S(2)}, u32[]{:S(2)}) collective-permute-start(bf16[256,1024]{1,0:T(8,128)(2,1)S(1)} %get-tuple-element.263.g0.refs_4_), channel_id=1, source_target_pairs={{2,0},{3,1},{0,2},{1,3},{6,4},{7,5},{4,6},{5,7},{10,8},{11,9},{8,1... | collective-permute-start | bytes 1572872 | tf_op jit(solution)/shard_map/ppermute | solution.py:72
  484.9 14.3 %collective-permute-start.63 = (bf16[256,1024]{1,0:T(8,128)(2,1)}, bf16[256,1024]{1,0:T(8,128)(2,1)}, u32[]{:S(2)}, u32[]{:S(2)}) collective-permute-start(bf16[256,1024]{1,0:T(8,128)(2,1)} %add_convert_fusion), channel_id=1, source_target_pairs={{2,0},{3,1},{0,2},{1,3},{6,4},{7,5},{4,6},{5,7},{10,8},{11,9},{8,1... | collective-permute-start | bytes 1572872 | tf_op jit(solution)/shard_map/ppermute | solution.py:72
  542.5 69.2 %collective-permute-start.67 = (bf16[128,256]{1,0:T(8,128)(2,1)S(1)}, bf16[128,256]{1,0:T(8,128)(2,1)S(1)}, u32[]{:S(2)}, u32[]{:S(2)}) collective-permute-start(bf16[128,256]{1,0:T(8,128)(2,1)S(1)} %get-tuple-element.381), channel_id=1, source_target_pairs={{0,0},{1,8},{2,16},{3,24},{4,1},{5,9},{6,17},{7,25},{8,2},{9,10},{... | collective-permute-start | bytes 196616 | tf_op jit(solution)/shard_map/ppermute | solution.py:1393
  (164 other events, 1647.4 us)
Sparse Core Ops, SparseCore 0:
  23.9 103.2 all-gather.6
  129.9 42.3 all-gather.8
  175.0 72.2 all-gather.10
  322.0 86.6 reduce-scatter.7
  430.0 79.5 reduce-scatter.5
  513.6 92.1 reduce-scatter.3

commit v4 on v3

--- a/solution.py
+++ b/solution.py
@@ -11,6 +11,7 @@
 RELMAX = 8
 LANES = 128
 EPS = 1e-05
+LOG2E = 1.4426950408889634
 BF = jnp.bfloat16
 F32 = jnp.float32
 SMEM = pl.BlockSpec(memory_space=pltpu.SMEM)
@@ -294,7 +295,7 @@
         functools.partial(cut_kernel, unit=unit),
         in_specs=[SMEM] + vmem(2),
         out_shape=[jax.ShapeDtypeStruct((m + unit, w), BF)] * size,
-        compiler_params=params(8),
+        compiler_params=params(60),
         cost_estimate=cost(0, w_in, w_out),
     )(to, w_in, w_out)
     got = [pieces[0]] + [from_peer(p, *at) for p, at in zip(pieces[1:], rel[1:])]
@@ -303,7 +304,7 @@
         functools.partial(lay_kernel, size=size),
         in_specs=[SMEM] + vmem(size + len(more)),
         out_shape=jax.ShapeDtypeStruct((n, w * size), BF),
-        compiler_params=params(8),
+        compiler_params=params(60),
         cost_estimate=cost(0, w_in, w_out),
     )(order, *got, *more)
 
@@ -538,7 +539,7 @@
     n, d = x.shape
     return pl.pallas_call(
         functools.partial(add_norm_kernel, scale=scale),
-        out_shape=[jax.ShapeDtypeStruct((n, d), F32), jax.ShapeDtypeStruct((n, d), BF)],
+        out_shape=[pltpu.HBM((n, d), F32), jax.ShapeDtypeStruct((n, d), BF)],
         compiler_params=params(12),
         cost_estimate=cost(0, x, x, x),
     )(*parts, x, gain[None])
@@ -563,7 +564,7 @@
         turn_kernel,
         out_shape=[
             jax.ShapeDtypeStruct((n, d), BF),
-            jax.ShapeDtypeStruct((n, d), F32),
+            pltpu.HBM((n, d), F32),
             jax.ShapeDtypeStruct((n, d), BF),
             jax.ShapeDtypeStruct((1, d), F32),
         ],
@@ -590,7 +591,7 @@
     return pl.pallas_call(
         functools.partial(back_norm_kernel, scale=scale),
         out_shape=[
-            jax.ShapeDtypeStruct((n, d), F32),
+            pltpu.HBM((n, d), F32),
             jax.ShapeDtypeStruct((n, d), BF),
             jax.ShapeDtypeStruct((1, d), F32),
         ],
@@ -627,7 +628,8 @@
 
 def fill_bias(tab_ref, head, strip, length):
     lo, hi = length - LANES, length + 2 * LANES
-    first, last = tab_ref[head, 0], tab_ref[head, 2 * RELMAX]
+    entry = lambda b: tab_ref[head, b] * LOG2E
+    first, last = entry(0), entry(2 * RELMAX)
     offset = (
         lax.broadcasted_iota(jnp.int32, (LANES, hi - lo), 1)
         - LANES
@@ -635,14 +637,14 @@
     )
     tile = jnp.where(offset <= -RELMAX, first, last)
     for b in range(1, 2 * RELMAX):
-        tile = jnp.where(offset == b - RELMAX, tab_ref[head, b], tile)
+        tile = jnp.where(offset == b - RELMAX, entry(b), tile)
     strip[:, :lo] = jnp.full((LANES, lo), first, F32)
     strip[:, lo:hi] = tile
     strip[:, hi:] = jnp.full((LANES, 2 * length - hi), last, F32)
 
 
 def biased(q, k, seg_col, seg_row, strip, first, length):
-    raw = mm_nt(q, k) * HEAD_DIM ** (-0.5)
+    raw = mm_nt(q, k) * (HEAD_DIM ** (-0.5) * LOG2E)
     parts = [
         strip[:, length - (first + a) : 2 * length - (first + a)]
         for a in range(0, q.shape[0], LANES)
@@ -678,11 +680,11 @@
         q = qkv[own, head_columns(0, head, heads)]
         sc = biased(q, k, seg_col_ref[own, :], seg_row_ref[...], strip, first, length)
         peak = jnp.max(sc, axis=1, keepdims=True)
-        e = jnp.exp(sc - peak)
+        e = jnp.exp2(sc - peak)
         total = jnp.sum(e, axis=1, keepdims=True)
-        p = (e * (1.0 / total)).astype(BF)
-        att[own, head_columns(0, head, heads)] = mm(p, v).astype(BF)
-        lse_ref[0, own, :] = peak + jnp.log(total)
+        inverse = 1.0 / total
+        att[own, head_columns(0, head, heads)] = (mm(e.astype(BF), v) * inverse).astype(BF)
+        lse_ref[0, own, :] = peak + jnp.log(total) * LOG2E
 
     @pl.when(head == heads - 1)
     def _():
@@ -786,7 +788,7 @@
         own = slice(first, first + block)
         q, do = qkv[own, at(0)], grad[own, at(0)]
         sc = biased(q, k, seg_col_ref[own, :], seg_row_ref[...], strip, first, length)
-        p = jnp.exp(sc - lse_ref[0, own, :])
+        p = jnp.exp2(sc - lse_ref[0, own, :])
         dp = mm_nt(do, v)
         inner = jnp.sum(p * dp, axis=1, keepdims=True)
         ds = (p * (dp - inner)).astype(BF)
@@ -1307,7 +1309,7 @@
         ),
     )
     d3, g, gain_four = back_norm(parts, x3, norm_gains[3], d4, 1.0)
-    sum_four = scatter_rows(packed_four)
+    sum_four = scatter_rows(after(packed_four, g))
 
     g3, local = spread(g, lambda near: conv_out_grad(near, conv_out_w))
     pairs = [local] + [conv_out_grad(pair, conv_out_w) for pair in g3[1:]]

time: 629 us -> 621 us (0.987)
  waiting for transfers between devices: 374 us -> 365 us
  local copies, waits for them, and re-layouts: 61.2 us -> 53.2 us
  Pallas kernels: 96.2 us -> 103 us
    ppermute x66, waiting for transfers between devices: 221 us -> 210 us  [from_peer(): return lax.ppermute(a, 'tm', tm_peer(dx, dc))]
    unnamed x208 -> x210, local copies, waits for them, and re-layouts: 42.7 us -> 34.6 us
  transfers between devices with their start and end apart: 85 -> 85, of which waited for: 59 -> 58; matrix products, arithmetic and copies ran while one was open for 6% -> 6% of each run, Pallas kernels for 13% -> 14%
where the time goes in v4:
time: 621 us; the launch traced here: 616 us
  waiting for transfers between devices  365 us (59%)
  Pallas kernels  103 us (17%)
  starting transfers between devices  60.7 us (10%)
  local copies, waits for them, and re-layouts  53.2 us (9%)
  other arithmetic  18.2 us (3%)
  between operations  16 us (3%)
    ppermute x66, waiting for transfers between devices, from_peer(): return lax.ppermute(a, 'tm', tm_peer(dx, dc))  210 us
    reduce_scatter x3, waiting for transfers between devices, scatter_rows(): return lax.psum_scatter(packed, 'rows', scatter_dimension=0, tiled=False)  64.8 us
    all_gather x2, waiting for transfers between devices, gather_ffn(): full = lax.all_gather(sent, 'rows', axis=0, tiled=False)  62.4 us
    ppermute x66, starting transfers between devices, from_peer(): return lax.ppermute(a, 'tm', tm_peer(dx, dc))  46.6 us
    unnamed x210, local copies, waits for them, and re-layouts  34.6 us
    ppermute x11, waiting for transfers between devices, sum_axis(): v = v + lax.ppermute(v, axis, [(i, i ^ bit) for i in range(size)])  27 us
  transfers between devices with their start and end apart: 85, of which 58 were waited for; matrix products, arithmetic and copies ran while one was open for 6% of the time, Pallas kernels for 14%

profile of v4, /device:TPU:0, one launch (start us, length us, event | category | flops | bytes accessed | tf_op | source)
XLA Modules:
  0.0 616.1 jit_solution(15818827992421562516)
XLA Ops:
  24.7 4.9 collective-permute-start.8
  36.3 13.0 %collective-permute-done.4.h0.refs_2_ = bf16[256,1024]{1,0:T(8,128)(2,1)S(1)} collective-permute-done((bf16[256,1024]{1,0:T(8,128)(2,1)S(1)}, bf16[256,1024]{1,0:T(8,128)(2,1)S(1)}, u32[]{:S(2)}, u32[]{:S(2)}) %collective-permute-start.4) | collective-permute-done | bytes 524320 | tf_op jit(solution)/shard_map/ppermute | solution.py:73
  53.3 5.0 collective-permute-done.11.refs_2_
  63.5 62.4 %all-gather.7.cloned.1.call-done = bf16[3072,1024]{1,0:T(8,128)(2,1)} async-done(((bf16[384,1024]{1,0:T(8,128)(2,1)}), bf16[3072,1024]{1,0:T(8,128)(2,1)}) %all-gather.7.cloned.1.call-update) | async-done | bytes 6291472 | tf_op jit(solution)/shard_map/all_gather | solution.py:198
  137.4 11.9 %collective-permute-done.15.refs_2_ = bf16[256,1024]{1,0:T(8,128)(2,1)S(1)} collective-permute-done((bf16[256,1024]{1,0:T(8,128)(2,1)S(1)}, bf16[256,1024]{1,0:T(8,128)(2,1)S(1)}, u32[]{:S(2)}, u32[]{:S(2)}) %collective-permute-start.15) | collective-permute-done | bytes 524320 | tf_op jit(solution)/shard_map/ppermute | solution.py:73
  155.2 9.7 %collective-permute-done.17.h0.refs_2_ = bf16[256,1024]{1,0:T(8,128)(2,1)S(1)} collective-permute-done((bf16[256,1024]{1,0:T(8,128)(2,1)S(1)}, bf16[256,1024]{1,0:T(8,128)(2,1)S(1)}, u32[]{:S(2)}, u32[]{:S(2)}) %collective-permute-start.17) | collective-permute-done | bytes 524320 | tf_op jit(solution)/shard_map/ppermute | solution.py:73
  167.9 6.4 %shard_map.314 = (bf16[1024,768]{1,0:T(8,128)(2,1)S(1)}, bf16[1024,256]{1,0:T(8,128)(2,1)S(1)}, f32[2,1024,1]{2,1,0:T(8,128)S(1)}, f32[256,1024]{1,0:T(8,128)S(1...) custom-call(s32[4]{0:T(128)S(1)} %copy-done.78, ...), custom_call_target="tpu_custom_call" | custom-call | flops 1610612736 | bytes 1572864 | tf_op jit(solution)/shard_map/pallas_call | solution.py:708
  177.9 12.5 %collective-permute-done.21.refs_2_ = bf16[256,1024]{1,0:T(8,128)(2,1)S(1)} collective-permute-done((bf16[256,1024]{1,0:T(8,128)(2,1)S(1)}, bf16[256,1024]{1,0:T(8,128)(2,1)S(1)}, u32[]{:S(2)}, u32[]{:S(2)}) %collective-permute-start.21) | collective-permute-done | bytes 524320 | tf_op jit(solution)/shard_map/ppermute | solution.py:73
  198.1 8.3 %collective-permute-done.23.h0.refs_2_ = bf16[256,1024]{1,0:T(8,128)(2,1)} collective-permute-done((bf16[256,1024]{1,0:T(8,128)(2,1)}, bf16[256,1024]{1,0:T(8,128)(2,1)}, u32[]{:S(2)}, u32[]{:S(2)}) %collective-permute-start.23) | collective-permute-done | bytes 524320 | tf_op jit(solution)/shard_map/ppermute | solution.py:73
  234.0 12.5 %collective-permute-done.30.refs_2_ = bf16[256,1024]{1,0:T(8,128)(2,1)S(1)} collective-permute-done((bf16[256,1024]{1,0:T(8,128)(2,1)S(1)}, bf16[256,1024]{1,0:T(8,128)(2,1)S(1)}, u32[]{:S(2)}, u32[]{:S(2)}) %collective-permute-start.30) | collective-permute-done | bytes 524320 | tf_op jit(solution)/shard_map/ppermute | solution.py:73
  256.0 6.4 %collective-permute-done.33.h0.refs_2_ = bf16[256,1024]{1,0:T(8,128)(2,1)} collective-permute-done((bf16[256,1024]{1,0:T(8,128)(2,1)}, bf16[256,1024]{1,0:T(8,128)(2,1)}, u32[]{:S(2)}, u32[]{:S(2)}) %collective-permute-start.33) | collective-permute-done | bytes 524320 | tf_op jit(solution)/shard_map/ppermute | solution.py:73
  271.7 12.5 %collective-permute-done.36.refs_2_ = bf16[256,1024]{1,0:T(8,128)(2,1)S(1)} collective-permute-done((bf16[256,1024]{1,0:T(8,128)(2,1)S(1)}, bf16[256,1024]{1,0:T(8,128)(2,1)S(1)}, u32[]{:S(2)}, u32[]{:S(2)}) %collective-permute-start.36) | collective-permute-done | bytes 524320 | tf_op jit(solution)/shard_map/ppermute | solution.py:73
  291.7 9.3 %collective-permute-done.39.g0.refs_6_ = bf16[256,1024]{1,0:T(8,128)(2,1)S(1)} collective-permute-done((bf16[256,1024]{1,0:T(8,128)(2,1)S(1)}, bf16[256,1024]{1,0:T(8,128)(2,1)S(1)}, u32[]{:S(2)}, u32[]{:S(2)}) %collective-permute-start.39) | collective-permute-done | bytes 524320 | tf_op jit(solution)/shard_map/ppermute | solution.py:73
  309.7 6.0 shard_map.326
  317.7 4.8 collective-permute-done.42.refs_2_
  335.1 9.8 %collective-permute-done.44.g0.refs_6_ = bf16[256,1024]{1,0:T(8,128)(2,1)S(1)} collective-permute-done((bf16[256,1024]{1,0:T(8,128)(2,1)}, bf16[256,1024]{1,0:T(8,128)(2,1)S(1)}, u32[]{:S(2)}, u32[]{:S(2)}) %collective-permute-start.44) | collective-permute-done | bytes 524320 | tf_op jit(solution)/shard_map/ppermute | solution.py:73
  368.6 12.5 %collective-permute-done.51.refs_2_ = bf16[256,1024]{1,0:T(8,128)(2,1)S(1)} collective-permute-done((bf16[256,1024]{1,0:T(8,128)(2,1)S(1)}, bf16[256,1024]{1,0:T(8,128)(2,1)S(1)}, u32[]{:S(2)}, u32[]{:S(2)}) %collective-permute-start.51) | collective-permute-done | bytes 524320 | tf_op jit(solution)/shard_map/ppermute | solution.py:73
  388.3 9.0 %collective-permute-done.53.g0.refs_6_ = bf16[256,1024]{1,0:T(8,128)(2,1)S(1)} collective-permute-done((bf16[256,1024]{1,0:T(8,128)(2,1)S(1)}, bf16[256,1024]{1,0:T(8,128)(2,1)S(1)}, u32[]{:S(2)}, u32[]{:S(2)}) %collective-permute-start.53) | collective-permute-done | bytes 524320 | tf_op jit(solution)/shard_map/ppermute | solution.py:73
  399.7 11.2 %shard_map.336 = (bf16[1024,768]{1,0:T(8,128)(2,1)S(1)}, f32[2,128,640]{2,1,0:T(8,128)S(1)}, f32[256,1024]{1,0:T(8,128)S(1)}, f32[256,1024]{1,0:T(8,128)S(1)}, b...) custom-call(s32[4]{0:T(128)S(1)} %copy-done.78, f32[2,17]{1,0:T(2,128)S(1)} %constant_dynamic-slice_fusion.2.tab_ref, ...), custom_call_target="tpu_custom_call" | custom-call | flops 3221225472 | bytes 524288 | tf_op jit(solution)/shard_map/pallas_call | solution.py:837
  421.6 12.4 %collective-permute-done.57.refs_2_ = bf16[256,1024]{1,0:T(8,128)(2,1)S(1)} collective-permute-done((bf16[256,1024]{1,0:T(8,128)(2,1)}, bf16[256,1024]{1,0:T(8,128)(2,1)S(1)}, u32[]{:S(2)}, u32[]{:S(2)}) %collective-permute-start.57) | collective-permute-done | bytes 524320 | tf_op jit(solution)/shard_map/ppermute | solution.py:73
  445.1 6.4 %collective-permute-done.60.g0.refs_6_ = bf16[256,1024]{1,0:T(8,128)(2,1)S(1)} collective-permute-done((bf16[256,1024]{1,0:T(8,128)(2,1)S(1)}, bf16[256,1024]{1,0:T(8,128)(2,1)S(1)}, u32[]{:S(2)}, u32[]{:S(2)}) %collective-permute-start.60) | collective-permute-done | bytes 524320 | tf_op jit(solution)/shard_map/ppermute | solution.py:73
  457.6 5.2 shard_map.342
  476.6 11.0 %collective-permute-done.63.refs_2_ = bf16[256,1024]{1,0:T(8,128)(2,1)} collective-permute-done((bf16[256,1024]{1,0:T(8,128)(2,1)}, bf16[256,1024]{1,0:T(8,128)(2,1)}, u32[]{:S(2)}, u32[]{:S(2)}) %collective-permute-start.63) | collective-permute-done | bytes 524320 | tf_op jit(solution)/shard_map/ppermute | solution.py:73
  532.6 64.8 %reduce-scatter.4.cloned.1.call-done = bf16[1,256,1024]{2,1,0:T(8,128)(2,1)} async-done(((bf16[8,256,1024]{2,1,0:T(8,128)(2,1)}), bf16[1,256,1024]{2,1,0:T(8,128)(2,1)}) %reduce-scatter.4.cloned.1.call-update) | async-done | bytes 524304 | tf_op jit(solution)/shard_map/reduce_scatter | solution.py:190
  (527 shorter events, 272.3 us)
Async XLA Ops:
  7.2 118.7 %all-gather.7.cloned.1.call-start = ((), (), s32[]{:S(2)}) async-start(), calls=%async_computation.6 | async-start | bytes 7077888 | tf_op jit(solution)/shard_map/all_gather | solution.py:198
  22.7 170.7 %all-gather.9.cloned.1.call-start = ((), (), s32[]{:S(2)}) async-start(), calls=%async_computation.7 | async-start | bytes 1769472 | tf_op jit(solution)/shard_map/all_gather | solution.py:1263
  34.4 215.0 %all-gather.11.cloned.1.call-start = ((), (), s32[]{:S(2)}) async-start(), calls=%async_computation.8 | async-start | bytes 4718592 | tf_op jit(solution)/shard_map/all_gather | solution.py:198
  35.3 14.1 %collective-permute-start.4 = (bf16[256,1024]{1,0:T(8,128)(2,1)S(1)}, bf16[256,1024]{1,0:T(8,128)(2,1)S(1)}, u32[]{:S(2)}, u32[]{:S(2)}) collective-permute-start(bf16[256,1024]{1,0:T(8,128)(2,1)S(1)} %multiply_convert_fusion.h0.refs_0_), channel_id=1, source_target_pairs={{2,0},{3,1},{0,2},{1,3},{6,4},{7,5},{4,6},{5,7},{10,8},{11,9},{8,1... | collective-permute-start | bytes 1572872 | tf_op jit(solution)/shard_map/ppermute | solution.py:73
  49.3 14.2 %collective-permute-start.5 = (bf16[256,1024]{1,0:T(8,128)(2,1)S(1)}, bf16[256,1024]{1,0:T(8,128)(2,1)S(1)}, u32[]{:S(2)}, u32[]{:S(2)}) collective-permute-start(bf16[256,1024]{1,0:T(8,128)(2,1)S(1)} %collective-permute-done.4.h0.refs_2_), channel_id=1, source_target_pairs={{1,0},{0,1},{3,2},{2,3},{5,4},{4,5},{7,6},{6,7},{9,8},{8,9},{11,10... | collective-permute-start | bytes 1572872 | tf_op jit(solution)/shard_map/ppermute | solution.py:73
  62.3 449.7 %reduce-scatter.8.cloned.1.call-start = ((), (), s32[]{:S(2)}) async-start(), calls=%async_computation.5 | async-start | bytes 4718592 | tf_op jit(solution)/shard_map/reduce_scatter | solution.py:190
  62.5 69.7 %collective-permute-start.13 = (bf16[256,1024]{1,0:T(8,128)(2,1)S(1)}, bf16[256,1024]{1,0:T(8,128)(2,1)S(1)}, u32[]{:S(2)}, u32[]{:S(2)}) collective-permute-start(bf16[256,1024]{1,0:T(8,128)(2,1)S(1)} %multiply_convert_fusion.h0.refs_0_), channel_id=1, source_target_pairs={{1,0},{0,1},{3,2},{2,3},{5,4},{4,5},{7,6},{6,7},{9,8},{8,9},{11,10... | collective-permute-start | bytes 1572872 | tf_op jit(solution)/shard_map/ppermute | solution.py:73
  150.6 14.3 %collective-permute-start.17 = (bf16[256,1024]{1,0:T(8,128)(2,1)S(1)}, bf16[256,1024]{1,0:T(8,128)(2,1)S(1)}, u32[]{:S(2)}, u32[]{:S(2)}) collective-permute-start(bf16[256,1024]{1,0:T(8,128)(2,1)S(1)} %get-tuple-element.258.h0.refs_0_), channel_id=1, source_target_pairs={{2,0},{3,1},{0,2},{1,3},{6,4},{7,5},{4,6},{5,7},{10,8},{11,9},{8,1... | collective-permute-start | bytes 1572872 | tf_op jit(solution)/shard_map/ppermute | solution.py:73
  176.4 14.0 %collective-permute-start.21 = (bf16[256,1024]{1,0:T(8,128)(2,1)S(1)}, bf16[256,1024]{1,0:T(8,128)(2,1)S(1)}, u32[]{:S(2)}, u32[]{:S(2)}) collective-permute-start(bf16[256,1024]{1,0:T(8,128)(2,1)S(1)} %add_convert_fusion.6), channel_id=1, source_target_pairs={{2,0},{3,1},{0,2},{1,3},{6,4},{7,5},{4,6},{5,7},{10,8},{11,9},{8,1... | collective-permute-start | bytes 1572872 | tf_op jit(solution)/shard_map/ppermute | solution.py:73
  191.8 14.7 %collective-permute-start.23 = (bf16[256,1024]{1,0:T(8,128)(2,1)}, bf16[256,1024]{1,0:T(8,128)(2,1)}, u32[]{:S(2)}, u32[]{:S(2)}) collective-permute-start(bf16[256,1024]{1,0:T(8,128)(2,1)} %get-tuple-element.245.h0.refs_0_), channel_id=1, source_target_pairs={{2,0},{3,1},{0,2},{1,3},{6,4},{7,5},{4,6},{5,7},{10,8},{11,9},{8,1... | collective-permute-start | bytes 1572872 | tf_op jit(solution)/shard_map/ppermute | solution.py:73
  232.4 14.0 %collective-permute-start.30 = (bf16[256,1024]{1,0:T(8,128)(2,1)S(1)}, bf16[256,1024]{1,0:T(8,128)(2,1)S(1)}, u32[]{:S(2)}, u32[]{:S(2)}) collective-permute-start(bf16[256,1024]{1,0:T(8,128)(2,1)S(1)} %add_convert_fusion.5), channel_id=1, source_target_pairs={{2,0},{3,1},{0,2},{1,3},{6,4},{7,5},{4,6},{5,7},{10,8},{11,9},{8,1... | collective-permute-start | bytes 1572872 | tf_op jit(solution)/shard_map/ppermute | solution.py:73
  247.8 14.6 %collective-permute-start.33 = (bf16[256,1024]{1,0:T(8,128)(2,1)}, bf16[256,1024]{1,0:T(8,128)(2,1)}, u32[]{:S(2)}, u32[]{:S(2)}) collective-permute-start(bf16[256,1024]{1,0:T(8,128)(2,1)} %get-tuple-element.220.h0.refs_0_), channel_id=1, source_target_pairs={{2,0},{3,1},{0,2},{1,3},{6,4},{7,5},{4,6},{5,7},{10,8},{11,9},{8,1... | collective-permute-start | bytes 1572872 | tf_op jit(solution)/shard_map/ppermute | solution.py:73
  270.2 14.0 %collective-permute-start.36 = (bf16[256,1024]{1,0:T(8,128)(2,1)S(1)}, bf16[256,1024]{1,0:T(8,128)(2,1)S(1)}, u32[]{:S(2)}, u32[]{:S(2)}) collective-permute-start(bf16[256,1024]{1,0:T(8,128)(2,1)S(1)} %add_convert_fusion.4), channel_id=1, source_target_pairs={{2,0},{3,1},{0,2},{1,3},{6,4},{7,5},{4,6},{5,7},{10,8},{11,9},{8,1... | collective-permute-start | bytes 1572872 | tf_op jit(solution)/shard_map/ppermute | solution.py:73
  286.6 14.3 %collective-permute-start.39 = (bf16[256,1024]{1,0:T(8,128)(2,1)S(1)}, bf16[256,1024]{1,0:T(8,128)(2,1)S(1)}, u32[]{:S(2)}, u32[]{:S(2)}) collective-permute-start(bf16[256,1024]{1,0:T(8,128)(2,1)S(1)} %get-tuple-element.212.g0.refs_4_), channel_id=1, source_target_pairs={{2,0},{3,1},{0,2},{1,3},{6,4},{7,5},{4,6},{5,7},{10,8},{11,9},{8,1... | collective-permute-start | bytes 1572872 | tf_op jit(solution)/shard_map/ppermute | solution.py:73
  308.2 14.3 %collective-permute-start.42 = (bf16[256,1024]{1,0:T(8,128)(2,1)}, bf16[256,1024]{1,0:T(8,128)(2,1)}, u32[]{:S(2)}, u32[]{:S(2)}) collective-permute-start(bf16[256,1024]{1,0:T(8,128)(2,1)} %add_convert_fusion.3), channel_id=1, source_target_pairs={{2,0},{3,1},{0,2},{1,3},{6,4},{7,5},{4,6},{5,7},{10,8},{11,9},{8,1... | collective-permute-start | bytes 1572872 | tf_op jit(solution)/shard_map/ppermute | solution.py:73
  330.1 194.1 %reduce-scatter.6.cloned.1.call-start = ((), (), s32[]{:S(2)}) async-start(), calls=%async_computation.4 | async-start | bytes 4128768 | tf_op jit(solution)/shard_map/reduce_scatter | solution.py:190
  330.4 14.6 %collective-permute-start.44 = (bf16[256,1024]{1,0:T(8,128)(2,1)}, bf16[256,1024]{1,0:T(8,128)(2,1)S(1)}, u32[]{:S(2)}, u32[]{:S(2)}) collective-permute-start(bf16[256,1024]{1,0:T(8,128)(2,1)} %copy-done.61), channel_id=1, source_target_pairs={{2,0},{3,1},{0,2},{1,3},{6,4},{7,5},{4,6},{5,7},{10,8},{11,9},{8,1... | collective-permute-start | bytes 1572872 | tf_op jit(solution)/shard_map/ppermute | solution.py:73
  367.0 14.0 %collective-permute-start.51 = (bf16[256,1024]{1,0:T(8,128)(2,1)S(1)}, bf16[256,1024]{1,0:T(8,128)(2,1)S(1)}, u32[]{:S(2)}, u32[]{:S(2)}) collective-permute-start(bf16[256,1024]{1,0:T(8,128)(2,1)S(1)} %add_convert_fusion.2), channel_id=1, source_target_pairs={{2,0},{3,1},{0,2},{1,3},{6,4},{7,5},{4,6},{5,7},{10,8},{11,9},{8,1... | collective-permute-start | bytes 1572872 | tf_op jit(solution)/shard_map/ppermute | solution.py:73
  382.9 14.3 %collective-permute-start.53 = (bf16[256,1024]{1,0:T(8,128)(2,1)S(1)}, bf16[256,1024]{1,0:T(8,128)(2,1)S(1)}, u32[]{:S(2)}, u32[]{:S(2)}) collective-permute-start(bf16[256,1024]{1,0:T(8,128)(2,1)S(1)} %get-tuple-element.242.g0.refs_4_), channel_id=1, source_target_pairs={{2,0},{3,1},{0,2},{1,3},{6,4},{7,5},{4,6},{5,7},{10,8},{11,9},{8,1... | collective-permute-start | bytes 1572872 | tf_op jit(solution)/shard_map/ppermute | solution.py:73
  419.1 178.2 %reduce-scatter.4.cloned.1.call-start = ((), (), s32[]{:S(2)}) async-start(), calls=%async_computation.3 | async-start | bytes 4718592 | tf_op jit(solution)/shard_map/reduce_scatter | solution.py:190
  419.6 14.4 %collective-permute-start.57 = (bf16[256,1024]{1,0:T(8,128)(2,1)}, bf16[256,1024]{1,0:T(8,128)(2,1)S(1)}, u32[]{:S(2)}, u32[]{:S(2)}) collective-permute-start(bf16[256,1024]{1,0:T(8,128)(2,1)} %add_convert_fusion.1), channel_id=1, source_target_pairs={{2,0},{3,1},{0,2},{1,3},{6,4},{7,5},{4,6},{5,7},{10,8},{11,9},{8,1... | collective-permute-start | bytes 1572872 | tf_op jit(solution)/shard_map/ppermute | solution.py:73
  437.2 14.3 %collective-permute-start.60 = (bf16[256,1024]{1,0:T(8,128)(2,1)S(1)}, bf16[256,1024]{1,0:T(8,128)(2,1)S(1)}, u32[]{:S(2)}, u32[]{:S(2)}) collective-permute-start(bf16[256,1024]{1,0:T(8,128)(2,1)S(1)} %get-tuple-element.264.g0.refs_4_), channel_id=1, source_target_pairs={{2,0},{3,1},{0,2},{1,3},{6,4},{7,5},{4,6},{5,7},{10,8},{11,9},{8,1... | collective-permute-start | bytes 1572872 | tf_op jit(solution)/shard_map/ppermute | solution.py:73
  473.3 14.3 %collective-permute-start.63 = (bf16[256,1024]{1,0:T(8,128)(2,1)}, bf16[256,1024]{1,0:T(8,128)(2,1)}, u32[]{:S(2)}, u32[]{:S(2)}) collective-permute-start(bf16[256,1024]{1,0:T(8,128)(2,1)} %add_convert_fusion), channel_id=1, source_target_pairs={{2,0},{3,1},{0,2},{1,3},{6,4},{7,5},{4,6},{5,7},{10,8},{11,9},{8,1... | collective-permute-start | bytes 1572872 | tf_op jit(solution)/shard_map/ppermute | solution.py:73
  530.2 73.0 %collective-permute-start.67 = (bf16[128,256]{1,0:T(8,128)(2,1)S(1)}, bf16[128,256]{1,0:T(8,128)(2,1)S(1)}, u32[]{:S(2)}, u32[]{:S(2)}) collective-permute-start(bf16[128,256]{1,0:T(8,128)(2,1)S(1)} %get-tuple-element.383), channel_id=1, source_target_pairs={{0,0},{1,8},{2,16},{3,24},{4,1},{5,9},{6,17},{7,25},{8,2},{9,10},{... | collective-permute-start | bytes 196616 | tf_op jit(solution)/shard_map/ppermute | solution.py:1395
  (165 other events, 1629.6 us)
Sparse Core Ops, SparseCore 0:
  22.8 103.0 all-gather.6
  128.6 42.0 all-gather.8
  173.4 72.2 all-gather.10
  330.2 86.7 reduce-scatter.7
  421.0 80.5 reduce-scatter.5
  505.5 91.8 reduce-scatter.3

commit v5 on v4

--- a/solution.py
+++ b/solution.py
@@ -173,9 +173,8 @@
     return out
 
 
-def scatter_parity(own, other):
+def scatter_parity(own, near):
     rows = lax.axis_size("rows")
-    near = lax.ppermute(other, "rows", [(i, i ^ 1) for i in range(rows)])
     packed = (own.astype(F32) + near.astype(F32)).astype(BF)
     return lax.psum_scatter(
         packed,
@@ -486,35 +485,6 @@
     )(*h, *g, *da, *s)
 
 
-def half_grads_kernel(odd_ref, *refs, count):
-    own, other = refs[-2:]
-    refs = refs[:-2]
-    join = lambda v: jnp.concatenate([r[...] for r in v], axis=0)
-    v = mm_tn(join(refs[:count]), join(refs[count:])).astype(BF)
-    v = v.reshape(own.shape[0], 2, own.shape[1], own.shape[2])
-    even = odd_ref[0] == 0
-    own[...] = jnp.where(even, v[:, 0], v[:, 1])
-    other[...] = jnp.where(even, v[:, 1], v[:, 0])
-
-
-def half_grads(left, right):
-    rows = lax.axis_size("rows")
-    d, units = left[0].shape[1], right[0].shape[1]
-    m = d // rows
-    if m % 16:
-        v = mm_tn(jnp.concatenate(left, axis=0), jnp.concatenate(right, axis=0)).astype(BF)
-        return by_parity(v.reshape(rows, m, units))
-    odd = (lax.axis_index("rows") % 2).astype(jnp.int32).reshape(1)
-    return pl.pallas_call(
-        functools.partial(half_grads_kernel, count=len(left)),
-        in_specs=[pl.BlockSpec(memory_space=pltpu.SMEM)]
-        + [pl.BlockSpec(memory_space=pltpu.VMEM)] * (len(left) + len(right)),
-        out_shape=[jax.ShapeDtypeStruct((rows // 2, m, units), BF)] * 2,
-        compiler_params=params(28),
-        cost_estimate=cost(2 * len(left) * left[0].shape[0] * d * units, *left),
-    )(odd, *left, *right)
-
-
 def by_parity(packed):
     rows = packed.shape[0]
     odd = lax.axis_index("rows") % 2
@@ -523,6 +493,48 @@
         lax.dynamic_index_in_dim(v, odd, 1, keepdims=False),
         lax.dynamic_index_in_dim(v, 1 - odd, 1, keepdims=False),
     ]
+
+
+def parity_grads_kernel(odd_ref, *refs):
+    outs, refs = refs[-2:], refs[:-2]
+    count = len(refs) // 6
+    h, g = refs[: 2 * count], refs[2 * count : 4 * count]
+    da, s = refs[4 * count : 5 * count], refs[5 * count : 6 * count]
+    steps, m2, width = outs[0].shape
+    half = m2 // 2
+    join = lambda v: jnp.concatenate([r[...] for r in v], axis=0)
+    even = odd_ref[0] == 0
+    for i, (a, b) in enumerate(((h, da), (s, g))):
+        v = mm_tn(join(a), join(b)).astype(BF).reshape(steps, 2, half, width)
+        rows = slice(i * half, (i + 1) * half)
+        outs[0][:, rows, :] = jnp.where(even, v[:, 0], v[:, 1])
+        outs[1][:, rows, :] = jnp.where(even, v[:, 1], v[:, 0])
+
+
+def parity_grads(h, g, da, s):
+    rows = lax.axis_size("rows")
+    n, d = h[0].shape
+    units, tile = da[0].shape[1], d // 2
+    m = d // rows
+    odd = (lax.axis_index("rows") % 2).astype(jnp.int32)
+    if units != d or tile % (2 * m):
+        h, g, da, s = (jnp.concatenate(v, axis=0) for v in (h, g, da, s))
+        return by_parity(pack_grads([mm_tn(h, da).astype(BF), mm_tn(s, g).astype(BF)]))
+    part = pl.BlockSpec((n, tile), lambda j: (0, j))
+    column = pl.BlockSpec((2 * n, tile), lambda j: (0, j))
+    return pl.pallas_call(
+        parity_grads_kernel,
+        grid=(d // tile,),
+        in_specs=[pl.BlockSpec(memory_space=pltpu.SMEM)]
+        + [part] * len(h)
+        + [whole((n, d))] * len(g)
+        + [whole((2 * n, units))] * len(da)
+        + [column] * len(s),
+        out_specs=[pl.BlockSpec((tile // m // 2, 2 * m, d), lambda j: (j, 0, 0))] * 2,
+        out_shape=[jax.ShapeDtypeStruct((rows // 2, 2 * m, d), BF)] * 2,
+        compiler_params=params(36),
+        cost_estimate=cost(4 * len(h) * n * d * units, *h),
+    )(odd.reshape(1), *h, *g, *da, *s)
 
 
 def add_norm_kernel(*refs, scale):
@@ -1361,10 +1373,10 @@
 
     g1, local = spread(g, lambda near: ffn_back(near, one[0][1], *f1))
     back = [local] + [ffn_back(p, one[i][1], *f1) for i, p in enumerate(g1[1:], 1)]
-    packed_one = ffn_grads(
+    part_one, other = parity_grads(
         sum(h1, ()), sum(g1, ()), [v[0] for v in back], [v[0] for v in one]
     )
-    sum_one = scatter_rows(packed_one)
+    rows_near = lax.ppermute(other, "rows", [(i, i ^ 1) for i in range(rows)])
     parts, _ = collect([v[1] for v in back], [v[2] for v in back])
     grad, _, gain_one = back_norm(parts, inputs, norm_gains[0], d1, 1.0)
     grad_frames = grad.astype(BF)[None]
@@ -1388,6 +1400,9 @@
         )
 
     grad_ffn2_in, grad_ffn2_out = ffn_owned(sum_four)
+    sum_one = scatter_parity(
+        part_one, after(rows_near, grad, grad_ffn2_in, grad_ffn2_out)
+    )
     grad_query, grad_key, grad_value, d_block = (
         sum_two[:, i * share : (i + 1) * share] for i in range(4)
     )
@@ -1426,7 +1441,7 @@
         ],
         axis=0,
     )
-    small = sum_axis(sum_axis(small, "tm"), "rows")
+    small = sum_axis(sum_axis(after(small, rows_near), "tm"), "rows")
     table_size = rel_table.shape[0] * rel_table.shape[1]
     return (
         output[None],

time: 621 us -> 599 us (0.965)
  waiting for transfers between devices: 365 us -> 336 us
  local copies, waits for them, and re-layouts: 53.2 us -> 59.7 us
    reduce_scatter x3 -> x2, waiting for transfers between devices: 64.8 us -> 0.01 us  [scatter_rows(): return lax.psum_scatter(packed, 'rows', scatter_dimension=0, tiled=False)]
    ppermute x0 -> x1, waiting for transfers between devices: none -> 28.7 us  [shards(): rows_near = lax.ppermute(other, 'rows', [(i, i ^ 1) for i in range(rows)])]
    ppermute x11, waiting for transfers between devices: 27 us -> 35.7 us  [sum_axis(): v = v + lax.ppermute(v, axis, [(i, i ^ bit) for i in range(size)])]
    ppermute x66, waiting for transfers between devices: 210 us -> 204 us  [from_peer(): return lax.ppermute(a, 'tm', tm_peer(dx, dc))]
    unnamed x210 -> x232, local copies, waits for them, and re-layouts: 34.6 us -> 41.2 us
  transfers between devices with their start and end apart: 85 -> 86, of which waited for: 58 -> 58; matrix products, arithmetic and copies ran while one was open for 6% -> 6% of each run, Pallas kernels for 14% -> 15%
where the time goes in v5:
time: 599 us; the launch traced here: 594 us
  waiting for transfers between devices  336 us (56%)
  Pallas kernels  105 us (18%)
  starting transfers between devices  60.3 us (10%)
  local copies, waits for them, and re-layouts  59.7 us (10%)
  other arithmetic  16.8 us (3%)
  between operations  16.1 us (3%)
    ppermute x66, waiting for transfers between devices, from_peer(): return lax.ppermute(a, 'tm', tm_peer(dx, dc))  204 us
    all_gather x2, waiting for transfers between devices, gather_ffn(): full = lax.all_gather(sent, 'rows', axis=0, tiled=False)  62.4 us
    ppermute x66, starting transfers between devices, from_peer(): return lax.ppermute(a, 'tm', tm_peer(dx, dc))  44.9 us
    unnamed x232, local copies, waits for them, and re-layouts  41.2 us
    ppermute x11, waiting for transfers between devices, sum_axis(): v = v + lax.ppermute(v, axis, [(i, i ^ bit) for i in range(size)])  35.7 us
    ppermute x1, waiting for transfers between devices, shards(): rows_near = lax.ppermute(other, 'rows', [(i, i ^ 1) for i in range(rows)])  28.7 us
    pallas_call x4, Pallas kernels, ffn(): pl.pallas_call(ffn_kernel, grid=(1,), in_specs=[whole((n, d)), whole((n,...  12.1 us
  transfers between devices with their start and end apart: 86, of which 58 were waited for; matrix products, arithmetic and copies ran while one was open for 6% of the time, Pallas kernels for 15%

profile of v5, /device:TPU:0, one launch (start us, length us, event | category | flops | bytes accessed | tf_op | source)
XLA Modules:
  0.0 594.0 jit_solution(10366007072660036384)
XLA Ops:
  36.3 13.0 %collective-permute-done.4.h0.refs_2_ = bf16[256,1024]{1,0:T(8,128)(2,1)S(1)} collective-permute-done((bf16[256,1024]{1,0:T(8,128)(2,1)S(1)}, bf16[256,1024]{1,0:T(8,128)(2,1)S(1)}, u32[]{:S(2)}, u32[]{:S(2)}) %collective-permute-start.4) | collective-permute-done | bytes 524320 | tf_op jit(solution)/shard_map/ppermute | solution.py:73
  53.2 5.0 collective-permute-done.11.refs_2_
  63.5 62.4 %all-gather.7.cloned.1.call-done = bf16[3072,1024]{1,0:T(8,128)(2,1)} async-done(((bf16[384,1024]{1,0:T(8,128)(2,1)}), bf16[3072,1024]{1,0:T(8,128)(2,1)}) %all-gather.7.cloned.1.call-update) | async-done | bytes 6291472 | tf_op jit(solution)/shard_map/all_gather | solution.py:197
  137.3 12.1 %collective-permute-done.15.refs_2_ = bf16[256,1024]{1,0:T(8,128)(2,1)S(1)} collective-permute-done((bf16[256,1024]{1,0:T(8,128)(2,1)S(1)}, bf16[256,1024]{1,0:T(8,128)(2,1)S(1)}, u32[]{:S(2)}, u32[]{:S(2)}) %collective-permute-start.15) | collective-permute-done | bytes 524320 | tf_op jit(solution)/shard_map/ppermute | solution.py:73
  155.3 9.7 %collective-permute-done.17.h0.refs_2_ = bf16[256,1024]{1,0:T(8,128)(2,1)S(1)} collective-permute-done((bf16[256,1024]{1,0:T(8,128)(2,1)S(1)}, bf16[256,1024]{1,0:T(8,128)(2,1)S(1)}, u32[]{:S(2)}, u32[]{:S(2)}) %collective-permute-start.17) | collective-permute-done | bytes 524320 | tf_op jit(solution)/shard_map/ppermute | solution.py:73
  168.0 6.4 %shard_map.314 = (bf16[1024,768]{1,0:T(8,128)(2,1)S(1)}, bf16[1024,256]{1,0:T(8,128)(2,1)S(1)}, f32[2,1024,1]{2,1,0:T(8,128)S(1)}, f32[256,1024]{1,0:T(8,128)S(1...) custom-call(s32[4]{0:T(128)S(1)} %copy-done.88, ...), custom_call_target="tpu_custom_call" | custom-call | flops 1610612736 | bytes 1572864 | tf_op jit(solution)/shard_map/pallas_call | solution.py:720
  178.1 12.5 %collective-permute-done.21.refs_2_ = bf16[256,1024]{1,0:T(8,128)(2,1)S(1)} collective-permute-done((bf16[256,1024]{1,0:T(8,128)(2,1)S(1)}, bf16[256,1024]{1,0:T(8,128)(2,1)S(1)}, u32[]{:S(2)}, u32[]{:S(2)}) %collective-permute-start.21) | collective-permute-done | bytes 524320 | tf_op jit(solution)/shard_map/ppermute | solution.py:73
  198.2 8.3 %collective-permute-done.23.h0.refs_2_ = bf16[256,1024]{1,0:T(8,128)(2,1)} collective-permute-done((bf16[256,1024]{1,0:T(8,128)(2,1)}, bf16[256,1024]{1,0:T(8,128)(2,1)}, u32[]{:S(2)}, u32[]{:S(2)}) %collective-permute-start.23) | collective-permute-done | bytes 524320 | tf_op jit(solution)/shard_map/ppermute | solution.py:73
  234.9 12.5 %collective-permute-done.30.refs_2_ = bf16[256,1024]{1,0:T(8,128)(2,1)S(1)} collective-permute-done((bf16[256,1024]{1,0:T(8,128)(2,1)S(1)}, bf16[256,1024]{1,0:T(8,128)(2,1)S(1)}, u32[]{:S(2)}, u32[]{:S(2)}) %collective-permute-start.30) | collective-permute-done | bytes 524320 | tf_op jit(solution)/shard_map/ppermute | solution.py:73
  257.0 6.4 %collective-permute-done.33.h0.refs_2_ = bf16[256,1024]{1,0:T(8,128)(2,1)} collective-permute-done((bf16[256,1024]{1,0:T(8,128)(2,1)}, bf16[256,1024]{1,0:T(8,128)(2,1)}, u32[]{:S(2)}, u32[]{:S(2)}) %collective-permute-start.33) | collective-permute-done | bytes 524320 | tf_op jit(solution)/shard_map/ppermute | solution.py:73
  272.7 12.5 %collective-permute-done.36.refs_2_ = bf16[256,1024]{1,0:T(8,128)(2,1)S(1)} collective-permute-done((bf16[256,1024]{1,0:T(8,128)(2,1)S(1)}, bf16[256,1024]{1,0:T(8,128)(2,1)S(1)}, u32[]{:S(2)}, u32[]{:S(2)}) %collective-permute-start.36) | collective-permute-done | bytes 524320 | tf_op jit(solution)/shard_map/ppermute | solution.py:73
  292.7 9.3 %collective-permute-done.39.g0.refs_6_ = bf16[256,1024]{1,0:T(8,128)(2,1)S(1)} collective-permute-done((bf16[256,1024]{1,0:T(8,128)(2,1)S(1)}, bf16[256,1024]{1,0:T(8,128)(2,1)S(1)}, u32[]{:S(2)}, u32[]{:S(2)}) %collective-permute-start.39) | collective-permute-done | bytes 524320 | tf_op jit(solution)/shard_map/ppermute | solution.py:73
  310.6 6.0 %shard_map.326 = bf16[8,256,1024]{2,1,0:T(8,128)(2,1)S(1)} custom-call(bf16[256,1024]{1,0:T(8,128)(2,1)} %get-tuple-element.224.h0.refs_0_, bf16[256,1024]{1,0:T(8,128)(2,1)} %collective-permute-done.31.h1.refs_1_, bf16[256,1024]{1,0:T(8,128)(2,1)} %collective-permute-done.33.h0.refs_2_, bf16[256,1024]{1,0:T(8,128)(2,1)S(1)} %collective-permute-done.34.h1.refs_3_, ...), custom_call_target="tpu_custom_call" | custom-call | flops 4294967296 | bytes 2097152 | tf_op jit(solution)/shard_map/pallas_call | solution.py:474
  336.1 9.8 %collective-permute-done.44.g0.refs_6_ = bf16[256,1024]{1,0:T(8,128)(2,1)S(1)} collective-permute-done((bf16[256,1024]{1,0:T(8,128)(2,1)}, bf16[256,1024]{1,0:T(8,128)(2,1)S(1)}, u32[]{:S(2)}, u32[]{:S(2)}) %collective-permute-start.44) | collective-permute-done | bytes 524320 | tf_op jit(solution)/shard_map/ppermute | solution.py:73
  369.5 12.5 %collective-permute-done.51.refs_2_ = bf16[256,1024]{1,0:T(8,128)(2,1)S(1)} collective-permute-done((bf16[256,1024]{1,0:T(8,128)(2,1)S(1)}, bf16[256,1024]{1,0:T(8,128)(2,1)S(1)}, u32[]{:S(2)}, u32[]{:S(2)}) %collective-permute-start.51) | collective-permute-done | bytes 524320 | tf_op jit(solution)/shard_map/ppermute | solution.py:73
  389.3 9.0 %collective-permute-done.53.g0.refs_6_ = bf16[256,1024]{1,0:T(8,128)(2,1)S(1)} collective-permute-done((bf16[256,1024]{1,0:T(8,128)(2,1)S(1)}, bf16[256,1024]{1,0:T(8,128)(2,1)S(1)}, u32[]{:S(2)}, u32[]{:S(2)}) %collective-permute-start.53) | collective-permute-done | bytes 524320 | tf_op jit(solution)/shard_map/ppermute | solution.py:73
  400.8 11.2 %shard_map.336 = (bf16[1024,768]{1,0:T(8,128)(2,1)S(1)}, f32[2,128,640]{2,1,0:T(8,128)S(1)}, f32[256,1024]{1,0:T(8,128)S(1)}, f32[256,1024]{1,0:T(8,128)S(1)}, b...) custom-call(s32[4]{0:T(128)S(1)} %copy-done.88, f32[2,17]{1,0:T(2,128)S(1)} %constant_dynamic-slice_fusion.2.tab_ref, ...), custom_call_target="tpu_custom_call" | custom-call | flops 3221225472 | bytes 524288 | tf_op jit(solution)/shard_map/pallas_call | solution.py:849
  422.7 12.4 %collective-permute-done.57.refs_2_ = bf16[256,1024]{1,0:T(8,128)(2,1)S(1)} collective-permute-done((bf16[256,1024]{1,0:T(8,128)(2,1)}, bf16[256,1024]{1,0:T(8,128)(2,1)S(1)}, u32[]{:S(2)}, u32[]{:S(2)}) %collective-permute-start.57) | collective-permute-done | bytes 524320 | tf_op jit(solution)/shard_map/ppermute | solution.py:73
  462.6 6.2 %shard_map.342 = (bf16[4,256,1024]{2,1,0:T(8,128)(2,1)S(1)}, bf16[4,256,1024]{2,1,0:T(8,128)(2,1)}) custom-call(s32[1]{0:T(128)} %bitcast.33.odd_ref, bf16[256,1024]{1,0:T(8,128)(2,1)S(1)} %copy-done.33, bf16[256,1024]{1,0:T(8,128)(2,1)S(1)} %copy-done.79, bf16[256,1024]{1,0:T(8,128)(2,1)S(1)} %copy-done.75, bf16[256,1024]{1,0:T(8,128)(2,1)S(1)} %copy-done.77, ...), custom_call_target="tpu_custom_call" | custom-call | flops 4294967296 | bytes 2097152 | tf_op jit(solution)/shard_map/pallas_call | solution.py:525
  477.9 10.0 %collective-permute-done.63.refs_2_ = bf16[256,1024]{1,0:T(8,128)(2,1)} collective-permute-done((bf16[256,1024]{1,0:T(8,128)(2,1)}, bf16[256,1024]{1,0:T(8,128)(2,1)}, u32[]{:S(2)}, u32[]{:S(2)}) %collective-permute-start.63) | collective-permute-done | bytes 524320 | tf_op jit(solution)/shard_map/ppermute | solution.py:73
  495.3 28.7 %collective-permute-done.64 = bf16[4,256,1024]{2,1,0:T(8,128)(2,1)} collective-permute-done((bf16[4,256,1024]{2,1,0:T(8,128)(2,1)}, bf16[4,256,1024]{2,1,0:T(8,128)(2,1)}, u32[]{:S(2)}, u32[]{:S(2)}) %collective-permute-start.64) | collective-permute-done | bytes 2097184 | tf_op jit(solution)/shard_map/ppermute | solution.py:1379
  544.5 5.8 collective-permute-done.78
  551.9 8.7 %collective-permute-done.79 = f32[13,1024]{1,0:T(8,128)S(1)} collective-permute-done((f32[13,1024]{1,0:T(8,128)S(1)}, f32[13,1024]{1,0:T(8,128)S(1)}, u32[]{:S(2)}, u32[]{:S(2)}) %collective-permute-start.79) | collective-permute-done | bytes 53280 | tf_op jit(solution)/shard_map/ppermute | solution.py:126
  570.1 5.2 reduce-scatter.6.cloned.1.call-done
  (552 shorter events, 282.2 us)
Async XLA Ops:
  7.2 118.6 %all-gather.7.cloned.1.call-start = ((), (), s32[]{:S(2)}) async-start(), calls=%async_computation.6 | async-start | bytes 7077888 | tf_op jit(solution)/shard_map/all_gather | solution.py:197
  22.6 170.8 %all-gather.9.cloned.1.call-start = ((), (), s32[]{:S(2)}) async-start(), calls=%async_computation.7 | async-start | bytes 1769472 | tf_op jit(solution)/shard_map/all_gather | solution.py:1275
  34.4 215.9 %all-gather.11.cloned.1.call-start = ((), (), s32[]{:S(2)}) async-start(), calls=%async_computation.8 | async-start | bytes 4718592 | tf_op jit(solution)/shard_map/all_gather | solution.py:197
  35.2 14.1 %collective-permute-start.4 = (bf16[256,1024]{1,0:T(8,128)(2,1)S(1)}, bf16[256,1024]{1,0:T(8,128)(2,1)S(1)}, u32[]{:S(2)}, u32[]{:S(2)}) collective-permute-start(bf16[256,1024]{1,0:T(8,128)(2,1)S(1)} %multiply_convert_fusion.h0.refs_0_), channel_id=1, source_target_pairs={{2,0},{3,1},{0,2},{1,3},{6,4},{7,5},{4,6},{5,7},{10,8},{11,9},{8,1... | collective-permute-start | bytes 1572872 | tf_op jit(solution)/shard_map/ppermute | solution.py:73
  49.3 14.2 %collective-permute-start.5 = (bf16[256,1024]{1,0:T(8,128)(2,1)S(1)}, bf16[256,1024]{1,0:T(8,128)(2,1)S(1)}, u32[]{:S(2)}, u32[]{:S(2)}) collective-permute-start(bf16[256,1024]{1,0:T(8,128)(2,1)S(1)} %collective-permute-done.4.h0.refs_2_), channel_id=1, source_target_pairs={{1,0},{0,1},{3,2},{2,3},{5,4},{4,5},{7,6},{6,7},{9,8},{8,9},{11,10... | collective-permute-start | bytes 1572872 | tf_op jit(solution)/shard_map/ppermute | solution.py:73
  62.2 412.1 %reduce-scatter.4.cloned.1.call-start = ((), (), s32[]{:S(2)}) async-start(), calls=%async_computation.3 | async-start | bytes 4718592 | tf_op jit(solution)/shard_map/reduce_scatter | solution.py:189
  62.4 68.8 %collective-permute-start.13 = (bf16[256,1024]{1,0:T(8,128)(2,1)S(1)}, bf16[256,1024]{1,0:T(8,128)(2,1)S(1)}, u32[]{:S(2)}, u32[]{:S(2)}) collective-permute-start(bf16[256,1024]{1,0:T(8,128)(2,1)S(1)} %multiply_convert_fusion.h0.refs_0_), channel_id=1, source_target_pairs={{1,0},{0,1},{3,2},{2,3},{5,4},{4,5},{7,6},{6,7},{9,8},{8,9},{11,10... | collective-permute-start | bytes 1572872 | tf_op jit(solution)/shard_map/ppermute | solution.py:73
  135.3 14.1 %collective-permute-start.15 = (bf16[256,1024]{1,0:T(8,128)(2,1)S(1)}, bf16[256,1024]{1,0:T(8,128)(2,1)S(1)}, u32[]{:S(2)}, u32[]{:S(2)}) collective-permute-start(bf16[256,1024]{1,0:T(8,128)(2,1)S(1)} %add_convert_fusion.8), channel_id=1, source_target_pairs={{2,0},{3,1},{0,2},{1,3},{6,4},{7,5},{4,6},{5,7},{10,8},{11,9},{8,1... | collective-permute-start | bytes 1572872 | tf_op jit(solution)/shard_map/ppermute | solution.py:73
  150.7 14.3 %collective-permute-start.17 = (bf16[256,1024]{1,0:T(8,128)(2,1)S(1)}, bf16[256,1024]{1,0:T(8,128)(2,1)S(1)}, u32[]{:S(2)}, u32[]{:S(2)}) collective-permute-start(bf16[256,1024]{1,0:T(8,128)(2,1)S(1)} %get-tuple-element.262.h0.refs_0_), channel_id=1, source_target_pairs={{2,0},{3,1},{0,2},{1,3},{6,4},{7,5},{4,6},{5,7},{10,8},{11,9},{8,1... | collective-permute-start | bytes 1572872 | tf_op jit(solution)/shard_map/ppermute | solution.py:73
  191.9 14.7 %collective-permute-start.23 = (bf16[256,1024]{1,0:T(8,128)(2,1)}, bf16[256,1024]{1,0:T(8,128)(2,1)}, u32[]{:S(2)}, u32[]{:S(2)}) collective-permute-start(bf16[256,1024]{1,0:T(8,128)(2,1)} %get-tuple-element.249.h0.refs_0_), channel_id=1, source_target_pairs={{2,0},{3,1},{0,2},{1,3},{6,4},{7,5},{4,6},{5,7},{10,8},{11,9},{8,1... | collective-permute-start | bytes 1572872 | tf_op jit(solution)/shard_map/ppermute | solution.py:73
  248.8 14.7 %collective-permute-start.33 = (bf16[256,1024]{1,0:T(8,128)(2,1)}, bf16[256,1024]{1,0:T(8,128)(2,1)}, u32[]{:S(2)}, u32[]{:S(2)}) collective-permute-start(bf16[256,1024]{1,0:T(8,128)(2,1)} %get-tuple-element.224.h0.refs_0_), channel_id=1, source_target_pairs={{2,0},{3,1},{0,2},{1,3},{6,4},{7,5},{4,6},{5,7},{10,8},{11,9},{8,1... | collective-permute-start | bytes 1572872 | tf_op jit(solution)/shard_map/ppermute | solution.py:73
  287.6 14.3 %collective-permute-start.39 = (bf16[256,1024]{1,0:T(8,128)(2,1)S(1)}, bf16[256,1024]{1,0:T(8,128)(2,1)S(1)}, u32[]{:S(2)}, u32[]{:S(2)}) collective-permute-start(bf16[256,1024]{1,0:T(8,128)(2,1)S(1)} %get-tuple-element.216.g0.refs_4_), channel_id=1, source_target_pairs={{2,0},{3,1},{0,2},{1,3},{6,4},{7,5},{4,6},{5,7},{10,8},{11,9},{8,1... | collective-permute-start | bytes 1572872 | tf_op jit(solution)/shard_map/ppermute | solution.py:73
  309.2 14.3 %collective-permute-start.42 = (bf16[256,1024]{1,0:T(8,128)(2,1)}, bf16[256,1024]{1,0:T(8,128)(2,1)}, u32[]{:S(2)}, u32[]{:S(2)}) collective-permute-start(bf16[256,1024]{1,0:T(8,128)(2,1)} %add_convert_fusion.4), channel_id=1, source_target_pairs={{2,0},{3,1},{0,2},{1,3},{6,4},{7,5},{4,6},{5,7},{10,8},{11,9},{8,1... | collective-permute-start | bytes 1572872 | tf_op jit(solution)/shard_map/ppermute | solution.py:73
  331.0 231.5 %reduce-scatter.8.cloned.1.call-start = ((), (), s32[]{:S(2)}) async-start(), calls=%async_computation.5 | async-start | bytes 4128768 | tf_op jit(solution)/shard_map/reduce_scatter | solution.py:189
  331.3 14.6 %collective-permute-start.44 = (bf16[256,1024]{1,0:T(8,128)(2,1)}, bf16[256,1024]{1,0:T(8,128)(2,1)S(1)}, u32[]{:S(2)}, u32[]{:S(2)}) collective-permute-start(bf16[256,1024]{1,0:T(8,128)(2,1)} %copy-done.71), channel_id=1, source_target_pairs={{2,0},{3,1},{0,2},{1,3},{6,4},{7,5},{4,6},{5,7},{10,8},{11,9},{8,1... | collective-permute-start | bytes 1572872 | tf_op jit(solution)/shard_map/ppermute | solution.py:73
  384.0 14.3 %collective-permute-start.53 = (bf16[256,1024]{1,0:T(8,128)(2,1)S(1)}, bf16[256,1024]{1,0:T(8,128)(2,1)S(1)}, u32[]{:S(2)}, u32[]{:S(2)}) collective-permute-start(bf16[256,1024]{1,0:T(8,128)(2,1)S(1)} %get-tuple-element.246.g0.refs_4_), channel_id=1, source_target_pairs={{2,0},{3,1},{0,2},{1,3},{6,4},{7,5},{4,6},{5,7},{10,8},{11,9},{8,1... | collective-permute-start | bytes 1572872 | tf_op jit(solution)/shard_map/ppermute | solution.py:73
  420.2 155.1 %reduce-scatter.6.cloned.1.call-start = ((), (), s32[]{:S(2)}) async-start(), calls=%async_computation.4 | async-start | bytes 2621440 | tf_op jit(solution)/shard_map/reduce_scatter | solution.py:179
  420.7 14.4 %collective-permute-start.57 = (bf16[256,1024]{1,0:T(8,128)(2,1)}, bf16[256,1024]{1,0:T(8,128)(2,1)S(1)}, u32[]{:S(2)}, u32[]{:S(2)}) collective-permute-start(bf16[256,1024]{1,0:T(8,128)(2,1)} %add_convert_fusion.2), channel_id=1, source_target_pairs={{2,0},{3,1},{0,2},{1,3},{6,4},{7,5},{4,6},{5,7},{10,8},{11,9},{8,1... | collective-permute-start | bytes 1572872 | tf_op jit(solution)/shard_map/ppermute | solution.py:73
  438.3 14.3 %collective-permute-start.60 = (bf16[256,1024]{1,0:T(8,128)(2,1)S(1)}, bf16[256,1024]{1,0:T(8,128)(2,1)S(1)}, u32[]{:S(2)}, u32[]{:S(2)}) collective-permute-start(bf16[256,1024]{1,0:T(8,128)(2,1)S(1)} %get-tuple-element.268.g0.refs_4_), channel_id=1, source_target_pairs={{2,0},{3,1},{0,2},{1,3},{6,4},{7,5},{4,6},{5,7},{10,8},{11,9},{8,1... | collective-permute-start | bytes 1572872 | tf_op jit(solution)/shard_map/ppermute | solution.py:73
  468.7 55.3 %collective-permute-start.64 = (bf16[4,256,1024]{2,1,0:T(8,128)(2,1)}, bf16[4,256,1024]{2,1,0:T(8,128)(2,1)}, u32[]{:S(2)}, u32[]{:S(2)}) collective-permute-start(bf16[4,256,1024]{2,1,0:T(8,128)(2,1)} %get-tuple-element.284), channel_id=1, source_target_pairs={{0,4},{4,0},{8,12},{12,8},{16,20},{20,16},{24,28},{28,24},{1,5},{5... | collective-permute-start | bytes 6291464 | tf_op jit(solution)/shard_map/ppermute | solution.py:1379
  472.9 15.1 %collective-permute-start.63 = (bf16[256,1024]{1,0:T(8,128)(2,1)}, bf16[256,1024]{1,0:T(8,128)(2,1)}, u32[]{:S(2)}, u32[]{:S(2)}) collective-permute-start(bf16[256,1024]{1,0:T(8,128)(2,1)} %add_convert_fusion.1), channel_id=1, source_target_pairs={{2,0},{3,1},{0,2},{1,3},{6,4},{7,5},{4,6},{5,7},{10,8},{11,9},{8,1... | collective-permute-start | bytes 1572872 | tf_op jit(solution)/shard_map/ppermute | solution.py:73
  476.0 17.7 %collective-permute-start.65 = (bf16[256,256]{1,0:T(8,128)(2,1)S(1)}, bf16[256,256]{1,0:T(8,128)(2,1)S(1)}, u32[]{:S(2)}, u32[]{:S(2)}) collective-permute-start(bf16[256,256]{1,0:T(8,128)(2,1)S(1)} %get-tuple-element.287), channel_id=1, source_target_pairs={{1,0},{0,1},{3,2},{2,3},{5,4},{4,5},{7,6},{6,7},{9,8},{8,9},{11,10... | collective-permute-start | bytes 393224 | tf_op jit(solution)/shard_map/ppermute | solution.py:73
  476.1 17.6 %collective-permute-start.66 = (bf16[256,256]{1,0:T(8,128)(2,1)S(1)}, bf16[256,256]{1,0:T(8,128)(2,1)S(1)}, u32[]{:S(2)}, u32[]{:S(2)}) collective-permute-start(bf16[256,256]{1,0:T(8,128)(2,1)S(1)} %get-tuple-element.288), channel_id=1, source_target_pairs={{2,0},{3,1},{0,2},{1,3},{6,4},{7,5},{4,6},{5,7},{10,8},{11,9},{8,1... | collective-permute-start | bytes 393224 | tf_op jit(solution)/shard_map/ppermute | solution.py:73
  476.7 17.0 %collective-permute-start.67 = (bf16[256,256]{1,0:T(8,128)(2,1)S(1)}, bf16[256,256]{1,0:T(8,128)(2,1)S(1)}, u32[]{:S(2)}, u32[]{:S(2)}) collective-permute-start(bf16[256,256]{1,0:T(8,128)(2,1)S(1)} %get-tuple-element.289), channel_id=1, source_target_pairs={{3,0},{2,1},{1,2},{0,3},{7,4},{6,5},{5,6},{4,7},{11,8},{10,9},{9,1... | collective-permute-start | bytes 393224 | tf_op jit(solution)/shard_map/ppermute | solution.py:73
  (177 other events, 1637.3 us)
Sparse Core Ops, SparseCore 0:
  22.8 103.0 all-gather.6
  128.6 42.3 all-gather.8
  173.7 72.2 all-gather.10
  331.1 86.9 reduce-scatter.3
  422.1 90.0 reduce-scatter.7
  528.2 47.0 reduce-scatter.5
